TPU v7x, 32 devices: a whole 2x2x4 slice. The times are simulated.
32 devices in a mesh: groups: 2 (over y), gx: 4 (over z), gy: 4 (over x, core).
Axes of the slice: x: 2, y: 2, z: 4, core: 2. Of those that a mesh axis runs over, the one named last changes fastest.
Arguments:
- hidden_in: bfloat16 [64, 2, 16384], P(('groups', 'gy'), None, 'gx'), parts along dimension 0, may hold values from -6 to 6
- joined_projection_weight: bfloat16 [16384, 14336], P('gx', 'gy'), may hold values from -0.046875 to 0.046875
- w_out: bfloat16 [12288, 16384], P('gy', 'gx'), may hold values from -0.21875 to 0.21875
- key_cache: bfloat16 [64, 768, 8, 128], P(('groups', 'gx'), None, 'gy'), parts along dimension 0, may hold values from -400 to 400
- cached_value_rows: bfloat16 [64, 768, 8, 128], P(('groups', 'gx'), None, 'gy'), parts along dimension 0, may hold values from -6 to 6
- lengths: int32 [64], P(('groups', 'gx')), parts along dimension 0, may hold values from 192 to 768, as said below
- positions: int32 [64], P(('groups', 'gx')), parts along dimension 0, may hold values from 0 to 32767
Outputs:
- output: bfloat16 [64, 2, 16384], P(('groups', 'gy'), None, 'gx'), parts along dimension 0
There are 2 independent parts, one for each index of `groups`. A program takes and returns all parts, laid end to end along the dimension named above; an argument that names none is the same for every part. Nothing has to cross between parts.
Inputs may be any that keep to these rules, and one draw needn't show every extreme that they name: `lengths`: some request's cache is full at 768 slots.
All inputs are finite; a program needn't handle non-finite values.
Results may differ from a plain program's by a relative error of at most 0.011.
Values may be sent and summed in bfloat16 or wider, within the bound.
No kernel may reach another device: no remote copies, remote signals or barrier semaphores. Data moves between devices by JAX's collectives and lax.ppermute only.
A program may use at most 128 MiB of HBM per device.

v0:
```python
import math

import jax
import jax.numpy as jnp
from jax import lax
from jax.sharding import PartitionSpec as P


def angles(positions, head_dim):
    step_pos = positions.astype(jnp.float32)[:, None] + jnp.arange(2, dtype=jnp.float32)[None, :]
    frequencies = jnp.exp(
        jnp.arange(head_dim // 2, dtype=jnp.float32) * (-2.0 * math.log(500000.0) / head_dim)
    )
    turned = step_pos[:, :, None] * frequencies
    return (jnp.cos(turned), jnp.sin(turned))


def rotate(values, cosine, sine_part):
    half_dim = values.shape[-1] // 2
    first_half = values[..., :half_dim]
    second = values[..., half_dim:]
    return jnp.concatenate(
        [first_half * cosine - second * sine_part, second * cosine + first_half * sine_part],
        axis=-1,
    )


def attend(joined_rows, key_cache, cached_value_rows, lengths, positions):
    row_count = joined_rows.shape[0]
    kv_groups = key_cache.shape[2]
    head_dim = key_cache.shape[3]
    cache_len = key_cache.shape[1]
    per_group = joined_rows.shape[2] // (kv_groups * head_dim) - 2
    splitted = joined_rows.reshape(row_count, 2, kv_groups, per_group + 2, head_dim)
    cosine, sine_part = angles(positions, head_dim)
    queries = rotate(
        splitted[:, :, :, :per_group, :],
        cosine[:, :, None, None, :],
        sine_part[:, :, None, None, :],
    ).astype(jnp.bfloat16)
    new_key = rotate(
        splitted[:, :, :, per_group, :], cosine[:, :, None, :], sine_part[:, :, None, :]
    ).astype(jnp.bfloat16)
    new_value = splitted[:, :, :, per_group + 1, :].astype(jnp.bfloat16)
    score_scale = 1.0 / math.sqrt(head_dim)
    cached = (
        jnp.einsum("rtgqe,rcge->rtgqc", queries, key_cache, preferred_element_type=jnp.float32)
        * score_scale
    )
    fresh_scores = (
        jnp.einsum("rtgqe,rsge->rtgqs", queries, new_key, preferred_element_type=jnp.float32)
        * score_scale
    )
    cache_live = jnp.arange(cache_len, dtype=jnp.int32)[None, :] < lengths[:, None]
    fresh_live = jnp.arange(2, dtype=jnp.int32)[None, :] <= jnp.arange(2, dtype=jnp.int32)[:, None]
    cached = jnp.where(cache_live[:, None, None, None, :], cached, -1e30)
    fresh_scores = jnp.where(fresh_live[None, :, None, None, :], fresh_scores, -1e30)
    row_max = jnp.maximum(cached.max(axis=-1), fresh_scores.max(axis=-1))[..., None]
    cached_exp = jnp.exp(cached - row_max)
    fresh_exp = jnp.exp(fresh_scores - row_max)
    denom_sum = cached_exp.sum(axis=-1, keepdims=True) + fresh_exp.sum(axis=-1, keepdims=True)
    cached_w = (cached_exp / denom_sum).astype(jnp.bfloat16)
    fresh_w = (fresh_exp / denom_sum).astype(jnp.bfloat16)
    attended = jnp.einsum(
        "rtgqc,rcge->rtgqe", cached_w, cached_value_rows, preferred_element_type=jnp.float32
    )
    attended = attended + jnp.einsum(
        "rtgqs,rsge->rtgqe", fresh_w, new_value, preferred_element_type=jnp.float32
    )
    return attended.astype(jnp.bfloat16).reshape(row_count, 2, kv_groups * per_group * head_dim)


def on_device(
    hidden_in, joined_projection_weight, w_out, key_cache, cached_value_rows, lengths, positions
):
    gathered = lax.all_gather(hidden_in, "gy", axis=0, tiled=True)
    joined_rows = lax.psum_scatter(
        jnp.einsum(
            "rtd,df->rtf", gathered, joined_projection_weight, preferred_element_type=jnp.float32
        ),
        "gx",
        scatter_dimension=0,
        tiled=True,
    )
    attended = attend(joined_rows, key_cache, cached_value_rows, lengths, positions)
    partial_out = jnp.einsum(
        "rtf,fd->rtd",
        lax.all_gather(attended, "gx", axis=0, tiled=True),
        w_out,
        preferred_element_type=jnp.float32,
    )
    return lax.psum_scatter(partial_out, "gy", scatter_dimension=0, tiled=True).astype(jnp.bfloat16)


def solution(mesh):
    in_specs = (
        P(("groups", "gy"), None, "gx"),
        P("gx", "gy"),
        P("gy", "gx"),
        P(("groups", "gx"), None, "gy", None),
        P(("groups", "gx"), None, "gy", None),
        P(("groups", "gx")),
        P(("groups", "gx")),
    )
    out_specs = P(("groups", "gy"), None, "gx")
    return jax.shard_map(
        on_device, mesh=mesh, in_specs=in_specs, out_specs=out_specs, check_vma=False
    )
```

profile of v0, /device:TPU:0, one launch (start us, length us, event | category | flops | bytes accessed | tf_op | source)
XLA Modules:
  0.0 120.6 jit_solution(16387613577803790534)
XLA Ops:
  6.5 0.0 copy-start
  6.5 0.0 reduce-scatter.3.cloned.1.call-start
  6.5 1.1 copy.16
  7.7 8.6 %all_gather.6 = bf16[32,2,4096]{2,0,1:T(8,128)(2,1)S(1)} all-gather(bf16[8,2,4096]{2,0,1:T(8,128)(2,1)S(1)} %copy.16), channel_id=1, replica_groups=mesh['groups'=2,'gx'=4,'gy'=4] {'gy'}, dimensions={0}, use_global_device_ids=true | all-gather | bytes 655360 | tf_op jit(solution)/shard_map/all_gather | solution.py:76
  16.3 0.0 copy-start.4
  16.3 0.0 copy-start.2
  16.3 12.9 %fusion = f32[32,2,3584]{2,0,1:T(8,128)} fusion(bf16[32,2,4096]{2,0,1:T(8,128)(2,1)S(1)} %all_gather.6, bf16[4096,3584]{1,0:T(8,128)(2,1)} %param.8), kind=kOutput, calls=%fused_computation | convolution fusion | flops 1879048192 | bytes 30801920 | tf_op jit(solution)/shard_map/rtd,df->rtf/dot_general | solution.py:78
  29.2 0.0 reduce-scatter.3.cloned.1.call-update
  29.3 0.0 reduce-scatter.5.cloned.1.call-start
  29.3 0.0 copy-done.4
  29.4 0.1 iota_add_fusion
  29.4 0.0 copy-done.2
  29.4 0.1 iota_compare_fusion
  29.5 0.2 multiply_cosine_fusion
  29.7 25.7 %reduce-scatter.3.cloned.1.call-done = f32[8,2,3584]{2,0,1:T(8,128)} async-done(((f32[32,2,3584]{2,0,1:T(8,128)}), f32[8,2,3584]{2,0,1:T(8,128)}) %reduce-scatter.3.cloned.1.call-update) | async-done | bytes 229392 | tf_op jit(solution)/shard_map/reduce_scatter | solution.py:77
  55.4 0.7 slice.39
  56.1 0.7 slice.30
  56.9 1.1 fusion.36
  58.0 0.1 subtract_convert_fusion
  58.1 0.1 fusion.26
  58.2 0.0 copy-done
  58.2 0.0 copy-start.3
  58.2 1.3 %bitcast_reduce_fusion = (f32[8,2,2,12]{3,1,2,0:T(2,128)S(1)}, f32[8,2,2,12,768]{4,3,2,1,0:T(8,128)S(1)}) fusion(bf16[8,768,2,128,1]{3,2,1,0,4:T(2,128)(2,1)S(1)} %bitcast.51, bf16[8,2,2,12,64]{4,3,1,2,0:T(8,128)(2,1)S(1)} %get-tuple-element.6, bf16[8,2,2,12,64]{4,3,1,2,0:T(8,128)(2,1)S(1)} %get-tuple-element.5, pred[8,768]{1,0:T(8,128)(4,1)S(1)} %iota_compare_fusion), kind=kOutput, calls=%fused_computation.9 | convolution fusion | flops 76578432 | bytes 4431360 | tf_op jit(solution)/shard_map/rtgqe,rcge->rtgqc/dot_general | solution.py:47
  59.6 0.5 fusion.37
  60.1 0.1 fusion.29
  60.2 0.5 fusion.11
  60.7 0.2 convolution_bitcast_fusion
  60.9 0.0 copy-done.3
  60.9 0.8 fusion.18
  61.8 0.1 reshape.80
  61.9 15.1 %all_gather.7 = bf16[32,2,3072]{2,0,1:T(8,128)(2,1)S(1)} all-gather(bf16[8,2,3072]{2,0,1:T(8,128)(2,1)S(1)} %reshape.80), channel_id=1, replica_groups=mesh['groups'=2,'gx'=4,'gy'=4] {'gx'}, dimensions={0}, use_global_device_ids=true | all-gather | bytes 491520 | tf_op jit(solution)/shard_map/all_gather | solution.py:88
  76.9 0.0 copy-start.1
  76.9 11.6 %fusion.2 = f32[32,2,4096]{2,0,1:T(8,128)} fusion(bf16[32,2,3072]{2,0,1:T(8,128)(2,1)S(1)} %all_gather.7, bf16[3072,4096]{1,0:T(8,128)(2,1)} %param.9), kind=kOutput, calls=%fused_computation.2 | convolution fusion | flops 1610612736 | bytes 26607616 | tf_op jit(solution)/shard_map/rtf,fd->rtd/dot_general | solution.py:86
  88.6 0.0 reduce-scatter.5.cloned.1.call-update
  88.6 23.4 %reduce-scatter.5.cloned.1.call-done = f32[8,2,4096]{2,0,1:T(8,128)} async-done(((f32[32,2,4096]{2,0,1:T(8,128)}), f32[8,2,4096]{2,0,1:T(8,128)}) %reduce-scatter.5.cloned.1.call-update) | async-done | bytes 262160 | tf_op jit(solution)/shard_map/reduce_scatter | solution.py:92
  112.0 1.0 convert_element_type.26
  113.0 0.8 copy.24
  113.8 0.0 copy-done.1
  (7 shorter events, 0.1 us)
Async XLA Ops:
  6.5 51.7 %copy-start = (bf16[8,768,2,128]{3,2,1,0:T(2,128)(2,1)S(1)}, bf16[8,768,2,128]{3,2,1,0:T(2,128)(2,1)}, u32[]{:S(2)}) copy-start(bf16[8,768,2,128]{3,2,1,0:T(2,128)(2,1)} %param.10) | copy-start | bytes 9437188
  6.5 48.9 %reduce-scatter.3.cloned.1.call-start = ((), (), s32[]{:S(2)}) async-start(), calls=%async_computation.2 | async-start | bytes 1146880 | tf_op jit(solution)/shard_map/reduce_scatter | solution.py:77
  16.3 13.0 %copy-start.4 = (s32[8]{0:T(128)S(1)}, s32[8]{0:T(128)}, u32[]{:S(2)}) copy-start(s32[8]{0:T(128)} %param.13) | copy-start | bytes 100
  16.3 13.1 %copy-start.2 = (s32[8]{0:T(128)S(1)}, s32[8]{0:T(128)}, u32[]{:S(2)}) copy-start(s32[8]{0:T(128)} %param.12) | copy-start | bytes 100
  29.3 82.7 %reduce-scatter.5.cloned.1.call-start = ((), (), s32[]{:S(2)}) async-start(), calls=%async_computation.3 | async-start | bytes 1310720 | tf_op jit(solution)/shard_map/reduce_scatter | solution.py:92
  58.2 2.7 %copy-start.3 = (bf16[8,768,2,128]{3,2,1,0:T(2,128)(2,1)S(1)}, bf16[8,768,2,128]{3,2,1,0:T(2,128)(2,1)}, u32[]{:S(2)}) copy-start(bf16[8,768,2,128]{3,2,1,0:T(2,128)(2,1)} %param.11) | copy-start | bytes 9437188
  76.9 36.8 %copy-start.1 = (bf16[8,768,2,128]{3,2,1,0:T(2,128)(2,1)S(1)}, bf16[8,768,2,128]{3,2,1,0:T(2,128)(2,1)}, u32[]{:S(2)}) copy-start(bf16[8,768,2,128]{3,2,1,0:T(2,128)(2,1)} %param.10) | copy-start | bytes 9437188
Sparse Core Ops, SparseCore 0:
  29.4 25.9 reduce-scatter.2
  88.7 23.2 reduce-scatter.4
where the time goes:
time: 121 us
  waiting for transfers between devices  49.2 us (41%)
  matrix products  27.5 us (23%)
  blocking collectives  23.7 us (20%)
  between operations  13.5 us (11%)
  local copies, waits for them, and re-layouts  4.62 us (4%)
  other arithmetic  2.08 us (2%)
    reduce_scatter x1, waiting for transfers between devices, on_device(): lax.psum_scatter(jnp.einsum('rtd,df->rtf', gathered, joined_projection_we...  25.7 us
    reduce_scatter x1, waiting for transfers between devices, on_device(): lax.psum_scatter(partial_out, 'gy', scatter_dimension=0, tiled=True)  23.4 us
    all_gather x1, blocking collectives, on_device(): lax.all_gather(attended, 'gx', axis=0, tiled=True)  15.1 us
    dot_general x1, matrix products, on_device(): jnp.einsum('rtd,df->rtf', gathered, joined_projection_weight, preferred_e...  12.9 us
    dot_general x1, matrix products, on_device(): jnp.einsum('rtf,fd->rtd', lax.all_gather(attended, 'gx', axis=0, tiled=Tr...  11.6 us
    all_gather x1, blocking collectives, on_device(): gathered = lax.all_gather(hidden_in, 'gy', axis=0, tiled=True)  8.62 us
  transfers between devices with their start and end apart: 2, of which 2 were waited for; matrix products, arithmetic and copies ran while one was open for 0% of the time, Pallas kernels for 0%

commit v1 on v0

v1 whole, which is shorter than its diff:
```python
import functools
import math

import jax
import jax.numpy as jnp
import numpy as np
from jax import lax
from jax.experimental import pallas as pl
from jax.experimental.pallas import tpu as pltpu
from jax.sharding import PartitionSpec as P

BF16 = jnp.bfloat16
F32 = jnp.float32
IN_VMEM = pl.BlockSpec(memory_space=pltpu.VMEM)
IN_SMEM = pl.BlockSpec(memory_space=pltpu.SMEM)
ANYWHERE = pl.BlockSpec(memory_space=pl.ANY)
HEAD_PAD = 16


def partner(index, step, count):
    if count & (count - 1) == 0:
        return index ^ step
    return lax.rem(index + count - step, count) if not isinstance(index, int) else (index - step) % count


def target(index, step, count):
    if count & (count - 1) == 0:
        return index ^ step
    return lax.rem(index + step, count) if not isinstance(index, int) else (index + step) % count


def swap(block, axis, step, count):
    return lax.ppermute(block, axis, [(i, target(i, step, count)) for i in range(count)])


def hbm(array):
    return pltpu.with_memory_space_constraint(array, pltpu.HBM)


def vmem(array):
    return pltpu.with_memory_space_constraint(array, pltpu.VMEM)


def rows_at(index, count):
    return pl.ds(pl.multiple_of(index * count, count), count)


def tile_of(width):
    for tile in (512, 256, 128):
        if width % tile == 0:
            return tile
    return width


def fetch_kernel(columns, tile, w_ref, o_ref, sems):
    copies = [
        pltpu.make_async_copy(
            w_ref.at[:, pl.ds(i * tile, tile)], o_ref.at[:, pl.ds(i * tile, tile)], sems.at[i]
        )
        for i in range(columns // tile)
    ]
    for copy in copies:
        copy.start()
    for copy in copies:
        copy.wait()


def fetch(weight, columns, tile, name, after=()):
    depth = weight.shape[0]
    count = len(after)

    def kernel(*refs):
        w_ref, rest = refs[0], refs[1 + count :]
        fetch_kernel(columns, tile, w_ref, *rest)

    return pl.pallas_call(
        kernel,
        out_shape=pltpu.VMEM((depth, columns), weight.dtype),
        in_specs=[ANYWHERE] * (1 + count),
        out_specs=IN_VMEM,
        scratch_shapes=[pltpu.SemaphoreType.DMA((columns // tile,))],
        cost_estimate=pl.CostEstimate(
            flops=0, bytes_accessed=2 * depth * columns * 2, transcendentals=0
        ),
        compiler_params=pltpu.CompilerParams(vmem_limit_bytes=1 << 20),
        name=name,
    )(hbm(weight), *after)


def project_kernel(ngx, ngy, tile, ready, *refs):
    x_refs = refs[:ngy]
    wa_ref, w_ref, k_ref, v_ref = refs[ngy : ngy + 4]
    outs = refs[ngy + 4 :]
    own_ref, send_refs = outs[0], outs[1:ngx]
    kv_ref, vv_ref = outs[ngx : ngx + 2]
    xs, acc, wb, sems, cache_sems = outs[ngx + 2 :]
    depth, width = w_ref.shape
    tiles = width // tile
    rest = [
        pltpu.make_async_copy(w_ref.at[:, pl.ds(i * tile, tile)], wb.at[i - ready], sems.at[i - ready])
        for i in range(ready, tiles)
    ]
    for copy in rest:
        copy.start()
    caches = [
        pltpu.make_async_copy(k_ref, kv_ref, cache_sems.at[0]),
        pltpu.make_async_copy(v_ref, vv_ref, cache_sems.at[1]),
    ]
    for copy in caches:
        copy.start()
    me_x, me_y = lax.axis_index("gx"), lax.axis_index("gy")
    block_rows = xs.shape[0] // ngy
    for step in range(ngy):
        xs[rows_at(partner(me_y, step, ngy), block_rows), :] = x_refs[step][...].reshape(block_rows, depth)

    @pl.loop(0, ready)
    def _(i):
        columns = pl.ds(pl.multiple_of(i * tile, tile), tile)
        acc[:, columns] = jnp.dot(xs[...], wa_ref[:, columns], preferred_element_type=F32)

    for i in range(ready, tiles):
        rest[i - ready].wait()
        acc[:, i * tile : (i + 1) * tile] = jnp.dot(xs[...], wb[i - ready], preferred_element_type=F32)
    part = own_ref.shape[0]
    own_ref[...] = acc[rows_at(me_x, part), :]
    for step in range(1, ngx):
        send_refs[step - 1][...] = acc[rows_at(target(me_x, step, ngx), part), :].astype(BF16)
    for copy in caches:
        copy.wait()


def project(blocks, wa, weight, keys, values, ngx, ngy):
    depth, width = weight.shape
    tile = tile_of(width)
    ready = wa.shape[1] // tile
    rows = 2 * blocks[0].shape[0] * ngy
    part = rows // ngx
    return pl.pallas_call(
        functools.partial(project_kernel, ngx, ngy, tile, ready),
        out_shape=[pltpu.VMEM((part, width), F32)]
        + [pltpu.VMEM((part, width), BF16)] * (ngx - 1)
        + [pltpu.VMEM(keys.shape, keys.dtype), pltpu.VMEM(values.shape, values.dtype)],
        in_specs=[IN_VMEM] * (ngy + 1) + [ANYWHERE] * 3,
        out_specs=[IN_VMEM] * (ngx + 2),
        scratch_shapes=[
            pltpu.VMEM((rows, depth), BF16),
            pltpu.VMEM((rows, width), F32),
            pltpu.VMEM((max(width // tile - ready, 1), depth, tile), BF16),
            pltpu.SemaphoreType.DMA((max(width // tile - ready, 1),)),
            pltpu.SemaphoreType.DMA((2,)),
        ],
        cost_estimate=pl.CostEstimate(
            flops=2 * rows * depth * width, bytes_accessed=depth * width * 2, transcendentals=0
        ),
        compiler_params=pltpu.CompilerParams(vmem_limit_bytes=24 << 20),
        name="project",
    )(*blocks, vmem(wa), hbm(weight), hbm(keys), hbm(values))


def attend_kernel(ngx, groups, per_group, *refs):
    own_ref, recv_refs = refs[0], refs[1:ngx]
    k_ref, v_ref, len_ref, cos_ref, sin_ref, out_ref, qs, at = refs[ngx:]
    tokens, head_dim = own_ref.shape[0], k_ref.shape[2]
    requests, slots = k_ref.shape[0], k_ref.shape[1]
    half = head_dim // 2
    per_request = 2 * HEAD_PAD
    scale = 1.0 / math.sqrt(head_dim)
    cosine, sine = cos_ref[...], sin_ref[...]

    def joined(column):
        s = slice(column * head_dim, (column + 1) * head_dim)
        total = own_ref[:, s]
        for ref in recv_refs:
            total = total + ref[:, s].astype(F32)
        return total

    def rotate(x):
        return x * cosine + pltpu.roll(x, half, 1) * sine

    fresh_keys, fresh_values, fresh = [], [], []
    row = lax.broadcasted_iota(jnp.int32, (tokens * HEAD_PAD, tokens), 0) // HEAD_PAD
    col = lax.broadcasted_iota(jnp.int32, (tokens * HEAD_PAD, tokens), 1)
    fresh_live = (row // 2 == col // 2) & (col <= row)
    for g in range(groups):
        base = g * (per_group + 2)
        for h in range(per_group):
            qs[g, pl.ds(h, tokens, stride=HEAD_PAD), :] = rotate(joined(base + h))
        for h in range(per_group, HEAD_PAD):
            qs[g, pl.ds(h, tokens, stride=HEAD_PAD), :] = jnp.zeros((tokens, head_dim), F32)
        fresh_keys.append(rotate(joined(base + per_group)).astype(BF16))
        fresh_values.append(joined(base + per_group + 1).astype(BF16))
        scores = (
            lax.dot_general(
                qs[g].astype(BF16), fresh_keys[g], (((1,), (1,)), ((), ())), preferred_element_type=F32
            )
            * scale
        )
        fresh.append(jnp.where(fresh_live, scores, -1e30))

    slot = lax.broadcasted_iota(jnp.int32, (1, slots), 1)
    for r in range(requests):
        rows = slice(r * per_request, (r + 1) * per_request)
        q = jnp.concatenate([qs[g, rows, :] for g in range(groups)], axis=0).astype(BF16)
        scores = (
            lax.dot_general(q, k_ref[r], (((1,), (1,)), ((), ())), preferred_element_type=F32) * scale
        )
        live = slot < len_ref[r] * groups
        weights, fresh_weights = [], []
        for g in range(groups):
            mine = live & (lax.rem(slot, groups) == g)
            s = jnp.where(mine, scores[g * per_request : (g + 1) * per_request], -1e30)
            f = fresh[g][rows]
            top = jnp.maximum(s.max(axis=1, keepdims=True), f.max(axis=1, keepdims=True))
            e, fe = jnp.exp(s - top), jnp.exp(f - top)
            inverse = 1.0 / (e.sum(axis=1, keepdims=True) + fe.sum(axis=1, keepdims=True))
            weights.append((e * inverse).astype(BF16))
            fresh_weights.append((fe * inverse).astype(BF16))
        total = jnp.dot(jnp.concatenate(weights, axis=0), v_ref[r], preferred_element_type=F32)
        for g in range(groups):
            at[g, rows, :] = total[g * per_request : (g + 1) * per_request] + jnp.dot(
                fresh_weights[g], fresh_values[g], preferred_element_type=F32
            )
    for g in range(groups):
        for h in range(per_group):
            c = (g * per_group + h) * head_dim
            out_ref[:, c : c + head_dim] = at[g, pl.ds(h, tokens, stride=HEAD_PAD), :].astype(BF16)


def attend(own, received, keys, values, lengths, cosine, sine, groups):
    tokens, width = own.shape
    head_dim = keys.shape[2]
    per_group = width // (groups * head_dim) - 2
    ngx = len(received) + 1
    return pl.pallas_call(
        functools.partial(attend_kernel, ngx, groups, per_group),
        out_shape=pltpu.VMEM((tokens, groups * per_group * head_dim), BF16),
        in_specs=[IN_VMEM] * (ngx + 2) + [IN_SMEM] + [IN_VMEM] * 2,
        out_specs=IN_VMEM,
        scratch_shapes=[
            pltpu.VMEM((groups, tokens * HEAD_PAD, head_dim), F32),
            pltpu.VMEM((groups, tokens * HEAD_PAD, head_dim), F32),
        ],
        cost_estimate=pl.CostEstimate(flops=1 << 30, bytes_accessed=8 << 20, transcendentals=1 << 20),
        compiler_params=pltpu.CompilerParams(vmem_limit_bytes=12 << 20),
        name="attend",
    )(own, *received, vmem(keys), vmem(values), lengths, cosine, sine)


def output_kernel(ngx, ngy, tile, *refs):
    a_refs = refs[:ngx]
    w_ref = refs[ngx]
    own_ref, send_refs = refs[ngx + 1], refs[ngx + 2 : ngx + 1 + ngy]
    xs, acc = refs[ngx + 1 + ngy :]
    me_x, me_y = lax.axis_index("gx"), lax.axis_index("gy")
    block_rows = a_refs[0].shape[0]
    for step in range(ngx):
        xs[rows_at(partner(me_x, step, ngx), block_rows), :] = a_refs[step][...]

    @pl.loop(0, w_ref.shape[1] // tile)
    def _(i):
        columns = pl.ds(pl.multiple_of(i * tile, tile), tile)
        acc[:, columns] = jnp.dot(xs[...], w_ref[:, columns], preferred_element_type=F32)

    part = own_ref.shape[0]
    own_ref[...] = acc[rows_at(me_y, part), :]
    for step in range(1, ngy):
        send_refs[step - 1][...] = acc[rows_at(target(me_y, step, ngy), part), :].astype(BF16)


def output(blocks, weight, ngx, ngy):
    depth, width = weight.shape
    rows = blocks[0].shape[0] * ngx
    part = rows // ngy
    return pl.pallas_call(
        functools.partial(output_kernel, ngx, ngy, tile_of(width)),
        out_shape=[pltpu.VMEM((part, width), F32)] + [pltpu.VMEM((part, width), BF16)] * (ngy - 1),
        in_specs=[IN_VMEM] * (ngx + 1),
        out_specs=[IN_VMEM] * ngy,
        scratch_shapes=[pltpu.VMEM((rows, depth), BF16), pltpu.VMEM((rows, width), F32)],
        cost_estimate=pl.CostEstimate(
            flops=2 * rows * depth * width, bytes_accessed=depth * width * 2, transcendentals=0
        ),
        compiler_params=pltpu.CompilerParams(vmem_limit_bytes=8 << 20),
        name="output",
    )(*blocks, vmem(weight))


def finish_kernel(*refs):
    out_ref = refs[-1]
    total = refs[0][...]
    for ref in refs[1:-1]:
        total = total + ref[...].astype(F32)
    out_ref[...] = total.reshape(out_ref.shape).astype(BF16)


def finish(own, received):
    rows, width = own.shape
    return pl.pallas_call(
        finish_kernel,
        out_shape=jax.ShapeDtypeStruct((rows // 2, 2, width), BF16),
        in_specs=[IN_VMEM] * (1 + len(received)),
        out_specs=IN_VMEM,
        compiler_params=pltpu.CompilerParams(vmem_limit_bytes=8 << 20),
        name="finish",
    )(own, *received)


def rotary(positions, head_dim):
    frequencies = np.exp(
        np.arange(head_dim // 2, dtype=np.float32)
        * np.float32(-2.0 * math.log(500000.0) / head_dim)
    ).astype(np.float32)
    step_pos = positions.astype(F32)[:, None] + jnp.arange(2, dtype=F32)[None, :]
    turned = step_pos[:, :, None] * frequencies
    cosine, sine = jnp.cos(turned), jnp.sin(turned)
    rows = 2 * positions.shape[0]
    return (
        jnp.concatenate([cosine, cosine], axis=-1).reshape(rows, head_dim),
        jnp.concatenate([-sine, sine], axis=-1).reshape(rows, head_dim),
    )


def on_device(
    ngx, ngy, hidden_in, joined_projection_weight, w_out, key_cache, cached_value_rows, lengths, positions
):
    requests, cache_len, groups, head_dim = key_cache.shape
    keys = key_cache.reshape(requests, cache_len * groups, head_dim)
    values = cached_value_rows.reshape(requests, cache_len * groups, head_dim)
    cosine, sine = rotary(positions, head_dim)

    blocks = [hidden_in] + [swap(hidden_in, "gy", s, ngy) for s in range(1, ngy)]
    width = joined_projection_weight.shape[1]
    tile = tile_of(width)
    tiles = width // tile
    wa = fetch(joined_projection_weight, max(1, tiles * 4 // 7) * tile, tile, "fetch_joined")
    made = project(blocks, wa, joined_projection_weight, keys, values, ngx, ngy)
    own, sends, keys_near, values_near = made[0], made[1:ngx], made[ngx], made[ngx + 1]

    received = [swap(sends[s - 1], "gx", s, ngx) for s in range(1, ngx)]
    wo = fetch(w_out, w_out.shape[1], tile_of(w_out.shape[1]), "fetch_out", (own,))
    attended = attend(own, received, keys_near, values_near, lengths, cosine, sine, groups)

    parts = [attended] + [swap(attended, "gx", s, ngx) for s in range(1, ngx)]
    made = output(parts, wo, ngx, ngy)
    return finish(made[0], [swap(made[s], "gy", s, ngy) for s in range(1, ngy)])


def solution(mesh):
    in_specs = (
        P(("groups", "gy"), None, "gx"),
        P("gx", "gy"),
        P("gy", "gx"),
        P(("groups", "gx"), None, "gy", None),
        P(("groups", "gx"), None, "gy", None),
        P(("groups", "gx")),
        P(("groups", "gx")),
    )
    out_specs = P(("groups", "gy"), None, "gx")
    return jax.shard_map(
        functools.partial(on_device, mesh.shape["gx"], mesh.shape["gy"]),
        mesh=mesh,
        in_specs=in_specs,
        out_specs=out_specs,
        check_vma=False,
    )
```

time: 121 us -> 64.4 us (0.53)
  waiting for transfers between devices: 49.2 us -> 15.5 us
  Pallas kernels: 0 us -> 33.4 us
  matrix products: 27.5 us -> 0 us
  blocking collectives: 23.7 us -> 0 us
  starting transfers between devices: 0.04 us -> 14.2 us
  between operations: 13.5 us -> 0.14 us
  local copies, waits for them, and re-layouts: 4.62 us -> 0.1 us
    reduce_scatter x2 -> x0, waiting for transfers between devices: 49.1 us -> none  [the longest x1 25.7 us: on_device(): lax.psum_scatter(jnp.einsum('rtd,df->rtf', gathered, joined_projection_we...]
    pallas_call x0 -> x6, Pallas kernels: none -> 33.4 us  [the longest x2 14.5 us: fetch(): pl.pallas_call(kernel, out_shape=pltpu.VMEM((depth, columns), weight.dtyp...]
    dot_general x6 -> x0, matrix products: 27.5 us -> none  [the longest x1 12.9 us: on_device(): jnp.einsum('rtd,df->rtf', gathered, joined_projection_weight, preferred_e...]
    all_gather x2 -> x0, blocking collectives: 23.7 us -> none  [the longest x1 15.1 us: on_device(): lax.all_gather(attended, 'gx', axis=0, tiled=True)]
    ppermute x0 -> x12, waiting for transfers between devices: none -> 15.5 us  [swap(): lax.ppermute(block, axis, [(i, target(i, step, count)) for i in range(cou...]
    ppermute x0 -> x12, starting transfers between devices: none -> 14.2 us  [swap(): lax.ppermute(block, axis, [(i, target(i, step, count)) for i in range(cou...]
    slice x3 -> x0, local copies, waits for them, and re-layouts: 2.57 us -> none  [the longest x1 1.13 us: rotate(): second = values[..., half_dim:]]
  transfers between devices with their start and end apart: 2 -> 12, of which waited for: 2 -> 4; matrix products, arithmetic and copies ran while one was open for 0% -> 2% of each run, Pallas kernels for 0% -> 23%
where the time goes in v1:
time: 64.4 us; the launch traced here: 64.2 us
  Pallas kernels  33.4 us (52%)
  waiting for transfers between devices  15.5 us (24%)
  starting transfers between devices  14.2 us (22%)
  other arithmetic  0.92 us (1%)
    ppermute x12, waiting for transfers between devices, swap(): lax.ppermute(block, axis, [(i, target(i, step, count)) for i in range(cou...  15.5 us
    pallas_call x2, Pallas kernels, fetch(): pl.pallas_call(kernel, out_shape=pltpu.VMEM((depth, columns), weight.dtyp...  14.5 us
    ppermute x12, starting transfers between devices, swap(): lax.ppermute(block, axis, [(i, target(i, step, count)) for i in range(cou...  14.2 us
    pallas_call x1, Pallas kernels, project(): pl.pallas_call(functools.partial(project_kernel, ngx, ngy, tile, ready),...  7.59 us
    pallas_call x1, Pallas kernels, output(): pl.pallas_call(functools.partial(output_kernel, ngx, ngy, tile_of(width))...  5.43 us
    pallas_call x1, Pallas kernels, attend(): pl.pallas_call(functools.partial(attend_kernel, ngx, groups, per_group),...  5.02 us
  transfers between devices with their start and end apart: 12, of which 4 were waited for; matrix products, arithmetic and copies ran while one was open for 2% of the time, Pallas kernels for 23%

profile of v1, /device:TPU:0, one launch (start us, length us, event | category | flops | bytes accessed | tf_op | source)
XLA Modules:
  0.0 64.2 jit_solution(7427976089386196010)
XLA Ops:
  0.0 2.9 %collective-permute-start.1 = (bf16[8,2,4096]{2,1,0:T(2,128)(2,1)}, bf16[8,2,4096]{2,1,0:T(2,128)(2,1)S(1)}, u32[]{:S(2)}, u32[]{:S(2)}) collective-permute-start(bf16[8,2,4096]{2,1,0:T(2,128)(2,1)} %refs_0_.4), channel_id=1, source_target_pairs={{0,2},{1,3},{2,0},{3,1},{4,6},{5,7},{6,4},{7,5},{8,10},{9,11},{10,... | collective-permute-start | bytes 393224 | tf_op jit(solution)/shard_map/ppermute | solution.py:33
  2.9 0.0 collective-permute-start
  2.9 0.1 collective-permute-start.2
  3.1 0.7 %convert_element_type.3 = f32[8]{0:T(128)S(1)} convert(s32[8]{0:T(128)} %param.14) | non-fusion elementwise | flops 8 | bytes 64 | tf_op jit(solution)/shard_map/convert_element_type | solution.py:313
  3.7 0.1 iota_add_fusion
  3.8 0.1 add.23
  3.9 0.0 copy-start
  3.9 6.1 %fetch_joined.1.refs_4_ = bf16[4096,2048]{1,0:T(8,128)(2,1)S(1)} custom-call(bf16[4096,3584]{1,0:T(8,128)(2,1)} %refs_5_.1), custom_call_target="tpu_custom_call" | custom-call | bytes 33554432 | tf_op jit(solution)/shard_map/fetch_joined/pallas_call | solution.py:76
  10.0 0.0 collective-permute-done.1.refs_2_
  10.0 0.0 collective-permute-done.refs_1_
  10.0 0.0 collective-permute-done.2.refs_3_
  10.0 0.0 copy-done
  10.0 0.0 copy-start.2
  10.0 0.0 copy-start.1
  10.1 7.6 %project.1 = (f32[16,3584]{1,0:T(8,128)S(1)}, bf16[16,3584]{1,0:T(8,128)(2,1)S(1)}, bf16[16,3584]{1,0:T(8,128)(2,1)S(1)}, bf16[16,3584]{1,0:T(8,128)(2,1)S(1)}, ...) custom-call(bf16[8,2,4096]{2,1,0:T(2,128)(2,1)S(1)} %copy-done, ...), custom_call_target="tpu_custom_call" | custom-call | flops 1879048192 | bytes 29360128 | tf_op jit(solution)/shard_map/project/pallas_call | solution.py:138
  17.7 2.2 %collective-permute-start.3 = (bf16[16,3584]{1,0:T(8,128)(2,1)S(1)}, bf16[16,3584]{1,0:T(8,128)(2,1)S(1)}, u32[]{:S(2)}, u32[]{:S(2)}) collective-permute-start(bf16[16,3584]{1,0:T(8,128)(2,1)S(1)} %get-tuple-element.16), channel_id=1, source_target_pairs={{0,4},{4,0},{8,12},{12,8},{1,5},{5,1},{9,13},{13,9},{2,6},{6,2},{1... | collective-permute-start | bytes 344072 | tf_op jit(solution)/shard_map/ppermute | solution.py:33
  19.8 2.6 %collective-permute-start.4 = (bf16[16,3584]{1,0:T(8,128)(2,1)S(1)}, bf16[16,3584]{1,0:T(8,128)(2,1)S(1)}, u32[]{:S(2)}, u32[]{:S(2)}) collective-permute-start(bf16[16,3584]{1,0:T(8,128)(2,1)S(1)} %get-tuple-element.17), channel_id=1, source_target_pairs={{0,8},{4,12},{8,0},{12,4},{1,9},{5,13},{9,1},{13,5},{2,10},{6,14},... | collective-permute-start | bytes 344072 | tf_op jit(solution)/shard_map/ppermute | solution.py:33
  22.4 0.0 collective-permute-start.5
  22.4 0.0 copy-done.2
  22.4 0.1 fusion
  22.6 0.1 pad_maximum_fusion
  22.6 1.9 %collective-permute-done.3.refs_1_ = bf16[16,3584]{1,0:T(8,128)(2,1)S(1)} collective-permute-done((bf16[16,3584]{1,0:T(8,128)(2,1)S(1)}, bf16[16,3584]{1,0:T(8,128)(2,1)S(1)}, u32[]{:S(2)}, u32[]{:S(2)}) %collective-permute-start.3) | collective-permute-done | bytes 114720 | tf_op jit(solution)/shard_map/ppermute | solution.py:33
  24.5 7.2 %collective-permute-done.4.refs_2_ = bf16[16,3584]{1,0:T(8,128)(2,1)S(1)} collective-permute-done((bf16[16,3584]{1,0:T(8,128)(2,1)S(1)}, bf16[16,3584]{1,0:T(8,128)(2,1)S(1)}, u32[]{:S(2)}, u32[]{:S(2)}) %collective-permute-start.4) | collective-permute-done | bytes 114720 | tf_op jit(solution)/shard_map/ppermute | solution.py:33
  31.7 0.0 collective-permute-done.5.refs_3_
  31.7 0.0 copy-done.1
  31.7 5.0 %attend.1.refs_0_ = bf16[16,3072]{1,0:T(8,128)(2,1)S(1)} custom-call(f32[16,3584]{1,0:T(8,128)S(1)} %get-tuple-element.15.refs_0_.refs_1_, bf16[16,3584]{1,0:T(8,128)(2,1)S(1)} %collective-permute-done.3.refs_1_, bf16[16,3584]{1,0:T(8,128)(2,1)S(1)} %collective-permute-done.4.refs_2_, bf16[16,3584]{1,0:T(8,128)(2,1)S(1)} %collective-permute-done.5.refs_3_, ...), custom_call_target="tpu_custom_call" | custom-call | flops 1073741824 | bytes 8388608 | tf_op jit(solution)/shard_map/attend/pallas_call | solution.py:234
  36.7 2.5 %collective-permute-start.8 = (bf16[16,3072]{1,0:T(8,128)(2,1)S(1)}, bf16[16,3072]{1,0:T(8,128)(2,1)S(1)}, u32[]{:S(2)}, u32[]{:S(2)}) collective-permute-start(bf16[16,3072]{1,0:T(8,128)(2,1)S(1)} %attend.1.refs_0_), channel_id=1, source_target_pairs={{0,12},{4,8},{8,4},{12,0},{1,13},{5,9},{9,5},{13,1},{2,14},{6,10},... | collective-permute-start | bytes 294920 | tf_op jit(solution)/shard_map/ppermute | solution.py:33
  39.2 0.9 %collective-permute-start.7 = (bf16[16,3072]{1,0:T(8,128)(2,1)S(1)}, bf16[16,3072]{1,0:T(8,128)(2,1)S(1)}, u32[]{:S(2)}, u32[]{:S(2)}) collective-permute-start(bf16[16,3072]{1,0:T(8,128)(2,1)S(1)} %attend.1.refs_0_), channel_id=1, source_target_pairs={{0,8},{4,12},{8,0},{12,4},{1,9},{5,13},{9,1},{13,5},{2,10},{6,14},... | collective-permute-start | bytes 294920 | tf_op jit(solution)/shard_map/ppermute | solution.py:33
  40.0 1.1 %collective-permute-start.6 = (bf16[16,3072]{1,0:T(8,128)(2,1)S(1)}, bf16[16,3072]{1,0:T(8,128)(2,1)S(1)}, u32[]{:S(2)}, u32[]{:S(2)}) collective-permute-start(bf16[16,3072]{1,0:T(8,128)(2,1)S(1)} %attend.1.refs_0_), channel_id=1, source_target_pairs={{0,4},{4,0},{8,12},{12,8},{1,5},{5,1},{9,13},{13,9},{2,6},{6,2},{1... | collective-permute-start | bytes 294920 | tf_op jit(solution)/shard_map/ppermute | solution.py:33
  41.2 8.4 %fetch_out.1.refs_4_ = bf16[3072,4096]{1,0:T(8,128)(2,1)S(1)} custom-call(bf16[3072,4096]{1,0:T(8,128)(2,1)} %refs_0_.5, f32[16,3584]{1,0:T(8,128)S(1)} %get-tuple-element.15.refs_0_.refs_1_), custom_call_target="tpu_custom_call" | custom-call | bytes 50331648 | tf_op jit(solution)/shard_map/fetch_out/pallas_call | solution.py:76
  49.6 0.0 collective-permute-done.8.refs_3_
  49.6 0.0 collective-permute-done.7.refs_2_
  49.6 0.0 collective-permute-done.6.refs_1_
  49.6 5.4 %output.1 = (f32[16,4096]{1,0:T(8,128)S(1)}, bf16[16,4096]{1,0:T(8,128)(2,1)S(1)}, bf16[16,4096]{1,0:T(8,128)(2,1)S(1)}, bf16[16,4096]{1,0:T(8,128)(2,1)S(1)}) custom-call(bf16[16,3072]{1,0:T(8,128)(2,1)S(1)} %attend.1.refs_0_, bf16[16,3072]{1,0:T(8,128)(2,1)S(1)} %collective-permute-done.6.refs_1_, bf16[16,3072]{1,0:T(8,128)(2,1)S(1)} %collective-permute-done.7.refs_2_, ...), custom_call_target="tpu_custom_call" | custom-call | flops 1610612736 | bytes 25165824 | tf_op jit(solution)/shard_map/output/pallas_call | solution.py:274
  55.0 0.1 collective-permute-start.9
  55.1 1.6 %collective-permute-start.10 = (bf16[16,4096]{1,0:T(8,128)(2,1)S(1)}, bf16[16,4096]{1,0:T(8,128)(2,1)S(1)}, u32[]{:S(2)}, u32[]{:S(2)}) collective-permute-start(bf16[16,4096]{1,0:T(8,128)(2,1)S(1)} %get-tuple-element.23), channel_id=1, source_target_pairs={{0,2},{1,3},{2,0},{3,1},{4,6},{5,7},{6,4},{7,5},{8,10},{9,11},{10,... | collective-permute-start | bytes 393224 | tf_op jit(solution)/shard_map/ppermute | solution.py:33
  56.7 0.3 collective-permute-start.11
  57.0 0.0 collective-permute-done.9.refs_1_
  57.0 4.5 %collective-permute-done.10.refs_2_ = bf16[16,4096]{1,0:T(8,128)(2,1)S(1)} collective-permute-done((bf16[16,4096]{1,0:T(8,128)(2,1)S(1)}, bf16[16,4096]{1,0:T(8,128)(2,1)S(1)}, u32[]{:S(2)}, u32[]{:S(2)}) %collective-permute-start.10) | collective-permute-done | bytes 131104 | tf_op jit(solution)/shard_map/ppermute | solution.py:33
  61.5 1.9 %collective-permute-done.11.refs_3_ = bf16[16,4096]{1,0:T(8,128)(2,1)S(1)} collective-permute-done((bf16[16,4096]{1,0:T(8,128)(2,1)S(1)}, bf16[16,4096]{1,0:T(8,128)(2,1)S(1)}, u32[]{:S(2)}, u32[]{:S(2)}) %collective-permute-start.11) | collective-permute-done | bytes 131104 | tf_op jit(solution)/shard_map/ppermute | solution.py:33
  63.4 0.8 %finish.1 = bf16[8,2,4096]{2,1,0:T(2,128)(2,1)} custom-call(f32[16,4096]{1,0:T(8,128)S(1)} %get-tuple-element.21.refs_0_, bf16[16,4096]{1,0:T(8,128)(2,1)S(1)} %collective-permute-done.9.refs_1_, bf16[16,4096]{1,0:T(8,128)(2,1)S(1)} %collective-permute-done.10.refs_2_, bf16[16,4096]{1,0:T(8,128)(2,1)S(1)} %collective-permute-done.11.refs_3_), custom_call_target="tpu_custom_call" | custom-call | tf_op jit(solution)/shard_map/finish/pallas_call | solution.py:298
Async XLA Ops:
  0.0 10.0 %collective-permute-start.1 = (bf16[8,2,4096]{2,1,0:T(2,128)(2,1)}, bf16[8,2,4096]{2,1,0:T(2,128)(2,1)S(1)}, u32[]{:S(2)}, u32[]{:S(2)}) collective-permute-start(bf16[8,2,4096]{2,1,0:T(2,128)(2,1)} %refs_0_.4), channel_id=1, source_target_pairs={{0,2},{1,3},{2,0},{3,1},{4,6},{5,7},{6,4},{7,5},{8,10},{9,11},{10,... | collective-permute-start | bytes 393224 | tf_op jit(solution)/shard_map/ppermute | solution.py:33
  2.9 7.1 %collective-permute-start = (bf16[8,2,4096]{2,1,0:T(2,128)(2,1)}, bf16[8,2,4096]{2,1,0:T(2,128)(2,1)S(1)}, u32[]{:S(2)}, u32[]{:S(2)}) collective-permute-start(bf16[8,2,4096]{2,1,0:T(2,128)(2,1)} %refs_0_.4), channel_id=1, source_target_pairs={{0,1},{1,0},{2,3},{3,2},{4,5},{5,4},{6,7},{7,6},{8,9},{9,8},{10,11... | collective-permute-start | bytes 393224 | tf_op jit(solution)/shard_map/ppermute | solution.py:33
  2.9 7.1 %collective-permute-start.2 = (bf16[8,2,4096]{2,1,0:T(2,128)(2,1)}, bf16[8,2,4096]{2,1,0:T(2,128)(2,1)S(1)}, u32[]{:S(2)}, u32[]{:S(2)}) collective-permute-start(bf16[8,2,4096]{2,1,0:T(2,128)(2,1)} %refs_0_.4), channel_id=1, source_target_pairs={{0,3},{1,2},{2,1},{3,0},{4,7},{5,6},{6,5},{7,4},{8,11},{9,10},{10,... | collective-permute-start | bytes 393224 | tf_op jit(solution)/shard_map/ppermute | solution.py:33
  3.9 6.2 %copy-start = (bf16[8,2,4096]{2,1,0:T(2,128)(2,1)S(1)}, bf16[8,2,4096]{2,1,0:T(2,128)(2,1)}, u32[]{:S(2)}) copy-start(bf16[8,2,4096]{2,1,0:T(2,128)(2,1)} %refs_0_.4) | copy-start | bytes 393220
  10.0 12.4 %copy-start.2 = (f32[64]{0:T(128)S(1)}, f32[64]{0:T(128)}, u32[]{:S(2)}) copy-start(f32[64]{0:T(128)} %constant.2.clone) | copy-start | bytes 772
  10.0 21.6 %copy-start.1 = (s32[8]{0:T(128)S(1)}, s32[8]{0:T(128)}, u32[]{:S(2)}) copy-start(s32[8]{0:T(128)} %refs_6_.1) | copy-start | bytes 100
  17.7 6.8 %collective-permute-start.3 = (bf16[16,3584]{1,0:T(8,128)(2,1)S(1)}, bf16[16,3584]{1,0:T(8,128)(2,1)S(1)}, u32[]{:S(2)}, u32[]{:S(2)}) collective-permute-start(bf16[16,3584]{1,0:T(8,128)(2,1)S(1)} %get-tuple-element.16), channel_id=1, source_target_pairs={{0,4},{4,0},{8,12},{12,8},{1,5},{5,1},{9,13},{13,9},{2,6},{6,2},{1... | collective-permute-start | bytes 344072 | tf_op jit(solution)/shard_map/ppermute | solution.py:33
  19.8 11.8 %collective-permute-start.4 = (bf16[16,3584]{1,0:T(8,128)(2,1)S(1)}, bf16[16,3584]{1,0:T(8,128)(2,1)S(1)}, u32[]{:S(2)}, u32[]{:S(2)}) collective-permute-start(bf16[16,3584]{1,0:T(8,128)(2,1)S(1)} %get-tuple-element.17), channel_id=1, source_target_pairs={{0,8},{4,12},{8,0},{12,4},{1,9},{5,13},{9,1},{13,5},{2,10},{6,14},... | collective-permute-start | bytes 344072 | tf_op jit(solution)/shard_map/ppermute | solution.py:33
  22.4 9.2 %collective-permute-start.5 = (bf16[16,3584]{1,0:T(8,128)(2,1)S(1)}, bf16[16,3584]{1,0:T(8,128)(2,1)S(1)}, u32[]{:S(2)}, u32[]{:S(2)}) collective-permute-start(bf16[16,3584]{1,0:T(8,128)(2,1)S(1)} %get-tuple-element.18), channel_id=1, source_target_pairs={{0,12},{4,8},{8,4},{12,0},{1,13},{5,9},{9,5},{13,1},{2,14},{6,10},... | collective-permute-start | bytes 344072 | tf_op jit(solution)/shard_map/ppermute | solution.py:33
  36.7 12.9 %collective-permute-start.8 = (bf16[16,3072]{1,0:T(8,128)(2,1)S(1)}, bf16[16,3072]{1,0:T(8,128)(2,1)S(1)}, u32[]{:S(2)}, u32[]{:S(2)}) collective-permute-start(bf16[16,3072]{1,0:T(8,128)(2,1)S(1)} %attend.1.refs_0_), channel_id=1, source_target_pairs={{0,12},{4,8},{8,4},{12,0},{1,13},{5,9},{9,5},{13,1},{2,14},{6,10},... | collective-permute-start | bytes 294920 | tf_op jit(solution)/shard_map/ppermute | solution.py:33
  39.2 10.4 %collective-permute-start.7 = (bf16[16,3072]{1,0:T(8,128)(2,1)S(1)}, bf16[16,3072]{1,0:T(8,128)(2,1)S(1)}, u32[]{:S(2)}, u32[]{:S(2)}) collective-permute-start(bf16[16,3072]{1,0:T(8,128)(2,1)S(1)} %attend.1.refs_0_), channel_id=1, source_target_pairs={{0,8},{4,12},{8,0},{12,4},{1,9},{5,13},{9,1},{13,5},{2,10},{6,14},... | collective-permute-start | bytes 294920 | tf_op jit(solution)/shard_map/ppermute | solution.py:33
  40.0 9.6 %collective-permute-start.6 = (bf16[16,3072]{1,0:T(8,128)(2,1)S(1)}, bf16[16,3072]{1,0:T(8,128)(2,1)S(1)}, u32[]{:S(2)}, u32[]{:S(2)}) collective-permute-start(bf16[16,3072]{1,0:T(8,128)(2,1)S(1)} %attend.1.refs_0_), channel_id=1, source_target_pairs={{0,4},{4,0},{8,12},{12,8},{1,5},{5,1},{9,13},{13,9},{2,6},{6,2},{1... | collective-permute-start | bytes 294920 | tf_op jit(solution)/shard_map/ppermute | solution.py:33
  55.0 1.9 %collective-permute-start.9 = (bf16[16,4096]{1,0:T(8,128)(2,1)S(1)}, bf16[16,4096]{1,0:T(8,128)(2,1)S(1)}, u32[]{:S(2)}, u32[]{:S(2)}) collective-permute-start(bf16[16,4096]{1,0:T(8,128)(2,1)S(1)} %get-tuple-element.22), channel_id=1, source_target_pairs={{0,1},{1,0},{2,3},{3,2},{4,5},{5,4},{6,7},{7,6},{8,9},{9,8},{10,11... | collective-permute-start | bytes 393224 | tf_op jit(solution)/shard_map/ppermute | solution.py:33
  55.1 6.4 %collective-permute-start.10 = (bf16[16,4096]{1,0:T(8,128)(2,1)S(1)}, bf16[16,4096]{1,0:T(8,128)(2,1)S(1)}, u32[]{:S(2)}, u32[]{:S(2)}) collective-permute-start(bf16[16,4096]{1,0:T(8,128)(2,1)S(1)} %get-tuple-element.23), channel_id=1, source_target_pairs={{0,2},{1,3},{2,0},{3,1},{4,6},{5,7},{6,4},{7,5},{8,10},{9,11},{10,... | collective-permute-start | bytes 393224 | tf_op jit(solution)/shard_map/ppermute | solution.py:33
  56.7 6.7 %collective-permute-start.11 = (bf16[16,4096]{1,0:T(8,128)(2,1)S(1)}, bf16[16,4096]{1,0:T(8,128)(2,1)S(1)}, u32[]{:S(2)}, u32[]{:S(2)}) collective-permute-start(bf16[16,4096]{1,0:T(8,128)(2,1)S(1)} %get-tuple-element.24), channel_id=1, source_target_pairs={{0,3},{1,2},{2,1},{3,0},{4,7},{5,6},{6,5},{7,4},{8,11},{9,10},{10,... | collective-permute-start | bytes 393224 | tf_op jit(solution)/shard_map/ppermute | solution.py:33

commit v2 on v0

v2 whole, which is shorter than its diff:
```python
import functools
import math

import jax
import jax.numpy as jnp
import numpy as np
from jax import lax
from jax.experimental import pallas as pl
from jax.experimental.pallas import tpu as pltpu
from jax.sharding import PartitionSpec as P

BF16 = jnp.bfloat16
F32 = jnp.float32
IN_VMEM = pl.BlockSpec(memory_space=pltpu.VMEM)
IN_SMEM = pl.BlockSpec(memory_space=pltpu.SMEM)
ANYWHERE = pl.BlockSpec(memory_space=pl.ANY)
HEAD_PAD = 16


def partner(index, step, count):
    if count & (count - 1) == 0:
        return index ^ step
    return lax.rem(index + count - step, count) if not isinstance(index, int) else (index - step) % count


def target(index, step, count):
    if count & (count - 1) == 0:
        return index ^ step
    return lax.rem(index + step, count) if not isinstance(index, int) else (index + step) % count


def swap(block, axis, step, count):
    return lax.ppermute(block, axis, [(i, target(i, step, count)) for i in range(count)])


def hbm(array):
    return pltpu.with_memory_space_constraint(array, pltpu.HBM)


def vmem(array):
    return pltpu.with_memory_space_constraint(array, pltpu.VMEM)


def rows_at(index, count):
    return pl.ds(pl.multiple_of(index * count, count), count)


def dot(x, w):
    return jnp.dot(x, w, preferred_element_type=F32)


def column_tiles(width, tile=512):
    return [slice(c, min(c + tile, width)) for c in range(0, width, tile)]


def columns_in_two_steps(width, body):
    half = width // 2

    if width % 256:
        for s in column_tiles(width):
            body(pl.ds(s.start, s.stop - s.start))
        return

    @pl.loop(0, 2)
    def _(step):
        for s in column_tiles(half):
            body(pl.ds(pl.multiple_of(step * half + s.start, 128), s.stop - s.start))


def cost(flops, read):
    return pl.CostEstimate(flops=flops, bytes_accessed=read, transcendentals=0)


def fetch(weight, width, keys, values, positions, frequencies, groups):
    depth = weight.shape[0]
    requests, rows, head_dim = keys.shape
    slots = rows // groups
    pieces = 4
    piece = depth // pieces

    def kernel(*refs):
        w_ref, k_ref, v_ref, pos_any, freq_any, near_ref, cos_ref, sin_ref = refs[:8]
        split_refs, rest = refs[8 : 8 + 2 * groups], refs[8 + 2 * groups :]
        raw, wide, pos_ref, freq_ref, w_sems, c_sems, s_sems = rest
        small = [
            pltpu.make_async_copy(pos_any, pos_ref, s_sems.at[0]),
            pltpu.make_async_copy(freq_any, freq_ref, s_sems.at[1]),
        ]
        for copy in small:
            copy.start()
        caches = []
        for r in range(requests):
            for n, ref in enumerate((k_ref, v_ref)):
                copy = pltpu.make_async_copy(ref.at[r], raw.at[n, r], c_sems.at[n, r])
                copy.start()
                caches.append((n, r, copy))
        copies = []
        for i in range(pieces):
            s = pl.ds(i * piece, piece)
            copy = pltpu.make_async_copy(w_ref.at[s, pl.ds(0, width)], near_ref.at[s], w_sems.at[i])
            copy.start()
            copies.append(copy)

        for copy in small:
            copy.wait()
        row = lax.broadcasted_iota(jnp.int32, (2 * requests, head_dim), 0)
        place = row % 2
        for r in range(requests):
            place = place + jnp.where(row // 2 == r, pos_ref[r], 0)
        turned = place.astype(F32) * freq_ref[...]
        lane = lax.broadcasted_iota(jnp.int32, (2 * requests, head_dim), 1)
        cos_ref[...] = jnp.cos(turned)
        sine = jnp.sin(turned)
        sin_ref[...] = jnp.where(lane < head_dim // 2, -sine, sine)

        for n, r, copy in caches:
            copy.wait()
            wide[n] = raw[n, r].astype(F32)
            for g in range(groups):
                split_refs[n * groups + g][r] = wide[n, pl.ds(g, slots, stride=groups), :].astype(BF16)
        for copy in copies:
            copy.wait()

    cache = pltpu.VMEM((requests, slots, head_dim), BF16)
    angle = pltpu.VMEM((2 * requests, head_dim), F32)
    return pl.pallas_call(
        kernel,
        out_shape=[pltpu.VMEM((depth, width), weight.dtype), angle, angle] + [cache] * (2 * groups),
        in_specs=[ANYWHERE] * 5,
        out_specs=[IN_VMEM] * (3 + 2 * groups),
        scratch_shapes=[
            pltpu.VMEM((2, requests, rows, head_dim), BF16),
            pltpu.VMEM((2, rows, head_dim), F32),
            pltpu.SMEM((requests,), jnp.int32),
            pltpu.VMEM((1, head_dim), F32),
            pltpu.SemaphoreType.DMA((pieces,)),
            pltpu.SemaphoreType.DMA((2, requests)),
            pltpu.SemaphoreType.DMA((2,)),
        ],
        cost_estimate=cost(0, 4 * depth * width),
        compiler_params=pltpu.CompilerParams(vmem_limit_bytes=12 << 20),
        name="fetch",
    )(hbm(weight), hbm(keys), hbm(values), hbm(positions), hbm(frequencies))


def project(blocks, near, weight, group, groups, width, ahead, ngx, ngy):
    depth, ready = near.shape
    late = width - ready
    count = len(blocks)
    rows = 2 * blocks[0].shape[0] * ngy if count > 1 else blocks[0].shape[0]
    part = rows // ngx
    last = group == groups - 1
    first = group * width
    pieces = 4
    piece = depth // pieces

    def kernel(*refs):
        x_refs, (near_ref, w_ref, own_ref), rest = refs[:count], refs[count : count + 3], refs[count + 3 :]
        send_refs, rest = rest[: ngx - 1], rest[ngx - 1 :]
        if not last:
            next_ref, rest = rest[0], rest[1:]
        if count > 1:
            xs, rest = rest[0], rest[1:]
        else:
            xs = x_refs[0]
        total, sems = rest[:2]

        def copies(begin, wide, to, row):
            made = []
            for i in range(pieces):
                s = pl.ds(i * piece, piece)
                copy = pltpu.make_async_copy(w_ref.at[s, pl.ds(begin, wide)], to.at[s], sems.at[row, i])
                copy.start()
                made.append(copy)
            return made

        late_copies = copies(first + ready, late, rest[2], 0) if late else []
        next_copies = [] if last else copies(first + width, ahead, next_ref, 1)
        me_x, me_y = lax.axis_index("gx"), lax.axis_index("gy")
        if count > 1:
            for step in range(ngy):
                xs[rows_at(partner(me_y, step, ngy), rows // ngy), :] = x_refs[step][...].reshape(
                    rows // ngy, depth
                )
        def product(s):
            total[:, s] = dot(xs[...], near_ref[:, s])

        columns_in_two_steps(ready, product)
        for copy in late_copies:
            copy.wait()
        for s in column_tiles(late):
            total[:, ready + s.start : ready + s.stop] = dot(xs[...], rest[2][:, s])
        own_ref[...] = total[rows_at(me_x, part), :]
        for step in range(1, ngx):
            send_refs[step - 1][...] = total[rows_at(target(me_x, step, ngx), part), :].astype(BF16)
        for copy in next_copies:
            copy.wait()

    out_shape = [pltpu.VMEM((part, width), F32)] + [pltpu.VMEM((part, width), BF16)] * (ngx - 1)
    if not last:
        out_shape.append(pltpu.VMEM((depth, ahead), weight.dtype))
    if count > 1:
        out_shape.append(pltpu.VMEM((rows, depth), BF16))
    scratch = [pltpu.VMEM((rows, width), F32), pltpu.SemaphoreType.DMA((2, pieces))]
    if late:
        scratch.append(pltpu.VMEM((depth, late), weight.dtype))
    return pl.pallas_call(
        kernel,
        out_shape=out_shape,
        in_specs=[IN_VMEM] * (count + 1) + [ANYWHERE],
        out_specs=[IN_VMEM] * len(out_shape),
        scratch_shapes=scratch,
        cost_estimate=cost(2 * rows * depth * width, 2 * depth * width),
        compiler_params=pltpu.CompilerParams(vmem_limit_bytes=14 << 20),
        name="project",
    )(*blocks, vmem(near), hbm(weight))


def attend(own, received, keys, values, lengths, cosine, sine):
    tokens, width = own.shape
    requests, slots, head_dim = keys.shape
    per_group = width // head_dim - 2
    half = head_dim // 2
    rows = 2 * HEAD_PAD
    scale = 1.0 / math.sqrt(head_dim)
    nrecv = len(received)

    def kernel(*refs):
        own_ref, recv_refs = refs[0], refs[1 : 1 + nrecv]
        k_ref, v_ref, len_ref, cos_ref, sin_ref, out_ref, qs, at, sc, wt, fw = refs[1 + nrecv :]
        cosine, sine = cos_ref[...], sin_ref[...]

        def joined(column):
            s = slice(column * head_dim, (column + 1) * head_dim)
            total = own_ref[:, s]
            for ref in recv_refs:
                total = total + ref[:, s].astype(F32)
            return total

        def rotate(x):
            return x * cosine + pltpu.roll(x, half, 1) * sine

        for h in range(HEAD_PAD):
            value = rotate(joined(h)) if h < per_group else jnp.zeros((tokens, head_dim), F32)
            qs[pl.ds(h, tokens, stride=HEAD_PAD), :] = value
        new_key = rotate(joined(per_group)).astype(BF16)
        new_value = joined(per_group + 1).astype(BF16)

        contract = (((1,), (1,)), ((), ()))
        for r in range(requests):
            s = slice(r * rows, (r + 1) * rows)
            sc[s, :] = lax.dot_general(
                qs[s, :].astype(BF16), k_ref[r], contract, preferred_element_type=F32
            )
        fresh = lax.dot_general(qs[...].astype(BF16), new_key, contract, preferred_element_type=F32)
        row = lax.broadcasted_iota(jnp.int32, fresh.shape, 0) // HEAD_PAD
        col = lax.broadcasted_iota(jnp.int32, fresh.shape, 1)
        fresh = jnp.where((row // 2 == col // 2) & (col <= row), fresh * scale, -1e30)

        slot = lax.broadcasted_iota(jnp.int32, (1, slots), 1)
        for r in range(requests):
            s = slice(r * rows, (r + 1) * rows)
            live = slot < len_ref[r]
            score = jnp.where(live, sc[s, :] * scale, -1e30)
            f = fresh[s]
            top = jnp.maximum(score.max(axis=1, keepdims=True), f.max(axis=1, keepdims=True))
            e, fe = jnp.exp(score - top), jnp.exp(f - top)
            inverse = 1.0 / (e.sum(axis=1, keepdims=True) + fe.sum(axis=1, keepdims=True))
            wt[s, :] = (e * inverse).astype(BF16)
            fw[s, :] = (fe * inverse).astype(BF16)
        at[...] = dot(fw[...], new_value)
        for r in range(requests):
            s = slice(r * rows, (r + 1) * rows)
            at[s, :] += dot(wt[s, :], v_ref[r])
        for h in range(per_group):
            out_ref[:, h * head_dim : (h + 1) * head_dim] = at[
                pl.ds(h, tokens, stride=HEAD_PAD), :
            ].astype(BF16)

    return pl.pallas_call(
        kernel,
        out_shape=pltpu.VMEM((tokens, per_group * head_dim), BF16),
        in_specs=[IN_VMEM] * (nrecv + 3) + [IN_SMEM] + [IN_VMEM] * 2,
        out_specs=IN_VMEM,
        scratch_shapes=[
            pltpu.VMEM((tokens * HEAD_PAD, head_dim), F32),
            pltpu.VMEM((tokens * HEAD_PAD, head_dim), F32),
            pltpu.VMEM((requests * rows, slots), F32),
            pltpu.VMEM((requests * rows, slots), BF16),
            pltpu.VMEM((requests * rows, tokens), BF16),
        ],
        cost_estimate=cost(1 << 31, 12 << 20),
        compiler_params=pltpu.CompilerParams(vmem_limit_bytes=10 << 20),
        name="attend",
    )(own, *received, keys, values, lengths, cosine, sine)


def project_out(blocks, acc, weight, first, last, ngx, ngy):
    width = weight.shape[1]
    block_rows, depth = blocks[0].shape
    rows = block_rows * ngx
    part = rows // ngy

    def kernel(*refs):
        a_refs, w_ref, rest = refs[:ngx], refs[ngx], refs[ngx + 1 :]
        if acc is not None:
            acc_ref, rest = rest[0], rest[1:]
        outs, rest = (rest[:ngy], rest[ngy:]) if last else (rest[:1], rest[1:])
        xs = rest[0]
        total = rest[1] if last else outs[0]
        me_x, me_y = lax.axis_index("gx"), lax.axis_index("gy")
        for step in range(ngx):
            xs[rows_at(partner(me_x, step, ngx), block_rows), :] = a_refs[step][...]
        for s in column_tiles(width):
            product = dot(xs[...], w_ref[first : first + depth, s])
            total[:, s] = product if acc is None else acc_ref[:, s] + product
        if last:
            outs[0][...] = total[rows_at(me_y, part), :]
            for step in range(1, ngy):
                outs[step][...] = total[rows_at(target(me_y, step, ngy), part), :].astype(BF16)

    if last:
        out_shape = [pltpu.VMEM((part, width), F32)] + [pltpu.VMEM((part, width), BF16)] * (ngy - 1)
    else:
        out_shape = [pltpu.VMEM((rows, width), F32)]
    extra = [] if acc is None else [acc]
    return pl.pallas_call(
        kernel,
        out_shape=out_shape,
        in_specs=[IN_VMEM] * (ngx + 1 + len(extra)),
        out_specs=[IN_VMEM] * len(out_shape),
        scratch_shapes=[pltpu.VMEM((rows, depth), BF16)]
        + ([pltpu.VMEM((rows, width), F32)] if last else []),
        cost_estimate=cost(2 * rows * depth * width, depth * width * 2),
        compiler_params=pltpu.CompilerParams(vmem_limit_bytes=8 << 20),
        name="project_out",
    )(*blocks, weight, *extra)


def finish(own, received):
    rows, width = own.shape

    def kernel(*refs):
        total = refs[0][...]
        for ref in refs[1:-1]:
            total = total + ref[...].astype(F32)
        refs[-1][...] = total.reshape(rows // 2, 2, width).astype(BF16)

    return pl.pallas_call(
        kernel,
        out_shape=jax.ShapeDtypeStruct((rows // 2, 2, width), BF16),
        in_specs=[IN_VMEM] * (1 + len(received)),
        out_specs=IN_VMEM,
        compiler_params=pltpu.CompilerParams(vmem_limit_bytes=8 << 20),
        name="finish",
    )(own, *received)


def frequencies_of(head_dim):
    half = np.exp(
        np.arange(head_dim // 2, dtype=np.float32)
        * np.float32(-2.0 * math.log(500000.0) / head_dim)
    ).astype(np.float32)
    return jnp.asarray(np.concatenate([half, half])[None])


def on_device(
    ngx, ngy, hidden_in, joined_projection_weight, w_out, key_cache, cached_value_rows, lengths, positions
):
    requests, cache_len, groups, head_dim = key_cache.shape
    keys = key_cache.reshape(requests, cache_len * groups, head_dim)
    values = cached_value_rows.reshape(requests, cache_len * groups, head_dim)
    width = joined_projection_weight.shape[1] // groups
    near_width, ahead = width * 6 // 7 // 256 * 256, width * 4 // 7 // 256 * 256

    rows = [hidden_in] + [swap(hidden_in, "gy", s, ngy) for s in range(1, ngy)]
    near, cosine, sine, *caches = fetch(
        joined_projection_weight, near_width, keys, values, positions, frequencies_of(head_dim), groups
    )
    joined = []
    for g in range(groups):
        made = project(rows, near, joined_projection_weight, g, groups, width, ahead, ngx, ngy)
        joined.append((made[0], [swap(made[s], "gx", s, ngx) for s in range(1, ngx)]))
        if g < groups - 1:
            near = made[ngx]
        if len(rows) > 1:
            rows = [made[-1]]

    attended = []
    for g in range(groups):
        own, received = joined[g]
        mine = attend(own, received, caches[g], caches[groups + g], lengths, cosine, sine)
        attended.append([mine] + [swap(mine, "gx", s, ngx) for s in range(1, ngx)])
    total = None
    depth_out = w_out.shape[0] // groups
    for g in range(groups):
        made = project_out(attended[g], total, w_out, g * depth_out, g == groups - 1, ngx, ngy)
        total = made[0]
    return finish(made[0], [swap(made[s], "gy", s, ngy) for s in range(1, ngy)])


def solution(mesh):
    in_specs = (
        P(("groups", "gy"), None, "gx"),
        P("gx", "gy"),
        P("gy", "gx"),
        P(("groups", "gx"), None, "gy", None),
        P(("groups", "gx"), None, "gy", None),
        P(("groups", "gx")),
        P(("groups", "gx")),
    )
    out_specs = P(("groups", "gy"), None, "gx")
    return jax.shard_map(
        functools.partial(on_device, mesh.shape["gx"], mesh.shape["gy"]),
        mesh=mesh,
        in_specs=in_specs,
        out_specs=out_specs,
        check_vma=False,
    )
```

time: 121 us -> 56.6 us (0.47)
  waiting for transfers between devices: 49.2 us -> 8.41 us
  matrix products: 27.5 us -> 0 us
  Pallas kernels: 0 us -> 24.6 us
  blocking collectives: 23.7 us -> 0 us
  starting transfers between devices: 0.04 us -> 23.2 us
  between operations: 13.5 us -> 0.22 us
  local copies, waits for them, and re-layouts: 4.62 us -> 0.04 us
  other arithmetic: 2.08 us -> 0.01 us
    reduce_scatter x2 -> x0, waiting for transfers between devices: 49.1 us -> none  [the longest x1 25.7 us: on_device(): lax.psum_scatter(jnp.einsum('rtd,df->rtf', gathered, joined_projection_we...]
    dot_general x6 -> x0, matrix products: 27.5 us -> none  [the longest x1 12.9 us: on_device(): jnp.einsum('rtd,df->rtf', gathered, joined_projection_weight, preferred_e...]
    pallas_call x0 -> x8, Pallas kernels: none -> 24.6 us  [the longest x2 8.52 us: project(): pl.pallas_call(kernel, out_shape=out_shape, in_specs=[IN_VMEM] * (count +...]
    all_gather x2 -> x0, blocking collectives: 23.7 us -> none  [the longest x1 15.1 us: on_device(): lax.all_gather(attended, 'gx', axis=0, tiled=True)]
    ppermute x0 -> x18, starting transfers between devices: none -> 23.2 us  [swap(): lax.ppermute(block, axis, [(i, target(i, step, count)) for i in range(cou...]
    ppermute x0 -> x18, waiting for transfers between devices: none -> 8.41 us  [swap(): lax.ppermute(block, axis, [(i, target(i, step, count)) for i in range(cou...]
    slice x3 -> x0, local copies, waits for them, and re-layouts: 2.57 us -> none  [the longest x1 1.13 us: rotate(): second = values[..., half_dim:]]
  transfers between devices with their start and end apart: 2 -> 18, of which waited for: 2 -> 4; matrix products, arithmetic and copies ran while one was open for 0% -> 0% of each run, Pallas kernels for 0% -> 31%
where the time goes in v2:
time: 56.6 us; the launch traced here: 56.5 us
  Pallas kernels  24.6 us (43%)
  starting transfers between devices  23.2 us (41%)
  waiting for transfers between devices  8.41 us (15%)
    ppermute x18, starting transfers between devices, swap(): lax.ppermute(block, axis, [(i, target(i, step, count)) for i in range(cou...  23.2 us
    pallas_call x2, Pallas kernels, project(): pl.pallas_call(kernel, out_shape=out_shape, in_specs=[IN_VMEM] * (count +...  8.52 us
    ppermute x18, waiting for transfers between devices, swap(): lax.ppermute(block, axis, [(i, target(i, step, count)) for i in range(cou...  8.41 us
    pallas_call x1, Pallas kernels, fetch(): pl.pallas_call(kernel, out_shape=[pltpu.VMEM((depth, width), weight.dtype...  6.86 us
    pallas_call x2, Pallas kernels, project_out(): pl.pallas_call(kernel, out_shape=out_shape, in_specs=[IN_VMEM] * (ngx + 1...  4.61 us
    pallas_call x2, Pallas kernels, attend(): pl.pallas_call(kernel, out_shape=pltpu.VMEM((tokens, per_group * head_dim...  3.81 us
  transfers between devices with their start and end apart: 18, of which 4 were waited for; matrix products, arithmetic and copies ran while one was open for 0% of the time, Pallas kernels for 31%

profile of v2, /device:TPU:0, one launch (start us, length us, event | category | flops | bytes accessed | tf_op | source)
XLA Modules:
  0.0 56.5 jit_solution(2413972384738004411)
XLA Ops:
  0.0 2.9 %collective-permute-start.1 = (bf16[8,2,4096]{2,1,0:T(2,128)(2,1)}, bf16[8,2,4096]{2,1,0:T(2,128)(2,1)S(1)}, u32[]{:S(2)}, u32[]{:S(2)}) collective-permute-start(bf16[8,2,4096]{2,1,0:T(2,128)(2,1)} %refs_0_.3), channel_id=1, source_target_pairs={{0,2},{1,3},{2,0},{3,1},{4,6},{5,7},{6,4},{7,5},{8,10},{9,11},{10,... | collective-permute-start | bytes 393224 | tf_op jit(solution)/shard_map/ppermute | solution.py:33
  2.9 0.0 collective-permute-start
  2.9 0.1 collective-permute-start.2
  3.1 0.0 copy-start
  3.1 6.9 %fetch.1 = (bf16[4096,1536]{1,0:T(8,128)(2,1)S(1)}, f32[16,128]{1,0:T(8,128)S(1)}, f32[16,128]{1,0:T(8,128)S(1)}, bf16[8,768,128]{2,1,0:T(8,128)(2,1)S(1)}, bf16...) custom-call(bf16[4096,3584]{1,0:T(8,128)(2,1)} %refs_2_.1, ...), custom_call_target="tpu_custom_call" | custom-call | bytes 25165824 | tf_op jit(solution)/shard_map/fetch/pallas_call | solution.py:126
  9.9 0.0 collective-permute-done.1.refs_2_
  9.9 0.0 collective-permute-done.refs_1_
  9.9 0.0 collective-permute-done.2.refs_3_
  10.0 0.0 copy-done
  10.0 4.2 %project.2 = (f32[16,1792]{1,0:T(8,128)S(1)}, bf16[16,1792]{1,0:T(8,128)(2,1)S(1)}, bf16[16,1792]{1,0:T(8,128)(2,1)S(1)}, bf16[16,1792]{1,0:T(8,128)(2,1)S(1)}, ...) custom-call(bf16[8,2,4096]{2,1,0:T(2,128)(2,1)S(1)} %copy-done, ...), custom_call_target="tpu_custom_call" | custom-call | flops 939524096 | bytes 14680064 | tf_op jit(solution)/shard_map/project/pallas_call | solution.py:207
  14.2 2.2 %collective-permute-start.9 = (bf16[16,1792]{1,0:T(8,128)(2,1)S(1)}, bf16[16,1792]{1,0:T(8,128)(2,1)S(1)}, u32[]{:S(2)}, u32[]{:S(2)}) collective-permute-start(bf16[16,1792]{1,0:T(8,128)(2,1)S(1)} %get-tuple-element.38), channel_id=1, source_target_pairs={{0,4},{4,0},{8,12},{12,8},{1,5},{5,1},{9,13},{13,9},{2,6},{6,2},{1... | collective-permute-start | bytes 172040 | tf_op jit(solution)/shard_map/ppermute | solution.py:33
  16.4 2.6 %collective-permute-start.10 = (bf16[16,1792]{1,0:T(8,128)(2,1)S(1)}, bf16[16,1792]{1,0:T(8,128)(2,1)S(1)}, u32[]{:S(2)}, u32[]{:S(2)}) collective-permute-start(bf16[16,1792]{1,0:T(8,128)(2,1)S(1)} %get-tuple-element.39), channel_id=1, source_target_pairs={{0,8},{4,12},{8,0},{12,4},{1,9},{5,13},{9,1},{13,5},{2,10},{6,14},... | collective-permute-start | bytes 172040 | tf_op jit(solution)/shard_map/ppermute | solution.py:33
  19.0 0.0 collective-permute-start.11
  19.0 0.0 copy-start.1
  19.0 0.0 slice-start
  19.0 0.0 slice-start.1
  19.0 0.0 slice-start.2
  19.0 0.0 slice-start.3
  19.0 0.0 slice-start.4
  19.0 4.3 %project.3 = (f32[16,1792]{1,0:T(8,128)S(1)}, bf16[16,1792]{1,0:T(8,128)(2,1)S(1)}, bf16[16,1792]{1,0:T(8,128)(2,1)S(1)}, bf16[16,1792]{1,0:T(8,128)(2,1)S(1)}) custom-call(bf16[64,4096]{1,0:T(8,128)(2,1)S(1)} %get-tuple-element.27.refs_0_, bf16[4096,1024]{1,0:T(8,128)(2,1)S(1)} %get-tuple-element.28.refs_1_, bf16[4096,3584]{1,0:T(8,128)(2,1)} %refs_2_.1), custom_call_target="tpu_custom_call" | custom-call | flops 939524096 | bytes 14680064 | tf_op jit(solution)/shard_map/project/pallas_call | solution.py:207
  23.3 1.0 %collective-permute-start.3 = (bf16[16,1792]{1,0:T(8,128)(2,1)S(1)}, bf16[16,1792]{1,0:T(8,128)(2,1)S(1)}, u32[]{:S(2)}, u32[]{:S(2)}) collective-permute-start(bf16[16,1792]{1,0:T(8,128)(2,1)S(1)} %get-tuple-element.30), channel_id=1, source_target_pairs={{0,4},{4,0},{8,12},{12,8},{1,5},{5,1},{9,13},{13,9},{2,6},{6,2},{1... | collective-permute-start | bytes 172040 | tf_op jit(solution)/shard_map/ppermute | solution.py:33
  24.3 3.5 %collective-permute-start.4 = (bf16[16,1792]{1,0:T(8,128)(2,1)S(1)}, bf16[16,1792]{1,0:T(8,128)(2,1)S(1)}, u32[]{:S(2)}, u32[]{:S(2)}) collective-permute-start(bf16[16,1792]{1,0:T(8,128)(2,1)S(1)} %get-tuple-element.31), channel_id=1, source_target_pairs={{0,8},{4,12},{8,0},{12,4},{1,9},{5,13},{9,1},{13,5},{2,10},{6,14},... | collective-permute-start | bytes 172040 | tf_op jit(solution)/shard_map/ppermute | solution.py:33
  27.8 0.0 collective-permute-done.9.refs_1_
  27.8 0.0 collective-permute-start.5
  27.8 0.0 collective-permute-done.10.refs_2_
  27.8 0.0 collective-permute-done.11.refs_3_
  27.8 0.0 copy-done.1
  27.8 0.0 slice-start.5
  27.8 1.9 %attend.3.refs_0_ = bf16[16,1536]{1,0:T(8,128)(2,1)S(1)} custom-call(f32[16,1792]{1,0:T(8,128)S(1)} %get-tuple-element.37.refs_0_, bf16[16,1792]{1,0:T(8,128)(2,1)S(1)} %collective-permute-done.9.refs_1_, bf16[16,1792]{1,0:T(8,128)(2,1)S(1)} %collective-permute-done.10.refs_2_, bf16[16,1792]{1,0:T(8,128)(2,1)S(1)} %collective-permute-done.11.refs_3_, ...), custom_call_target="tpu_custom_call" | custom-call | flops 2147483648 | bytes 12582912 | tf_op jit(solution)/shard_map/attend/pallas_call | solution.py:280
  29.7 3.9 %collective-permute-start.14 = (bf16[16,1536]{1,0:T(8,128)(2,1)S(1)}, bf16[16,1536]{1,0:T(8,128)(2,1)S(1)}, u32[]{:S(2)}, u32[]{:S(2)}) collective-permute-start(bf16[16,1536]{1,0:T(8,128)(2,1)S(1)} %attend.3.refs_0_), channel_id=1, source_target_pairs={{0,12},{4,8},{8,4},{12,0},{1,13},{5,9},{9,5},{13,1},{2,14},{6,10},... | collective-permute-start | bytes 147464 | tf_op jit(solution)/shard_map/ppermute | solution.py:33
  33.6 0.0 collective-permute-start.13
  33.6 0.0 collective-permute-done.3.refs_1_
  33.6 0.6 %collective-permute-start.12 = (bf16[16,1536]{1,0:T(8,128)(2,1)S(1)}, bf16[16,1536]{1,0:T(8,128)(2,1)S(1)}, u32[]{:S(2)}, u32[]{:S(2)}) collective-permute-start(bf16[16,1536]{1,0:T(8,128)(2,1)S(1)} %attend.3.refs_0_), channel_id=1, source_target_pairs={{0,4},{4,0},{8,12},{12,8},{1,5},{5,1},{9,13},{13,9},{2,6},{6,2},{1... | collective-permute-start | bytes 147464 | tf_op jit(solution)/shard_map/ppermute | solution.py:33
  34.3 0.0 collective-permute-done.4.refs_2_
  34.3 0.2 collective-permute-done.5.refs_3_
  34.5 1.9 %attend.2.refs_0_ = bf16[16,1536]{1,0:T(8,128)(2,1)S(1)} custom-call(f32[16,1792]{1,0:T(8,128)S(1)} %get-tuple-element.29.refs_0_, bf16[16,1792]{1,0:T(8,128)(2,1)S(1)} %collective-permute-done.3.refs_1_, bf16[16,1792]{1,0:T(8,128)(2,1)S(1)} %collective-permute-done.4.refs_2_, bf16[16,1792]{1,0:T(8,128)(2,1)S(1)} %collective-permute-done.5.refs_3_, ...), custom_call_target="tpu_custom_call" | custom-call | flops 2147483648 | bytes 12582912 | tf_op jit(solution)/shard_map/attend/pallas_call | solution.py:280
  36.4 3.6 %collective-permute-start.8 = (bf16[16,1536]{1,0:T(8,128)(2,1)S(1)}, bf16[16,1536]{1,0:T(8,128)(2,1)S(1)}, u32[]{:S(2)}, u32[]{:S(2)}) collective-permute-start(bf16[16,1536]{1,0:T(8,128)(2,1)S(1)} %attend.2.refs_0_), channel_id=1, source_target_pairs={{0,12},{4,8},{8,4},{12,0},{1,13},{5,9},{9,5},{13,1},{2,14},{6,10},... | collective-permute-start | bytes 147464 | tf_op jit(solution)/shard_map/ppermute | solution.py:33
  40.0 0.0 collective-permute-start.7
  40.0 0.0 collective-permute-done.14.refs_3_
  40.0 0.8 %collective-permute-start.6 = (bf16[16,1536]{1,0:T(8,128)(2,1)S(1)}, bf16[16,1536]{1,0:T(8,128)(2,1)S(1)}, u32[]{:S(2)}, u32[]{:S(2)}) collective-permute-start(bf16[16,1536]{1,0:T(8,128)(2,1)S(1)} %attend.2.refs_0_), channel_id=1, source_target_pairs={{0,4},{4,0},{8,12},{12,8},{1,5},{5,1},{9,13},{13,9},{2,6},{6,2},{1... | collective-permute-start | bytes 147464 | tf_op jit(solution)/shard_map/ppermute | solution.py:33
  40.8 0.0 collective-permute-done.13.refs_2_
  40.8 0.0 collective-permute-done.12.refs_1_
  40.8 0.0 slice-done
  40.8 0.0 slice-done.1
  40.8 0.0 slice-done.2
  40.8 0.0 slice-done.3
  40.9 0.0 slice-done.4
  40.9 0.0 slice-done.5
  40.9 2.3 %project_out.2.refs_5_ = f32[64,4096]{1,0:T(8,128)S(1)} custom-call(bf16[16,1536]{1,0:T(8,128)(2,1)S(1)} %attend.3.refs_0_, bf16[16,1536]{1,0:T(8,128)(2,1)S(1)} %collective-permute-done.12.refs_1_, bf16[16,1536]{1,0:T(8,128)(2,1)S(1)} %collective-permute-done.13.refs_2_, bf16[16,1536]{1,0:T(8,128)(2,1)S(1)} %collective-permute-done.14.refs_3_, ...), custom_call_target="tpu_custom_call" | custom-call | flops 805306368 | bytes 12582912 | tf_op jit(solution)/shard_map/project_out/pallas_call | solution.py:327
  43.2 0.0 collective-permute-done.8.refs_3_
  43.2 1.8 %collective-permute-done.7.refs_2_ = bf16[16,1536]{1,0:T(8,128)(2,1)S(1)} collective-permute-done((bf16[16,1536]{1,0:T(8,128)(2,1)S(1)}, bf16[16,1536]{1,0:T(8,128)(2,1)S(1)}, u32[]{:S(2)}, u32[]{:S(2)}) %collective-permute-start.7) | collective-permute-done | bytes 49184 | tf_op jit(solution)/shard_map/ppermute | solution.py:33
  45.0 0.0 collective-permute-done.6.refs_1_
  45.0 2.3 %project_out.3 = (f32[16,4096]{1,0:T(8,128)S(1)}, bf16[16,4096]{1,0:T(8,128)(2,1)S(1)}, bf16[16,4096]{1,0:T(8,128)(2,1)S(1)}, bf16[16,4096]{1,0:T(8,128)(2,1)S(1)}) custom-call(bf16[16,1536]{1,0:T(8,128)(2,1)S(1)} %attend.2.refs_0_, bf16[16,1536]{1,0:T(8,128)(2,1)S(1)} %collective-permute-done.6.refs_1_, ...), custom_call_target="tpu_custom_call" | custom-call | flops 805306368 | bytes 12582912 | tf_op jit(solution)/shard_map/project_out/pallas_call | solution.py:327
  47.3 0.1 collective-permute-start.15
  47.4 1.6 %collective-permute-start.16 = (bf16[16,4096]{1,0:T(8,128)(2,1)S(1)}, bf16[16,4096]{1,0:T(8,128)(2,1)S(1)}, u32[]{:S(2)}, u32[]{:S(2)}) collective-permute-start(bf16[16,4096]{1,0:T(8,128)(2,1)S(1)} %get-tuple-element.45), channel_id=1, source_target_pairs={{0,2},{1,3},{2,0},{3,1},{4,6},{5,7},{6,4},{7,5},{8,10},{9,11},{10,... | collective-permute-start | bytes 393224 | tf_op jit(solution)/shard_map/ppermute | solution.py:33
  48.9 0.3 collective-permute-start.17
  49.2 0.0 collective-permute-done.15.refs_1_
  49.2 4.5 %collective-permute-done.16.refs_2_ = bf16[16,4096]{1,0:T(8,128)(2,1)S(1)} collective-permute-done((bf16[16,4096]{1,0:T(8,128)(2,1)S(1)}, bf16[16,4096]{1,0:T(8,128)(2,1)S(1)}, u32[]{:S(2)}, u32[]{:S(2)}) %collective-permute-start.16) | collective-permute-done | bytes 131104 | tf_op jit(solution)/shard_map/ppermute | solution.py:33
  53.7 1.9 %collective-permute-done.17.refs_3_ = bf16[16,4096]{1,0:T(8,128)(2,1)S(1)} collective-permute-done((bf16[16,4096]{1,0:T(8,128)(2,1)S(1)}, bf16[16,4096]{1,0:T(8,128)(2,1)S(1)}, u32[]{:S(2)}, u32[]{:S(2)}) %collective-permute-start.17) | collective-permute-done | bytes 131104 | tf_op jit(solution)/shard_map/ppermute | solution.py:33
  55.6 0.8 %finish.1 = bf16[8,2,4096]{2,1,0:T(2,128)(2,1)} custom-call(f32[16,4096]{1,0:T(8,128)S(1)} %get-tuple-element.43.refs_0_, bf16[16,4096]{1,0:T(8,128)(2,1)S(1)} %collective-permute-done.15.refs_1_, bf16[16,4096]{1,0:T(8,128)(2,1)S(1)} %collective-permute-done.16.refs_2_, bf16[16,4096]{1,0:T(8,128)(2,1)S(1)} %collective-permute-done.17.refs_3_), custom_call_target="tpu_custom_call" | custom-call | tf_op jit(solution)/shard_map/finish/pallas_call | solution.py:349
  (1 shorter events, 0.0 us)
Async XLA Ops:
  0.0 9.9 %collective-permute-start.1 = (bf16[8,2,4096]{2,1,0:T(2,128)(2,1)}, bf16[8,2,4096]{2,1,0:T(2,128)(2,1)S(1)}, u32[]{:S(2)}, u32[]{:S(2)}) collective-permute-start(bf16[8,2,4096]{2,1,0:T(2,128)(2,1)} %refs_0_.3), channel_id=1, source_target_pairs={{0,2},{1,3},{2,0},{3,1},{4,6},{5,7},{6,4},{7,5},{8,10},{9,11},{10,... | collective-permute-start | bytes 393224 | tf_op jit(solution)/shard_map/ppermute | solution.py:33
  2.9 7.0 %collective-permute-start = (bf16[8,2,4096]{2,1,0:T(2,128)(2,1)}, bf16[8,2,4096]{2,1,0:T(2,128)(2,1)S(1)}, u32[]{:S(2)}, u32[]{:S(2)}) collective-permute-start(bf16[8,2,4096]{2,1,0:T(2,128)(2,1)} %refs_0_.3), channel_id=1, source_target_pairs={{0,1},{1,0},{2,3},{3,2},{4,5},{5,4},{6,7},{7,6},{8,9},{9,8},{10,11... | collective-permute-start | bytes 393224 | tf_op jit(solution)/shard_map/ppermute | solution.py:33
  2.9 7.0 %collective-permute-start.2 = (bf16[8,2,4096]{2,1,0:T(2,128)(2,1)}, bf16[8,2,4096]{2,1,0:T(2,128)(2,1)S(1)}, u32[]{:S(2)}, u32[]{:S(2)}) collective-permute-start(bf16[8,2,4096]{2,1,0:T(2,128)(2,1)} %refs_0_.3), channel_id=1, source_target_pairs={{0,3},{1,2},{2,1},{3,0},{4,7},{5,6},{6,5},{7,4},{8,11},{9,10},{10,... | collective-permute-start | bytes 393224 | tf_op jit(solution)/shard_map/ppermute | solution.py:33
  3.1 6.9 %copy-start = (bf16[8,2,4096]{2,1,0:T(2,128)(2,1)S(1)}, bf16[8,2,4096]{2,1,0:T(2,128)(2,1)}, u32[]{:S(2)}) copy-start(bf16[8,2,4096]{2,1,0:T(2,128)(2,1)} %refs_0_.3) | copy-start | bytes 393220
  14.2 13.6 %collective-permute-start.9 = (bf16[16,1792]{1,0:T(8,128)(2,1)S(1)}, bf16[16,1792]{1,0:T(8,128)(2,1)S(1)}, u32[]{:S(2)}, u32[]{:S(2)}) collective-permute-start(bf16[16,1792]{1,0:T(8,128)(2,1)S(1)} %get-tuple-element.38), channel_id=1, source_target_pairs={{0,4},{4,0},{8,12},{12,8},{1,5},{5,1},{9,13},{13,9},{2,6},{6,2},{1... | collective-permute-start | bytes 172040 | tf_op jit(solution)/shard_map/ppermute | solution.py:33
  16.4 11.4 %collective-permute-start.10 = (bf16[16,1792]{1,0:T(8,128)(2,1)S(1)}, bf16[16,1792]{1,0:T(8,128)(2,1)S(1)}, u32[]{:S(2)}, u32[]{:S(2)}) collective-permute-start(bf16[16,1792]{1,0:T(8,128)(2,1)S(1)} %get-tuple-element.39), channel_id=1, source_target_pairs={{0,8},{4,12},{8,0},{12,4},{1,9},{5,13},{9,1},{13,5},{2,10},{6,14},... | collective-permute-start | bytes 172040 | tf_op jit(solution)/shard_map/ppermute | solution.py:33
  19.0 8.8 %collective-permute-start.11 = (bf16[16,1792]{1,0:T(8,128)(2,1)S(1)}, bf16[16,1792]{1,0:T(8,128)(2,1)S(1)}, u32[]{:S(2)}, u32[]{:S(2)}) collective-permute-start(bf16[16,1792]{1,0:T(8,128)(2,1)S(1)} %get-tuple-element.40), channel_id=1, source_target_pairs={{0,12},{4,8},{8,4},{12,0},{1,13},{5,9},{9,5},{13,1},{2,14},{6,10},... | collective-permute-start | bytes 172040 | tf_op jit(solution)/shard_map/ppermute | solution.py:33
  19.0 8.8 %copy-start.1 = (s32[8]{0:T(128)S(1)}, s32[8]{0:T(128)}, u32[]{:S(2)}) copy-start(s32[8]{0:T(128)} %refs_6_.3) | copy-start | bytes 100
  19.0 21.9 %slice-start = ((s8[25165824]{0:T(1024)(128)(4,1)}), s8[4194304]{0:T(1024)(128)(4,1)S(1)}, s32[]{:S(2)}) async-start(s8[25165824]{0:T(1024)(128)(4,1)} %bitcast.2), calls=%async_computation | async-start | bytes 8388608
  19.0 21.9 %slice-start.1 = ((s8[25165824]{0:T(1024)(128)(4,1)}), s8[4194304]{0:T(1024)(128)(4,1)S(1)}, s32[]{:S(2)}) async-start(s8[25165824]{0:T(1024)(128)(4,1)} %bitcast.2), calls=%async_computation.1 | async-start | bytes 8388608
  19.0 21.9 %slice-start.2 = ((s8[25165824]{0:T(1024)(128)(4,1)}), s8[4194304]{0:T(1024)(128)(4,1)S(1)}, s32[]{:S(2)}) async-start(s8[25165824]{0:T(1024)(128)(4,1)} %bitcast.2), calls=%async_computation.2 | async-start | bytes 8388608
  19.0 21.9 %slice-start.3 = ((s8[25165824]{0:T(1024)(128)(4,1)}), s8[4194304]{0:T(1024)(128)(4,1)S(1)}, s32[]{:S(2)}) async-start(s8[25165824]{0:T(1024)(128)(4,1)} %bitcast.2), calls=%async_computation.3 | async-start | bytes 8388608
  19.0 21.9 %slice-start.4 = ((s8[25165824]{0:T(1024)(128)(4,1)}), s8[4194304]{0:T(1024)(128)(4,1)S(1)}, s32[]{:S(2)}) async-start(s8[25165824]{0:T(1024)(128)(4,1)} %bitcast.2), calls=%async_computation.4 | async-start | bytes 8388608
  23.3 10.3 %collective-permute-start.3 = (bf16[16,1792]{1,0:T(8,128)(2,1)S(1)}, bf16[16,1792]{1,0:T(8,128)(2,1)S(1)}, u32[]{:S(2)}, u32[]{:S(2)}) collective-permute-start(bf16[16,1792]{1,0:T(8,128)(2,1)S(1)} %get-tuple-element.30), channel_id=1, source_target_pairs={{0,4},{4,0},{8,12},{12,8},{1,5},{5,1},{9,13},{13,9},{2,6},{6,2},{1... | collective-permute-start | bytes 172040 | tf_op jit(solution)/shard_map/ppermute | solution.py:33
  24.3 10.0 %collective-permute-start.4 = (bf16[16,1792]{1,0:T(8,128)(2,1)S(1)}, bf16[16,1792]{1,0:T(8,128)(2,1)S(1)}, u32[]{:S(2)}, u32[]{:S(2)}) collective-permute-start(bf16[16,1792]{1,0:T(8,128)(2,1)S(1)} %get-tuple-element.31), channel_id=1, source_target_pairs={{0,8},{4,12},{8,0},{12,4},{1,9},{5,13},{9,1},{13,5},{2,10},{6,14},... | collective-permute-start | bytes 172040 | tf_op jit(solution)/shard_map/ppermute | solution.py:33
  27.8 6.7 %collective-permute-start.5 = (bf16[16,1792]{1,0:T(8,128)(2,1)S(1)}, bf16[16,1792]{1,0:T(8,128)(2,1)S(1)}, u32[]{:S(2)}, u32[]{:S(2)}) collective-permute-start(bf16[16,1792]{1,0:T(8,128)(2,1)S(1)} %get-tuple-element.32), channel_id=1, source_target_pairs={{0,12},{4,8},{8,4},{12,0},{1,13},{5,9},{9,5},{13,1},{2,14},{6,10},... | collective-permute-start | bytes 172040 | tf_op jit(solution)/shard_map/ppermute | solution.py:33
  27.8 13.1 %slice-start.5 = ((s8[25165824]{0:T(1024)(128)(4,1)}), s8[4194304]{0:T(1024)(128)(4,1)S(1)}, s32[]{:S(2)}) async-start(s8[25165824]{0:T(1024)(128)(4,1)} %bitcast.2), calls=%async_computation.5 | async-start | bytes 8388608
  29.7 10.2 %collective-permute-start.14 = (bf16[16,1536]{1,0:T(8,128)(2,1)S(1)}, bf16[16,1536]{1,0:T(8,128)(2,1)S(1)}, u32[]{:S(2)}, u32[]{:S(2)}) collective-permute-start(bf16[16,1536]{1,0:T(8,128)(2,1)S(1)} %attend.3.refs_0_), channel_id=1, source_target_pairs={{0,12},{4,8},{8,4},{12,0},{1,13},{5,9},{9,5},{13,1},{2,14},{6,10},... | collective-permute-start | bytes 147464 | tf_op jit(solution)/shard_map/ppermute | solution.py:33
  33.6 7.2 %collective-permute-start.13 = (bf16[16,1536]{1,0:T(8,128)(2,1)S(1)}, bf16[16,1536]{1,0:T(8,128)(2,1)S(1)}, u32[]{:S(2)}, u32[]{:S(2)}) collective-permute-start(bf16[16,1536]{1,0:T(8,128)(2,1)S(1)} %attend.3.refs_0_), channel_id=1, source_target_pairs={{0,8},{4,12},{8,0},{12,4},{1,9},{5,13},{9,1},{13,5},{2,10},{6,14},... | collective-permute-start | bytes 147464 | tf_op jit(solution)/shard_map/ppermute | solution.py:33
  33.6 7.2 %collective-permute-start.12 = (bf16[16,1536]{1,0:T(8,128)(2,1)S(1)}, bf16[16,1536]{1,0:T(8,128)(2,1)S(1)}, u32[]{:S(2)}, u32[]{:S(2)}) collective-permute-start(bf16[16,1536]{1,0:T(8,128)(2,1)S(1)} %attend.3.refs_0_), channel_id=1, source_target_pairs={{0,4},{4,0},{8,12},{12,8},{1,5},{5,1},{9,13},{13,9},{2,6},{6,2},{1... | collective-permute-start | bytes 147464 | tf_op jit(solution)/shard_map/ppermute | solution.py:33
  36.4 6.8 %collective-permute-start.8 = (bf16[16,1536]{1,0:T(8,128)(2,1)S(1)}, bf16[16,1536]{1,0:T(8,128)(2,1)S(1)}, u32[]{:S(2)}, u32[]{:S(2)}) collective-permute-start(bf16[16,1536]{1,0:T(8,128)(2,1)S(1)} %attend.2.refs_0_), channel_id=1, source_target_pairs={{0,12},{4,8},{8,4},{12,0},{1,13},{5,9},{9,5},{13,1},{2,14},{6,10},... | collective-permute-start | bytes 147464 | tf_op jit(solution)/shard_map/ppermute | solution.py:33
  40.0 5.0 %collective-permute-start.7 = (bf16[16,1536]{1,0:T(8,128)(2,1)S(1)}, bf16[16,1536]{1,0:T(8,128)(2,1)S(1)}, u32[]{:S(2)}, u32[]{:S(2)}) collective-permute-start(bf16[16,1536]{1,0:T(8,128)(2,1)S(1)} %attend.2.refs_0_), channel_id=1, source_target_pairs={{0,8},{4,12},{8,0},{12,4},{1,9},{5,13},{9,1},{13,5},{2,10},{6,14},... | collective-permute-start | bytes 147464 | tf_op jit(solution)/shard_map/ppermute | solution.py:33
  40.0 5.0 %collective-permute-start.6 = (bf16[16,1536]{1,0:T(8,128)(2,1)S(1)}, bf16[16,1536]{1,0:T(8,128)(2,1)S(1)}, u32[]{:S(2)}, u32[]{:S(2)}) collective-permute-start(bf16[16,1536]{1,0:T(8,128)(2,1)S(1)} %attend.2.refs_0_), channel_id=1, source_target_pairs={{0,4},{4,0},{8,12},{12,8},{1,5},{5,1},{9,13},{13,9},{2,6},{6,2},{1... | collective-permute-start | bytes 147464 | tf_op jit(solution)/shard_map/ppermute | solution.py:33
  47.3 1.9 %collective-permute-start.15 = (bf16[16,4096]{1,0:T(8,128)(2,1)S(1)}, bf16[16,4096]{1,0:T(8,128)(2,1)S(1)}, u32[]{:S(2)}, u32[]{:S(2)}) collective-permute-start(bf16[16,4096]{1,0:T(8,128)(2,1)S(1)} %get-tuple-element.44), channel_id=1, source_target_pairs={{0,1},{1,0},{2,3},{3,2},{4,5},{5,4},{6,7},{7,6},{8,9},{9,8},{10,11... | collective-permute-start | bytes 393224 | tf_op jit(solution)/shard_map/ppermute | solution.py:33
  47.4 6.4 %collective-permute-start.16 = (bf16[16,4096]{1,0:T(8,128)(2,1)S(1)}, bf16[16,4096]{1,0:T(8,128)(2,1)S(1)}, u32[]{:S(2)}, u32[]{:S(2)}) collective-permute-start(bf16[16,4096]{1,0:T(8,128)(2,1)S(1)} %get-tuple-element.45), channel_id=1, source_target_pairs={{0,2},{1,3},{2,0},{3,1},{4,6},{5,7},{6,4},{7,5},{8,10},{9,11},{10,... | collective-permute-start | bytes 393224 | tf_op jit(solution)/shard_map/ppermute | solution.py:33
  48.9 6.7 %collective-permute-start.17 = (bf16[16,4096]{1,0:T(8,128)(2,1)S(1)}, bf16[16,4096]{1,0:T(8,128)(2,1)S(1)}, u32[]{:S(2)}, u32[]{:S(2)}) collective-permute-start(bf16[16,4096]{1,0:T(8,128)(2,1)S(1)} %get-tuple-element.46), channel_id=1, source_target_pairs={{0,3},{1,2},{2,1},{3,0},{4,7},{5,6},{6,5},{7,4},{8,11},{9,10},{10,... | collective-permute-start | bytes 393224 | tf_op jit(solution)/shard_map/ppermute | solution.py:33

commit v3 on v2

v3 whole, which is shorter than its diff:
```python
import functools
import math

import jax
import jax.numpy as jnp
import numpy as np
from jax import lax
from jax.experimental import pallas as pl
from jax.experimental.pallas import tpu as pltpu
from jax.sharding import PartitionSpec as P

BF16 = jnp.bfloat16
F32 = jnp.float32
IN_VMEM = pl.BlockSpec(memory_space=pltpu.VMEM)
IN_SMEM = pl.BlockSpec(memory_space=pltpu.SMEM)
ANYWHERE = pl.BlockSpec(memory_space=pl.ANY)
PIECES = 4


def partner(index, step, count):
    if count & (count - 1) == 0:
        return index ^ step
    return lax.rem(index + count - step, count) if not isinstance(index, int) else (index - step) % count


def target(index, step, count):
    if count & (count - 1) == 0:
        return index ^ step
    return lax.rem(index + step, count) if not isinstance(index, int) else (index + step) % count


def swap(block, axis, step, count):
    return lax.ppermute(block, axis, [(i, target(i, step, count)) for i in range(count)])


def hbm(array):
    return pltpu.with_memory_space_constraint(array, pltpu.HBM)


def vmem(array):
    return pltpu.with_memory_space_constraint(array, pltpu.VMEM)


def rows_at(index, count):
    return pl.ds(pl.multiple_of(index * count, count), count)


def dot(x, w):
    return jnp.dot(x, w, preferred_element_type=F32)


def column_tiles(width, tile=512):
    return [slice(c, min(c + tile, width)) for c in range(0, width, tile)]


def columns_in_two_steps(width, body):
    half = width // 2

    if width % 256:
        for s in column_tiles(width):
            body(pl.ds(s.start, s.stop - s.start))
        return

    @pl.loop(0, 2)
    def _(step):
        for s in column_tiles(half):
            body(pl.ds(pl.multiple_of(step * half + s.start, 128), s.stop - s.start))


def cost(flops, read):
    return pl.CostEstimate(flops=flops, bytes_accessed=read, transcendentals=0)


def chunks_of(groups, per_group, small=8):
    if per_group <= small:
        return [[(g, 0, per_group)] for g in range(groups)]
    first = [(g, 0, per_group) for g in range(groups - 1)] + [(groups - 1, 0, per_group - small)]
    return [first, [(groups - 1, per_group - small, small)]]


def ranges_of(chunk, per_group, unit):
    made = []
    for g, first, count in chunk:
        base = g * (per_group + 2)
        made.append([base + first, count])
        if first == 0:
            made.append([base + per_group, 2])
    merged = []
    for first, count in made:
        if merged and merged[-1][0] + merged[-1][1] == first:
            merged[-1][1] += count
        else:
            merged.append([first, count])
    return [(first * unit, count * unit) for first, count in merged]


def cut(ranges, begin, end):
    made, at = [], 0
    for first, width in ranges:
        low, high = max(begin, at), min(end, at + width)
        if low < high:
            made.append((first + low - at, low - begin, high - low))
        at += width
    return made


def copy_columns(w_ref, to, parts, sems):
    piece = w_ref.shape[0] // PIECES
    made = []
    for n, (source, place, width) in enumerate(parts):
        for i in range(PIECES):
            rows = pl.ds(i * piece, piece)
            copy = pltpu.make_async_copy(
                w_ref.at[rows, pl.ds(source, width)], to.at[rows, pl.ds(place, width)], sems.at[n, i]
            )
            copy.start()
            made.append(copy)
    return made


def fetch(weight, parts, positions, frequencies):
    depth = weight.shape[0]
    width = sum(part[2] for part in parts)
    requests, head_dim = positions.shape[0], frequencies.shape[1]

    def kernel(w_ref, pos_any, freq_any, near_ref, cos_ref, sin_ref, pos_ref, freq_ref, w_sems, s_sems):
        small = [
            pltpu.make_async_copy(pos_any, pos_ref, s_sems.at[0]),
            pltpu.make_async_copy(freq_any, freq_ref, s_sems.at[1]),
        ]
        for copy in small:
            copy.start()
        copies = copy_columns(w_ref, near_ref, parts, w_sems)
        for copy in small:
            copy.wait()
        row = lax.broadcasted_iota(jnp.int32, (2 * requests, head_dim), 0)
        place = row % 2
        for r in range(requests):
            place = place + jnp.where(row // 2 == r, pos_ref[r], 0)
        turned = place.astype(F32) * freq_ref[...]
        lane = lax.broadcasted_iota(jnp.int32, (2 * requests, head_dim), 1)
        cos_ref[...] = jnp.cos(turned)
        sine = jnp.sin(turned)
        sin_ref[...] = jnp.where(lane < head_dim // 2, -sine, sine)
        for copy in copies:
            copy.wait()

    angle = pltpu.VMEM((2 * requests, head_dim), F32)
    return pl.pallas_call(
        kernel,
        out_shape=[pltpu.VMEM((depth, width), weight.dtype), angle, angle],
        in_specs=[ANYWHERE] * 3,
        out_specs=[IN_VMEM] * 3,
        scratch_shapes=[
            pltpu.SMEM((requests,), jnp.int32),
            pltpu.VMEM((1, head_dim), F32),
            pltpu.SemaphoreType.DMA((len(parts), PIECES)),
            pltpu.SemaphoreType.DMA((2,)),
        ],
        cost_estimate=cost(0, 4 * depth * width),
        compiler_params=pltpu.CompilerParams(vmem_limit_bytes=4 << 20),
        name="fetch",
    )(hbm(weight), hbm(positions), hbm(frequencies))


def project(blocks, near, weight, ranges, coming, ngx, ngy):
    depth, ready = near.shape
    width = sum(count for _, count in ranges)
    late_tiles = column_tiles(width - ready, 256)
    late_parts = [cut(ranges, ready + t.start, ready + t.stop) for t in late_tiles]
    ahead = sum(part[2] for part in coming)
    count = len(blocks)
    rows = 2 * blocks[0].shape[0] * ngy if count > 1 else blocks[0].shape[0]
    part = rows // ngx

    def kernel(*refs):
        x_refs, (near_ref, w_ref, own_ref), rest = refs[:count], refs[count : count + 3], refs[count + 3 :]
        send_refs, rest = rest[: ngx - 1], rest[ngx - 1 :]
        if ahead:
            next_ref, rest = rest[0], rest[1:]
        if count > 1:
            xs, rest = rest[0], rest[1:]
        else:
            xs = x_refs[0]
        total, rest = rest[0], rest[1:]
        late_copies = []
        if late_tiles:
            late, late_sems, rest = rest[0], rest[1], rest[2:]
            late_copies = [
                copy_columns(w_ref, late.at[:, pl.ds(t.start, t.stop - t.start)], parts, late_sems.at[i])
                for i, (t, parts) in enumerate(zip(late_tiles, late_parts))
            ]
        next_copies = copy_columns(w_ref, next_ref, coming, rest[0]) if ahead else []
        me_x, me_y = lax.axis_index("gx"), lax.axis_index("gy")
        if count > 1:
            for step in range(ngy):
                xs[rows_at(partner(me_y, step, ngy), rows // ngy), :] = x_refs[step][...].reshape(
                    rows // ngy, depth
                )

        def product(s):
            total[:, s] = dot(xs[...], near_ref[:, s])

        columns_in_two_steps(ready, product)
        for s, arriving in zip(late_tiles, late_copies):
            for copy in arriving:
                copy.wait()
            total[:, ready + s.start : ready + s.stop] = dot(xs[...], late[:, s])
        own_ref[...] = total[rows_at(me_x, part), :]
        for step in range(1, ngx):
            send_refs[step - 1][...] = total[rows_at(target(me_x, step, ngx), part), :].astype(BF16)
        for copy in next_copies:
            copy.wait()

    out_shape = [pltpu.VMEM((part, width), F32)] + [pltpu.VMEM((part, width), BF16)] * (ngx - 1)
    if ahead:
        out_shape.append(pltpu.VMEM((depth, ahead), weight.dtype))
    if count > 1:
        out_shape.append(pltpu.VMEM((rows, depth), BF16))
    scratch = [pltpu.VMEM((rows, width), F32)]
    if late_tiles:
        scratch.append(pltpu.VMEM((depth, width - ready), weight.dtype))
        most = max(len(parts) for parts in late_parts)
        scratch.append(pltpu.SemaphoreType.DMA((len(late_tiles), most, PIECES)))
    if ahead:
        scratch.append(pltpu.SemaphoreType.DMA((len(coming), PIECES)))
    return pl.pallas_call(
        kernel,
        out_shape=out_shape,
        in_specs=[IN_VMEM] * (count + 1) + [ANYWHERE],
        out_specs=[IN_VMEM] * len(out_shape),
        scratch_shapes=scratch,
        cost_estimate=cost(2 * rows * depth * width, 2 * depth * width),
        compiler_params=pltpu.CompilerParams(vmem_limit_bytes=14 << 20),
        name="project",
    )(*blocks, vmem(near), hbm(weight))


def attend(own, received, fresh_pairs, keys, values, lengths, cosine, sine, chunk, keep, groups):
    tokens = own.shape[0]
    requests, slots, head_dim = keys.shape
    half = head_dim // 2
    scale = 1.0 / math.sqrt(head_dim)
    nrecv, npair = len(received), len(fresh_pairs)
    pads = [-(-count // 8) * 8 for _, _, count in chunk]
    starts = [2 * sum(pads[:i]) for i in range(len(pads) + 1)]
    rows, parts = starts[-1], len(chunk)

    def kernel(*refs):
        own_ref, recv_refs, rest = refs[0], refs[1 : 1 + nrecv], refs[1 + nrecv :]
        pair_refs, rest = rest[:npair], rest[npair:]
        k_ref, v_ref, len_ref, cos_ref, sin_ref, out_ref = rest[:6]
        kept_refs, rest = (rest[6:8], rest[8:]) if keep else ((), rest[6:])
        sc, wt = rest[:2]
        qs, at, fw = rest[2 : 2 + parts], rest[2 + parts : 2 + 2 * parts], rest[2 + 2 * parts :]
        cosine, sine = cos_ref[...], sin_ref[...]

        def joined(column):
            s = slice(column * head_dim, (column + 1) * head_dim)
            total = own_ref[:, s]
            for ref in recv_refs:
                total = total + ref[:, s].astype(F32)
            return total

        def rotate(x):
            return x * cosine + pltpu.roll(x, half, 1) * sine

        contract = (((1,), (1,)), ((), ()))
        column, fresh, new_values = 0, [], []
        for n, (_, first, count) in enumerate(chunk):
            pad = pads[n]
            for h in range(pad):
                value = rotate(joined(column + h)) if h < count else jnp.zeros((tokens, head_dim), F32)
                qs[n][pl.ds(h, tokens, stride=pad), :] = value
            column += count
            if first == 0:
                new_key = rotate(joined(column)).astype(BF16)
                new_value = joined(column + 1).astype(BF16)
                column += 2
            else:
                new_key, new_value = pair_refs[0][...], pair_refs[1][...]
            new_values.append(new_value)
            scores = lax.dot_general(
                qs[n][...].astype(BF16), new_key, contract, preferred_element_type=F32
            )
            row = lax.broadcasted_iota(jnp.int32, scores.shape, 0) // pad
            col = lax.broadcasted_iota(jnp.int32, scores.shape, 1)
            fresh.append(jnp.where((row // 2 == col // 2) & (col <= row), scores * scale, -1e30))
        if keep:
            kept_refs[0][...], kept_refs[1][...] = new_key, new_value

        for r in range(requests):
            q = [qs[n][2 * r * pads[n] : 2 * (r + 1) * pads[n], :].astype(BF16) for n in range(parts)]
            sc[r * rows : (r + 1) * rows, :] = lax.dot_general(
                jnp.concatenate(q, axis=0), k_ref[r], contract, preferred_element_type=F32
            )
        slot = lax.broadcasted_iota(jnp.int32, (1, slots), 1)
        mine = [lax.rem(slot, groups) == g for g, _, _ in chunk]
        for r in range(requests):
            live = slot < len_ref[r] * groups
            for n in range(parts):
                s = slice(r * rows + starts[n], r * rows + starts[n + 1])
                own_rows = slice(2 * r * pads[n], 2 * (r + 1) * pads[n])
                score = jnp.where(live & mine[n], sc[s, :] * scale, -1e30)
                f = fresh[n][own_rows]
                top = jnp.maximum(score.max(axis=1, keepdims=True), f.max(axis=1, keepdims=True))
                e, fe = jnp.exp(score - top), jnp.exp(f - top)
                inverse = 1.0 / (e.sum(axis=1, keepdims=True) + fe.sum(axis=1, keepdims=True))
                wt[s, :] = (e * inverse).astype(BF16)
                fw[n][own_rows, :] = (fe * inverse).astype(BF16)
        for n in range(parts):
            at[n][...] = dot(fw[n][...], new_values[n])
        for r in range(requests):
            total = dot(wt[r * rows : (r + 1) * rows, :], v_ref[r])
            for n in range(parts):
                at[n][2 * r * pads[n] : 2 * (r + 1) * pads[n], :] += total[starts[n] : starts[n + 1]]
        column = 0
        for n, (_, _, count) in enumerate(chunk):
            for h in range(count):
                out_ref[:, column : column + head_dim] = at[n][
                    pl.ds(h, tokens, stride=pads[n]), :
                ].astype(BF16)
                column += head_dim

    heads = sum(count for _, _, count in chunk)
    out_shape = [pltpu.VMEM((tokens, heads * head_dim), BF16)]
    if keep:
        out_shape += [pltpu.VMEM((tokens, head_dim), BF16)] * 2
    per_part = [pltpu.VMEM((tokens * pad, head_dim), F32) for pad in pads]
    return pl.pallas_call(
        kernel,
        out_shape=out_shape,
        in_specs=[IN_VMEM] * (1 + nrecv + npair + 2) + [IN_SMEM] + [IN_VMEM] * 2,
        out_specs=[IN_VMEM] * len(out_shape),
        scratch_shapes=[
            pltpu.VMEM((requests * rows, slots), F32),
            pltpu.VMEM((requests * rows, slots), BF16),
        ]
        + per_part
        + per_part
        + [pltpu.VMEM((tokens * pad, tokens), BF16) for pad in pads],
        cost_estimate=cost(1 << 31, 12 << 20),
        compiler_params=pltpu.CompilerParams(vmem_limit_bytes=10 << 20),
        name="attend",
    )(own, *received, *fresh_pairs, keys, values, lengths, cosine, sine)


def project_out(blocks, acc, weight, first, last, ngx, ngy):
    width = weight.shape[1]
    block_rows, depth = blocks[0].shape
    rows = block_rows * ngx
    part = rows // ngy

    def kernel(*refs):
        a_refs, w_ref, rest = refs[:ngx], refs[ngx], refs[ngx + 1 :]
        if acc is not None:
            acc_ref, rest = rest[0], rest[1:]
        outs, rest = (rest[:ngy], rest[ngy:]) if last else (rest[:1], rest[1:])
        xs = rest[0]
        total = rest[1] if last else outs[0]
        me_x, me_y = lax.axis_index("gx"), lax.axis_index("gy")
        for step in range(ngx):
            xs[rows_at(partner(me_x, step, ngx), block_rows), :] = a_refs[step][...]
        for s in column_tiles(width):
            product = dot(xs[...], w_ref[first : first + depth, s])
            total[:, s] = product if acc is None else acc_ref[:, s] + product
        if last:
            outs[0][...] = total[rows_at(me_y, part), :]
            for step in range(1, ngy):
                outs[step][...] = total[rows_at(target(me_y, step, ngy), part), :].astype(BF16)

    if last:
        out_shape = [pltpu.VMEM((part, width), F32)] + [pltpu.VMEM((part, width), BF16)] * (ngy - 1)
    else:
        out_shape = [pltpu.VMEM((rows, width), F32)]
    extra = [] if acc is None else [acc]
    return pl.pallas_call(
        kernel,
        out_shape=out_shape,
        in_specs=[IN_VMEM] * (ngx + 1 + len(extra)),
        out_specs=[IN_VMEM] * len(out_shape),
        scratch_shapes=[pltpu.VMEM((rows, depth), BF16)]
        + ([pltpu.VMEM((rows, width), F32)] if last else []),
        cost_estimate=cost(2 * rows * depth * width, depth * width * 2),
        compiler_params=pltpu.CompilerParams(vmem_limit_bytes=8 << 20),
        name="project_out",
    )(*blocks, weight, *extra)


def finish(own, received):
    rows, width = own.shape

    def kernel(*refs):
        total = refs[0][...]
        for ref in refs[1:-1]:
            total = total + ref[...].astype(F32)
        refs[-1][...] = total.reshape(rows // 2, 2, width).astype(BF16)

    return pl.pallas_call(
        kernel,
        out_shape=jax.ShapeDtypeStruct((rows // 2, 2, width), BF16),
        in_specs=[IN_VMEM] * (1 + len(received)),
        out_specs=IN_VMEM,
        compiler_params=pltpu.CompilerParams(vmem_limit_bytes=8 << 20),
        name="finish",
    )(own, *received)


def frequencies_of(head_dim):
    half = np.exp(
        np.arange(head_dim // 2, dtype=np.float32)
        * np.float32(-2.0 * math.log(500000.0) / head_dim)
    ).astype(np.float32)
    return jnp.asarray(np.concatenate([half, half])[None])


def on_device(
    ngx, ngy, hidden_in, joined_projection_weight, w_out, key_cache, cached_value_rows, lengths, positions
):
    requests, cache_len, groups, head_dim = key_cache.shape
    keys = key_cache.reshape(requests, cache_len * groups, head_dim)
    values = cached_value_rows.reshape(requests, cache_len * groups, head_dim)
    per_group = joined_projection_weight.shape[1] // (groups * head_dim) - 2
    chunks = chunks_of(groups, per_group)
    ranges = [ranges_of(chunk, per_group, head_dim) for chunk in chunks]
    widths = [sum(width for _, width in r) for r in ranges]

    rows = [hidden_in] + [swap(hidden_in, "gy", s, ngy) for s in range(1, ngy)]
    near, cosine, sine = fetch(
        joined_projection_weight,
        cut(ranges[0], 0, max(head_dim, widths[0] * 4 // 5 // 256 * 256)),
        positions,
        frequencies_of(head_dim),
    )
    joined = []
    for n in range(len(chunks)):
        last = n == len(chunks) - 1
        coming = [] if last else cut(ranges[n + 1], 0, max(head_dim, widths[n + 1] * 3 // 4 // 256 * 256))
        made = project(rows, near, joined_projection_weight, ranges[n], coming, ngx, ngy)
        joined.append((made[0], [swap(made[s], "gx", s, ngx) for s in range(1, ngx)]))
        if not last:
            near = made[ngx]
        if len(rows) > 1:
            rows = [made[-1]]

    attended, pair = [], []
    for n, chunk in enumerate(chunks):
        own, received = joined[n]
        keep = n + 1 < len(chunks) and chunks[n + 1][0][1] > 0
        mine, *pair = attend(
            own, received, pair, keys, values, lengths, cosine, sine, chunk, keep, groups
        )
        attended.append([mine] + [swap(mine, "gx", s, ngx) for s in range(1, ngx)])
    total, first = None, 0
    for n in range(len(chunks)):
        made = project_out(attended[n], total, w_out, first, n == len(chunks) - 1, ngx, ngy)
        first += attended[n][0].shape[1]
        total = made[0]
    return finish(made[0], [swap(made[s], "gy", s, ngy) for s in range(1, ngy)])


def solution(mesh):
    in_specs = (
        P(("groups", "gy"), None, "gx"),
        P("gx", "gy"),
        P("gy", "gx"),
        P(("groups", "gx"), None, "gy", None),
        P(("groups", "gx"), None, "gy", None),
        P(("groups", "gx")),
        P(("groups", "gx")),
    )
    out_specs = P(("groups", "gy"), None, "gx")
    return jax.shard_map(
        functools.partial(on_device, mesh.shape["gx"], mesh.shape["gy"]),
        mesh=mesh,
        in_specs=in_specs,
        out_specs=out_specs,
        check_vma=False,
    )
```

time: 56.6 us -> 54.8 us (0.968)
  Pallas kernels: 24.6 us -> 23.7 us
  waiting for transfers between devices: 8.41 us -> 7.55 us
    pallas_call x2, Pallas kernels: 8.52 us -> 7.06 us  [project(): pl.pallas_call(kernel, out_shape=out_shape, in_specs=[IN_VMEM] * (count +...]
    pallas_call x2, Pallas kernels: 3.81 us -> 5.08 us  [attend(): pl.pallas_call(kernel, out_shape=out_shape, in_specs=[IN_VMEM] * (1 + nre...]
    ppermute x18, waiting for transfers between devices: 8.41 us -> 7.55 us  [swap(): lax.ppermute(block, axis, [(i, target(i, step, count)) for i in range(cou...]
    pallas_call x1, Pallas kernels: 6.86 us -> 6.12 us  [fetch(): pl.pallas_call(kernel, out_shape=[pltpu.VMEM((depth, width), weight.dtype...]
  transfers between devices with their start and end apart: 18 -> 18, of which waited for: 4 -> 4; matrix products, arithmetic and copies ran while one was open for 0% -> 0% of each run, Pallas kernels for 31% -> 30%
where the time goes in v3:
time: 54.8 us; the launch traced here: 54.7 us
  Pallas kernels  23.7 us (43%)
  starting transfers between devices  23.1 us (42%)
  waiting for transfers between devices  7.55 us (14%)
    ppermute x18, starting transfers between devices, swap(): lax.ppermute(block, axis, [(i, target(i, step, count)) for i in range(cou...  23.1 us
    ppermute x18, waiting for transfers between devices, swap(): lax.ppermute(block, axis, [(i, target(i, step, count)) for i in range(cou...  7.55 us
    pallas_call x2, Pallas kernels, project(): pl.pallas_call(kernel, out_shape=out_shape, in_specs=[IN_VMEM] * (count +...  7.06 us
    pallas_call x1, Pallas kernels, fetch(): pl.pallas_call(kernel, out_shape=[pltpu.VMEM((depth, width), weight.dtype...  6.12 us
    pallas_call x2, Pallas kernels, attend(): pl.pallas_call(kernel, out_shape=out_shape, in_specs=[IN_VMEM] * (1 + nre...  5.08 us
    pallas_call x2, Pallas kernels, project_out(): pl.pallas_call(kernel, out_shape=out_shape, in_specs=[IN_VMEM] * (ngx + 1...  4.65 us
  transfers between devices with their start and end apart: 18, of which 4 were waited for; matrix products, arithmetic and copies ran while one was open for 0% of the time, Pallas kernels for 30%

profile of v3, /device:TPU:0, one launch (start us, length us, event | category | flops | bytes accessed | tf_op | source)
XLA Modules:
  0.0 54.7 jit_solution(18193013903010117310)
XLA Ops:
  0.0 0.0 copy-start
  0.0 2.9 %collective-permute-start.1 = (bf16[8,2,4096]{2,1,0:T(2,128)(2,1)}, bf16[8,2,4096]{2,1,0:T(2,128)(2,1)S(1)}, u32[]{:S(2)}, u32[]{:S(2)}) collective-permute-start(bf16[8,2,4096]{2,1,0:T(2,128)(2,1)} %refs_0_.1), channel_id=1, source_target_pairs={{0,2},{1,3},{2,0},{3,1},{4,6},{5,7},{6,4},{7,5},{8,10},{9,11},{10,... | collective-permute-start | bytes 393224 | tf_op jit(solution)/shard_map/ppermute | solution.py:33
  2.9 0.0 collective-permute-start
  2.9 0.2 collective-permute-start.2
  3.1 6.1 %fetch.1 = (bf16[4096,2048]{1,0:T(8,128)(2,1)S(1)}, f32[16,128]{1,0:T(8,128)S(1)}, f32[16,128]{1,0:T(8,128)S(1)}) custom-call(bf16[4096,3584]{1,0:T(8,128)(2,1)} %refs_2_.1, s32[8]{0:T(128)} %pos_any.1, f32[1,128]{1,0:T(1,128)} %constant.2.clone.freq_any), custom_call_target="tpu_custom_call" | custom-call | bytes 33554432 | tf_op jit(solution)/shard_map/fetch/pallas_call | solution.py:149
  9.3 0.0 collective-permute-done.1.refs_2_
  9.3 0.0 collective-permute-done.refs_1_
  9.3 0.0 collective-permute-done.2.refs_3_
  9.3 0.0 copy-done
  9.3 4.8 %project.2 = (f32[16,2560]{1,0:T(8,128)S(1)}, bf16[16,2560]{1,0:T(8,128)(2,1)S(1)}, bf16[16,2560]{1,0:T(8,128)(2,1)S(1)}, bf16[16,2560]{1,0:T(8,128)(2,1)S(1)}, ...) custom-call(bf16[8,2,4096]{2,1,0:T(2,128)(2,1)S(1)} %copy-done, ...), custom_call_target="tpu_custom_call" | custom-call | flops 1342177280 | bytes 20971520 | tf_op jit(solution)/shard_map/project/pallas_call | solution.py:227
  14.1 2.1 %collective-permute-start.6 = (bf16[16,2560]{1,0:T(8,128)(2,1)S(1)}, bf16[16,2560]{1,0:T(8,128)(2,1)S(1)}, u32[]{:S(2)}, u32[]{:S(2)}) collective-permute-start(bf16[16,2560]{1,0:T(8,128)(2,1)S(1)} %get-tuple-element.33), channel_id=1, source_target_pairs={{0,4},{4,0},{8,12},{12,8},{1,5},{5,1},{9,13},{13,9},{2,6},{6,2},{1... | collective-permute-start | bytes 245768 | tf_op jit(solution)/shard_map/ppermute | solution.py:33
  16.2 2.6 %collective-permute-start.7 = (bf16[16,2560]{1,0:T(8,128)(2,1)S(1)}, bf16[16,2560]{1,0:T(8,128)(2,1)S(1)}, u32[]{:S(2)}, u32[]{:S(2)}) collective-permute-start(bf16[16,2560]{1,0:T(8,128)(2,1)S(1)} %get-tuple-element.34), channel_id=1, source_target_pairs={{0,8},{4,12},{8,0},{12,4},{1,9},{5,13},{9,1},{13,5},{2,10},{6,14},... | collective-permute-start | bytes 245768 | tf_op jit(solution)/shard_map/ppermute | solution.py:33
  18.8 0.0 collective-permute-start.8
  18.8 0.0 copy-start.1
  18.8 0.0 copy-start.2
  18.8 0.0 copy-start.3
  18.9 0.0 slice-start
  18.9 0.0 slice-start.1
  18.9 0.0 slice-start.2
  18.9 0.0 slice-start.3
  18.9 0.0 slice-start.4
  18.9 2.2 %project.3 = (f32[16,1024]{1,0:T(8,128)S(1)}, bf16[16,1024]{1,0:T(8,128)(2,1)S(1)}, bf16[16,1024]{1,0:T(8,128)(2,1)S(1)}, bf16[16,1024]{1,0:T(8,128)(2,1)S(1)}) custom-call(bf16[64,4096]{1,0:T(8,128)(2,1)S(1)} %get-tuple-element.26.refs_0_, bf16[4096,768]{1,0:T(8,128)(2,1)S(1)} %get-tuple-element.27.refs_1_, bf16[4096,3584]{1,0:T(8,128)(2,1)} %refs_2_.1), custom_call_target="tpu_custom_call" | custom-call | flops 536870912 | bytes 8388608 | tf_op jit(solution)/shard_map/project/pallas_call | solution.py:227
  21.1 0.9 %collective-permute-start.3 = (bf16[16,1024]{1,0:T(8,128)(2,1)S(1)}, bf16[16,1024]{1,0:T(8,128)(2,1)S(1)}, u32[]{:S(2)}, u32[]{:S(2)}) collective-permute-start(bf16[16,1024]{1,0:T(8,128)(2,1)S(1)} %get-tuple-element.29), channel_id=1, source_target_pairs={{0,4},{4,0},{8,12},{12,8},{1,5},{5,1},{9,13},{13,9},{2,6},{6,2},{1... | collective-permute-start | bytes 98312 | tf_op jit(solution)/shard_map/ppermute | solution.py:33
  22.1 3.5 %collective-permute-start.4 = (bf16[16,1024]{1,0:T(8,128)(2,1)S(1)}, bf16[16,1024]{1,0:T(8,128)(2,1)S(1)}, u32[]{:S(2)}, u32[]{:S(2)}) collective-permute-start(bf16[16,1024]{1,0:T(8,128)(2,1)S(1)} %get-tuple-element.30), channel_id=1, source_target_pairs={{0,8},{4,12},{8,0},{12,4},{1,9},{5,13},{9,1},{13,5},{2,10},{6,14},... | collective-permute-start | bytes 98312 | tf_op jit(solution)/shard_map/ppermute | solution.py:33
  25.6 0.0 collective-permute-done.6.refs_1_
  25.6 0.0 collective-permute-start.5
  25.6 0.4 collective-permute-done.7.refs_2_
  26.0 0.0 collective-permute-done.8.refs_3_
  26.0 0.0 copy-done.1
  26.0 0.0 copy-done.2
  26.0 0.0 copy-done.3
  26.0 0.0 slice-start.5
  26.0 2.8 %attend.2 = (bf16[16,2048]{1,0:T(8,128)(2,1)S(1)}, bf16[16,128]{1,0:T(8,128)(2,1)S(1)}, bf16[16,128]{1,0:T(8,128)(2,1)S(1)}) custom-call(f32[16,2560]{1,0:T(8,128)S(1)} %get-tuple-element.32.refs_0_, bf16[16,2560]{1,0:T(8,128)(2,1)S(1)} %collective-permute-done.6.refs_1_, bf16[16,2560]{1,0:T(8,128)(2,1)S(1)} %collective-permute-done.7.refs_2_, ...), custom_call_target="tpu_custom_call" | custom-call | flops 2147483648 | bytes 12582912 | tf_op jit(solution)/shard_map/attend/pallas_call | solution.py:330
  28.8 3.5 %collective-permute-start.14 = (bf16[16,2048]{1,0:T(8,128)(2,1)S(1)}, bf16[16,2048]{1,0:T(8,128)(2,1)S(1)}, u32[]{:S(2)}, u32[]{:S(2)}) collective-permute-start(bf16[16,2048]{1,0:T(8,128)(2,1)S(1)} %get-tuple-element.40.refs_0_), channel_id=1, source_target_pairs={{0,12},{4,8},{8,4},{12,0},{1,13},{5,9},{9,5},{13,1},{2,14},{6,10},... | collective-permute-start | bytes 196616 | tf_op jit(solution)/shard_map/ppermute | solution.py:33
  32.3 0.5 collective-permute-start.13
  32.8 0.0 collective-permute-done.3.refs_1_
  32.8 0.4 collective-permute-start.12
  33.3 0.0 collective-permute-done.4.refs_2_
  33.3 0.0 collective-permute-done.5.refs_3_
  33.3 2.3 %attend.3.refs_0_ = bf16[16,1024]{1,0:T(8,128)(2,1)S(1)} custom-call(f32[16,1024]{1,0:T(8,128)S(1)} %get-tuple-element.28.refs_0_, bf16[16,1024]{1,0:T(8,128)(2,1)S(1)} %collective-permute-done.3.refs_1_, bf16[16,1024]{1,0:T(8,128)(2,1)S(1)} %collective-permute-done.4.refs_2_, bf16[16,1024]{1,0:T(8,128)(2,1)S(1)} %collective-permute-done.5.refs_3_, ...), custom_call_target="tpu_custom_call" | custom-call | flops 2147483648 | bytes 12582912 | tf_op jit(solution)/shard_map/attend/pallas_call | solution.py:330
  35.6 3.5 %collective-permute-start.11 = (bf16[16,1024]{1,0:T(8,128)(2,1)S(1)}, bf16[16,1024]{1,0:T(8,128)(2,1)S(1)}, u32[]{:S(2)}, u32[]{:S(2)}) collective-permute-start(bf16[16,1024]{1,0:T(8,128)(2,1)S(1)} %attend.3.refs_0_), channel_id=1, source_target_pairs={{0,12},{4,8},{8,4},{12,0},{1,13},{5,9},{9,5},{13,1},{2,14},{6,10},... | collective-permute-start | bytes 98312 | tf_op jit(solution)/shard_map/ppermute | solution.py:33
  39.1 0.0 collective-permute-start.10
  39.1 0.0 collective-permute-done.14.refs_3_
  39.1 0.9 %collective-permute-start.9 = (bf16[16,1024]{1,0:T(8,128)(2,1)S(1)}, bf16[16,1024]{1,0:T(8,128)(2,1)S(1)}, u32[]{:S(2)}, u32[]{:S(2)}) collective-permute-start(bf16[16,1024]{1,0:T(8,128)(2,1)S(1)} %attend.3.refs_0_), channel_id=1, source_target_pairs={{0,4},{4,0},{8,12},{12,8},{1,5},{5,1},{9,13},{13,9},{2,6},{6,2},{1... | collective-permute-start | bytes 98312 | tf_op jit(solution)/shard_map/ppermute | solution.py:33
  40.0 0.0 collective-permute-done.13.refs_2_
  40.0 0.0 collective-permute-done.12.refs_1_
  40.0 0.0 slice-done
  40.0 0.0 slice-done.1
  40.1 0.0 slice-done.2
  40.1 0.0 slice-done.3
  40.1 0.0 slice-done.4
  40.1 0.0 slice-done.5
  40.1 3.0 %project_out.2.refs_5_ = f32[64,4096]{1,0:T(8,128)S(1)} custom-call(bf16[16,2048]{1,0:T(8,128)(2,1)S(1)} %get-tuple-element.40.refs_0_, bf16[16,2048]{1,0:T(8,128)(2,1)S(1)} %collective-permute-done.12.refs_1_, bf16[16,2048]{1,0:T(8,128)(2,1)S(1)} %collective-permute-done.13.refs_2_, bf16[16,2048]{1,0:T(8,128)(2,1)S(1)} %collective-permute-done.14.refs_3_, ...), custom_call_target="tpu_custom_call" | custom-call | flops 1073741824 | bytes 16777216 | tf_op jit(solution)/shard_map/project_out/pallas_call | solution.py:377
  43.1 0.0 collective-permute-done.11.refs_3_
  43.2 0.7 %collective-permute-done.10.refs_2_ = bf16[16,1024]{1,0:T(8,128)(2,1)S(1)} collective-permute-done((bf16[16,1024]{1,0:T(8,128)(2,1)S(1)}, bf16[16,1024]{1,0:T(8,128)(2,1)S(1)}, u32[]{:S(2)}, u32[]{:S(2)}) %collective-permute-start.10) | collective-permute-done | bytes 32800 | tf_op jit(solution)/shard_map/ppermute | solution.py:33
  43.9 0.0 collective-permute-done.9.refs_1_
  43.9 1.6 %project_out.3 = (f32[16,4096]{1,0:T(8,128)S(1)}, bf16[16,4096]{1,0:T(8,128)(2,1)S(1)}, bf16[16,4096]{1,0:T(8,128)(2,1)S(1)}, bf16[16,4096]{1,0:T(8,128)(2,1)S(1)}) custom-call(bf16[16,1024]{1,0:T(8,128)(2,1)S(1)} %attend.3.refs_0_, bf16[16,1024]{1,0:T(8,128)(2,1)S(1)} %collective-permute-done.9.refs_1_, ...), custom_call_target="tpu_custom_call" | custom-call | flops 536870912 | bytes 8388608 | tf_op jit(solution)/shard_map/project_out/pallas_call | solution.py:377
  45.5 0.1 collective-permute-start.15
  45.6 1.6 %collective-permute-start.16 = (bf16[16,4096]{1,0:T(8,128)(2,1)S(1)}, bf16[16,4096]{1,0:T(8,128)(2,1)S(1)}, u32[]{:S(2)}, u32[]{:S(2)}) collective-permute-start(bf16[16,4096]{1,0:T(8,128)(2,1)S(1)} %get-tuple-element.43), channel_id=1, source_target_pairs={{0,2},{1,3},{2,0},{3,1},{4,6},{5,7},{6,4},{7,5},{8,10},{9,11},{10,... | collective-permute-start | bytes 393224 | tf_op jit(solution)/shard_map/ppermute | solution.py:33
  47.2 0.3 collective-permute-start.17
  47.5 0.0 collective-permute-done.15.refs_1_
  47.5 4.5 %collective-permute-done.16.refs_2_ = bf16[16,4096]{1,0:T(8,128)(2,1)S(1)} collective-permute-done((bf16[16,4096]{1,0:T(8,128)(2,1)S(1)}, bf16[16,4096]{1,0:T(8,128)(2,1)S(1)}, u32[]{:S(2)}, u32[]{:S(2)}) %collective-permute-start.16) | collective-permute-done | bytes 131104 | tf_op jit(solution)/shard_map/ppermute | solution.py:33
  52.0 1.9 %collective-permute-done.17.refs_3_ = bf16[16,4096]{1,0:T(8,128)(2,1)S(1)} collective-permute-done((bf16[16,4096]{1,0:T(8,128)(2,1)S(1)}, bf16[16,4096]{1,0:T(8,128)(2,1)S(1)}, u32[]{:S(2)}, u32[]{:S(2)}) %collective-permute-start.17) | collective-permute-done | bytes 131104 | tf_op jit(solution)/shard_map/ppermute | solution.py:33
  53.9 0.8 %finish.1 = bf16[8,2,4096]{2,1,0:T(2,128)(2,1)} custom-call(f32[16,4096]{1,0:T(8,128)S(1)} %get-tuple-element.41.refs_0_, bf16[16,4096]{1,0:T(8,128)(2,1)S(1)} %collective-permute-done.15.refs_1_, bf16[16,4096]{1,0:T(8,128)(2,1)S(1)} %collective-permute-done.16.refs_2_, bf16[16,4096]{1,0:T(8,128)(2,1)S(1)} %collective-permute-done.17.refs_3_), custom_call_target="tpu_custom_call" | custom-call | tf_op jit(solution)/shard_map/finish/pallas_call | solution.py:399
  (1 shorter events, 0.0 us)
Async XLA Ops:
  0.0 9.3 %copy-start = (bf16[8,2,4096]{2,1,0:T(2,128)(2,1)S(1)}, bf16[8,2,4096]{2,1,0:T(2,128)(2,1)}, u32[]{:S(2)}) copy-start(bf16[8,2,4096]{2,1,0:T(2,128)(2,1)} %refs_0_.1) | copy-start | bytes 393220
  0.0 9.3 %collective-permute-start.1 = (bf16[8,2,4096]{2,1,0:T(2,128)(2,1)}, bf16[8,2,4096]{2,1,0:T(2,128)(2,1)S(1)}, u32[]{:S(2)}, u32[]{:S(2)}) collective-permute-start(bf16[8,2,4096]{2,1,0:T(2,128)(2,1)} %refs_0_.1), channel_id=1, source_target_pairs={{0,2},{1,3},{2,0},{3,1},{4,6},{5,7},{6,4},{7,5},{8,10},{9,11},{10,... | collective-permute-start | bytes 393224 | tf_op jit(solution)/shard_map/ppermute | solution.py:33
  2.9 6.3 %collective-permute-start = (bf16[8,2,4096]{2,1,0:T(2,128)(2,1)}, bf16[8,2,4096]{2,1,0:T(2,128)(2,1)S(1)}, u32[]{:S(2)}, u32[]{:S(2)}) collective-permute-start(bf16[8,2,4096]{2,1,0:T(2,128)(2,1)} %refs_0_.1), channel_id=1, source_target_pairs={{0,1},{1,0},{2,3},{3,2},{4,5},{5,4},{6,7},{7,6},{8,9},{9,8},{10,11... | collective-permute-start | bytes 393224 | tf_op jit(solution)/shard_map/ppermute | solution.py:33
  2.9 6.3 %collective-permute-start.2 = (bf16[8,2,4096]{2,1,0:T(2,128)(2,1)}, bf16[8,2,4096]{2,1,0:T(2,128)(2,1)S(1)}, u32[]{:S(2)}, u32[]{:S(2)}) collective-permute-start(bf16[8,2,4096]{2,1,0:T(2,128)(2,1)} %refs_0_.1), channel_id=1, source_target_pairs={{0,3},{1,2},{2,1},{3,0},{4,7},{5,6},{6,5},{7,4},{8,11},{9,10},{10,... | collective-permute-start | bytes 393224 | tf_op jit(solution)/shard_map/ppermute | solution.py:33
  14.1 11.4 %collective-permute-start.6 = (bf16[16,2560]{1,0:T(8,128)(2,1)S(1)}, bf16[16,2560]{1,0:T(8,128)(2,1)S(1)}, u32[]{:S(2)}, u32[]{:S(2)}) collective-permute-start(bf16[16,2560]{1,0:T(8,128)(2,1)S(1)} %get-tuple-element.33), channel_id=1, source_target_pairs={{0,4},{4,0},{8,12},{12,8},{1,5},{5,1},{9,13},{13,9},{2,6},{6,2},{1... | collective-permute-start | bytes 245768 | tf_op jit(solution)/shard_map/ppermute | solution.py:33
  16.2 9.7 %collective-permute-start.7 = (bf16[16,2560]{1,0:T(8,128)(2,1)S(1)}, bf16[16,2560]{1,0:T(8,128)(2,1)S(1)}, u32[]{:S(2)}, u32[]{:S(2)}) collective-permute-start(bf16[16,2560]{1,0:T(8,128)(2,1)S(1)} %get-tuple-element.34), channel_id=1, source_target_pairs={{0,8},{4,12},{8,0},{12,4},{1,9},{5,13},{9,1},{13,5},{2,10},{6,14},... | collective-permute-start | bytes 245768 | tf_op jit(solution)/shard_map/ppermute | solution.py:33
  18.8 7.1 %collective-permute-start.8 = (bf16[16,2560]{1,0:T(8,128)(2,1)S(1)}, bf16[16,2560]{1,0:T(8,128)(2,1)S(1)}, u32[]{:S(2)}, u32[]{:S(2)}) collective-permute-start(bf16[16,2560]{1,0:T(8,128)(2,1)S(1)} %get-tuple-element.35), channel_id=1, source_target_pairs={{0,12},{4,8},{8,4},{12,0},{1,13},{5,9},{9,5},{13,1},{2,14},{6,10},... | collective-permute-start | bytes 245768 | tf_op jit(solution)/shard_map/ppermute | solution.py:33
  18.8 7.1 %copy-start.1 = (bf16[8,768,2,128]{3,2,1,0:T(2,128)(2,1)S(1)}, bf16[8,768,2,128]{3,2,1,0:T(2,128)(2,1)}, u32[]{:S(2)}) copy-start(bf16[8,768,2,128]{3,2,1,0:T(2,128)(2,1)} %param.11) | copy-start | bytes 9437188
  18.8 7.1 %copy-start.2 = (bf16[8,768,2,128]{3,2,1,0:T(2,128)(2,1)S(1)}, bf16[8,768,2,128]{3,2,1,0:T(2,128)(2,1)}, u32[]{:S(2)}) copy-start(bf16[8,768,2,128]{3,2,1,0:T(2,128)(2,1)} %param.12) | copy-start | bytes 9437188
  18.8 7.2 %copy-start.3 = (s32[8]{0:T(128)S(1)}, s32[8]{0:T(128)}, u32[]{:S(2)}) copy-start(s32[8]{0:T(128)} %refs_8_.1) | copy-start | bytes 100
  18.9 21.2 %slice-start = ((s8[25165824]{0:T(1024)(128)(4,1)}), s8[4194304]{0:T(1024)(128)(4,1)S(1)}, s32[]{:S(2)}) async-start(s8[25165824]{0:T(1024)(128)(4,1)} %bitcast.2), calls=%async_computation | async-start | bytes 8388608
  18.9 21.2 %slice-start.1 = ((s8[25165824]{0:T(1024)(128)(4,1)}), s8[4194304]{0:T(1024)(128)(4,1)S(1)}, s32[]{:S(2)}) async-start(s8[25165824]{0:T(1024)(128)(4,1)} %bitcast.2), calls=%async_computation.1 | async-start | bytes 8388608
  18.9 21.2 %slice-start.2 = ((s8[25165824]{0:T(1024)(128)(4,1)}), s8[4194304]{0:T(1024)(128)(4,1)S(1)}, s32[]{:S(2)}) async-start(s8[25165824]{0:T(1024)(128)(4,1)} %bitcast.2), calls=%async_computation.2 | async-start | bytes 8388608
  18.9 21.2 %slice-start.3 = ((s8[25165824]{0:T(1024)(128)(4,1)}), s8[4194304]{0:T(1024)(128)(4,1)S(1)}, s32[]{:S(2)}) async-start(s8[25165824]{0:T(1024)(128)(4,1)} %bitcast.2), calls=%async_computation.3 | async-start | bytes 8388608
  18.9 21.2 %slice-start.4 = ((s8[25165824]{0:T(1024)(128)(4,1)}), s8[4194304]{0:T(1024)(128)(4,1)S(1)}, s32[]{:S(2)}) async-start(s8[25165824]{0:T(1024)(128)(4,1)} %bitcast.2), calls=%async_computation.4 | async-start | bytes 8388608
  21.1 11.7 %collective-permute-start.3 = (bf16[16,1024]{1,0:T(8,128)(2,1)S(1)}, bf16[16,1024]{1,0:T(8,128)(2,1)S(1)}, u32[]{:S(2)}, u32[]{:S(2)}) collective-permute-start(bf16[16,1024]{1,0:T(8,128)(2,1)S(1)} %get-tuple-element.29), channel_id=1, source_target_pairs={{0,4},{4,0},{8,12},{12,8},{1,5},{5,1},{9,13},{13,9},{2,6},{6,2},{1... | collective-permute-start | bytes 98312 | tf_op jit(solution)/shard_map/ppermute | solution.py:33
  22.1 11.2 %collective-permute-start.4 = (bf16[16,1024]{1,0:T(8,128)(2,1)S(1)}, bf16[16,1024]{1,0:T(8,128)(2,1)S(1)}, u32[]{:S(2)}, u32[]{:S(2)}) collective-permute-start(bf16[16,1024]{1,0:T(8,128)(2,1)S(1)} %get-tuple-element.30), channel_id=1, source_target_pairs={{0,8},{4,12},{8,0},{12,4},{1,9},{5,13},{9,1},{13,5},{2,10},{6,14},... | collective-permute-start | bytes 98312 | tf_op jit(solution)/shard_map/ppermute | solution.py:33
  25.6 7.7 %collective-permute-start.5 = (bf16[16,1024]{1,0:T(8,128)(2,1)S(1)}, bf16[16,1024]{1,0:T(8,128)(2,1)S(1)}, u32[]{:S(2)}, u32[]{:S(2)}) collective-permute-start(bf16[16,1024]{1,0:T(8,128)(2,1)S(1)} %get-tuple-element.31), channel_id=1, source_target_pairs={{0,12},{4,8},{8,4},{12,0},{1,13},{5,9},{9,5},{13,1},{2,14},{6,10},... | collective-permute-start | bytes 98312 | tf_op jit(solution)/shard_map/ppermute | solution.py:33
  26.0 14.1 %slice-start.5 = ((s8[25165824]{0:T(1024)(128)(4,1)}), s8[4194304]{0:T(1024)(128)(4,1)S(1)}, s32[]{:S(2)}) async-start(s8[25165824]{0:T(1024)(128)(4,1)} %bitcast.2), calls=%async_computation.5 | async-start | bytes 8388608
  28.8 10.3 %collective-permute-start.14 = (bf16[16,2048]{1,0:T(8,128)(2,1)S(1)}, bf16[16,2048]{1,0:T(8,128)(2,1)S(1)}, u32[]{:S(2)}, u32[]{:S(2)}) collective-permute-start(bf16[16,2048]{1,0:T(8,128)(2,1)S(1)} %get-tuple-element.40.refs_0_), channel_id=1, source_target_pairs={{0,12},{4,8},{8,4},{12,0},{1,13},{5,9},{9,5},{13,1},{2,14},{6,10},... | collective-permute-start | bytes 196616 | tf_op jit(solution)/shard_map/ppermute | solution.py:33
  32.3 7.7 %collective-permute-start.13 = (bf16[16,2048]{1,0:T(8,128)(2,1)S(1)}, bf16[16,2048]{1,0:T(8,128)(2,1)S(1)}, u32[]{:S(2)}, u32[]{:S(2)}) collective-permute-start(bf16[16,2048]{1,0:T(8,128)(2,1)S(1)} %get-tuple-element.40.refs_0_), channel_id=1, source_target_pairs={{0,8},{4,12},{8,0},{12,4},{1,9},{5,13},{9,1},{13,5},{2,10},{6,14},... | collective-permute-start | bytes 196616 | tf_op jit(solution)/shard_map/ppermute | solution.py:33
  32.8 7.2 %collective-permute-start.12 = (bf16[16,2048]{1,0:T(8,128)(2,1)S(1)}, bf16[16,2048]{1,0:T(8,128)(2,1)S(1)}, u32[]{:S(2)}, u32[]{:S(2)}) collective-permute-start(bf16[16,2048]{1,0:T(8,128)(2,1)S(1)} %get-tuple-element.40.refs_0_), channel_id=1, source_target_pairs={{0,4},{4,0},{8,12},{12,8},{1,5},{5,1},{9,13},{13,9},{2,6},{6,2},{1... | collective-permute-start | bytes 196616 | tf_op jit(solution)/shard_map/ppermute | solution.py:33
  35.6 7.6 %collective-permute-start.11 = (bf16[16,1024]{1,0:T(8,128)(2,1)S(1)}, bf16[16,1024]{1,0:T(8,128)(2,1)S(1)}, u32[]{:S(2)}, u32[]{:S(2)}) collective-permute-start(bf16[16,1024]{1,0:T(8,128)(2,1)S(1)} %attend.3.refs_0_), channel_id=1, source_target_pairs={{0,12},{4,8},{8,4},{12,0},{1,13},{5,9},{9,5},{13,1},{2,14},{6,10},... | collective-permute-start | bytes 98312 | tf_op jit(solution)/shard_map/ppermute | solution.py:33
  39.1 4.8 %collective-permute-start.10 = (bf16[16,1024]{1,0:T(8,128)(2,1)S(1)}, bf16[16,1024]{1,0:T(8,128)(2,1)S(1)}, u32[]{:S(2)}, u32[]{:S(2)}) collective-permute-start(bf16[16,1024]{1,0:T(8,128)(2,1)S(1)} %attend.3.refs_0_), channel_id=1, source_target_pairs={{0,8},{4,12},{8,0},{12,4},{1,9},{5,13},{9,1},{13,5},{2,10},{6,14},... | collective-permute-start | bytes 98312 | tf_op jit(solution)/shard_map/ppermute | solution.py:33
  39.1 4.8 %collective-permute-start.9 = (bf16[16,1024]{1,0:T(8,128)(2,1)S(1)}, bf16[16,1024]{1,0:T(8,128)(2,1)S(1)}, u32[]{:S(2)}, u32[]{:S(2)}) collective-permute-start(bf16[16,1024]{1,0:T(8,128)(2,1)S(1)} %attend.3.refs_0_), channel_id=1, source_target_pairs={{0,4},{4,0},{8,12},{12,8},{1,5},{5,1},{9,13},{13,9},{2,6},{6,2},{1... | collective-permute-start | bytes 98312 | tf_op jit(solution)/shard_map/ppermute | solution.py:33
  45.5 1.9 %collective-permute-start.15 = (bf16[16,4096]{1,0:T(8,128)(2,1)S(1)}, bf16[16,4096]{1,0:T(8,128)(2,1)S(1)}, u32[]{:S(2)}, u32[]{:S(2)}) collective-permute-start(bf16[16,4096]{1,0:T(8,128)(2,1)S(1)} %get-tuple-element.42), channel_id=1, source_target_pairs={{0,1},{1,0},{2,3},{3,2},{4,5},{5,4},{6,7},{7,6},{8,9},{9,8},{10,11... | collective-permute-start | bytes 393224 | tf_op jit(solution)/shard_map/ppermute | solution.py:33
  45.6 6.4 %collective-permute-start.16 = (bf16[16,4096]{1,0:T(8,128)(2,1)S(1)}, bf16[16,4096]{1,0:T(8,128)(2,1)S(1)}, u32[]{:S(2)}, u32[]{:S(2)}) collective-permute-start(bf16[16,4096]{1,0:T(8,128)(2,1)S(1)} %get-tuple-element.43), channel_id=1, source_target_pairs={{0,2},{1,3},{2,0},{3,1},{4,6},{5,7},{6,4},{7,5},{8,10},{9,11},{10,... | collective-permute-start | bytes 393224 | tf_op jit(solution)/shard_map/ppermute | solution.py:33
  47.2 6.7 %collective-permute-start.17 = (bf16[16,4096]{1,0:T(8,128)(2,1)S(1)}, bf16[16,4096]{1,0:T(8,128)(2,1)S(1)}, u32[]{:S(2)}, u32[]{:S(2)}) collective-permute-start(bf16[16,4096]{1,0:T(8,128)(2,1)S(1)} %get-tuple-element.44), channel_id=1, source_target_pairs={{0,3},{1,2},{2,1},{3,0},{4,7},{5,6},{6,5},{7,4},{8,11},{9,10},{10,... | collective-permute-start | bytes 393224 | tf_op jit(solution)/shard_map/ppermute | solution.py:33

commit v4 on v3

--- a/solution.py
+++ b/solution.py
@@ -279,7 +279,7 @@
                 column += 2
             else:
                 new_key, new_value = pair_refs[0][...], pair_refs[1][...]
-            new_values.append(new_value)
+            new_values.append(new_value.astype(F32))
             scores = lax.dot_general(
                 qs[n][...].astype(BF16), new_key, contract, preferred_element_type=F32
             )
@@ -307,13 +307,15 @@
                 e, fe = jnp.exp(score - top), jnp.exp(f - top)
                 inverse = 1.0 / (e.sum(axis=1, keepdims=True) + fe.sum(axis=1, keepdims=True))
                 wt[s, :] = (e * inverse).astype(BF16)
-                fw[n][own_rows, :] = (fe * inverse).astype(BF16)
-        for n in range(parts):
-            at[n][...] = dot(fw[n][...], new_values[n])
+                fw[n][own_rows, :] = (fe * inverse).astype(BF16).astype(F32)
         for r in range(requests):
             total = dot(wt[r * rows : (r + 1) * rows, :], v_ref[r])
             for n in range(parts):
-                at[n][2 * r * pads[n] : 2 * (r + 1) * pads[n], :] += total[starts[n] : starts[n + 1]]
+                own_rows = slice(2 * r * pads[n], 2 * (r + 1) * pads[n])
+                value = total[starts[n] : starts[n + 1]]
+                for token in (2 * r, 2 * r + 1):
+                    value = value + fw[n][own_rows, token : token + 1] * new_values[n][token : token + 1]
+                at[n][own_rows, :] = value
         column = 0
         for n, (_, _, count) in enumerate(chunk):
             for h in range(count):
@@ -338,7 +340,7 @@
         ]
         + per_part
         + per_part
-        + [pltpu.VMEM((tokens * pad, tokens), BF16) for pad in pads],
+        + [pltpu.VMEM((tokens * pad, tokens), F32) for pad in pads],
         cost_estimate=cost(1 << 31, 12 << 20),
         compiler_params=pltpu.CompilerParams(vmem_limit_bytes=10 << 20),
         name="attend",
@@ -428,14 +430,14 @@
     rows = [hidden_in] + [swap(hidden_in, "gy", s, ngy) for s in range(1, ngy)]
     near, cosine, sine = fetch(
         joined_projection_weight,
-        cut(ranges[0], 0, max(head_dim, widths[0] * 4 // 5 // 256 * 256)),
+        cut(ranges[0], 0, max(head_dim, widths[0] * 9 // 10 // 256 * 256)),
         positions,
         frequencies_of(head_dim),
     )
     joined = []
     for n in range(len(chunks)):
         last = n == len(chunks) - 1
-        coming = [] if last else cut(ranges[n + 1], 0, max(head_dim, widths[n + 1] * 3 // 4 // 256 * 256))
+        coming = [] if last else cut(ranges[n + 1], 0, max(head_dim, widths[n + 1] // 256 * 256))
         made = project(rows, near, joined_projection_weight, ranges[n], coming, ngx, ngy)
         joined.append((made[0], [swap(made[s], "gx", s, ngx) for s in range(1, ngx)]))
         if not last:

time: 54.8 us -> 53.6 us (0.978)
  Pallas kernels: 23.7 us -> 22.5 us
    pallas_call x2, Pallas kernels: 7.06 us -> 5.95 us  [project(): pl.pallas_call(kernel, out_shape=out_shape, in_specs=[IN_VMEM] * (count +...]
    pallas_call x2, Pallas kernels: 5.08 us -> 4.41 us  [attend(): pl.pallas_call(kernel, out_shape=out_shape, in_specs=[IN_VMEM] * (1 + nre...]
where the time goes in v4:
time: 53.6 us; the launch traced here: 53.5 us
  starting transfers between devices  23.1 us (43%)
  Pallas kernels  22.5 us (42%)
  waiting for transfers between devices  7.55 us (14%)
    ppermute x18, starting transfers between devices, swap(): lax.ppermute(block, axis, [(i, target(i, step, count)) for i in range(cou...  23.1 us
    ppermute x18, waiting for transfers between devices, swap(): lax.ppermute(block, axis, [(i, target(i, step, count)) for i in range(cou...  7.55 us
    pallas_call x1, Pallas kernels, fetch(): pl.pallas_call(kernel, out_shape=[pltpu.VMEM((depth, width), weight.dtype...  6.67 us
    pallas_call x2, Pallas kernels, project(): pl.pallas_call(kernel, out_shape=out_shape, in_specs=[IN_VMEM] * (count +...  5.95 us
    pallas_call x2, Pallas kernels, project_out(): pl.pallas_call(kernel, out_shape=out_shape, in_specs=[IN_VMEM] * (ngx + 1...  4.65 us
    pallas_call x2, Pallas kernels, attend(): pl.pallas_call(kernel, out_shape=out_shape, in_specs=[IN_VMEM] * (1 + nre...  4.41 us
  transfers between devices with their start and end apart: 18, of which 4 were waited for; matrix products, arithmetic and copies ran while one was open for 0% of the time, Pallas kernels for 30%

profile of v4, /device:TPU:0, one launch (start us, length us, event | category | flops | bytes accessed | tf_op | source)
XLA Modules:
  0.0 53.5 jit_solution(1150942833134580737)
XLA Ops:
  0.0 0.0 copy-start
  0.0 2.9 %collective-permute-start.1 = (bf16[8,2,4096]{2,1,0:T(2,128)(2,1)}, bf16[8,2,4096]{2,1,0:T(2,128)(2,1)S(1)}, u32[]{:S(2)}, u32[]{:S(2)}) collective-permute-start(bf16[8,2,4096]{2,1,0:T(2,128)(2,1)} %refs_0_.1), channel_id=1, source_target_pairs={{0,2},{1,3},{2,0},{3,1},{4,6},{5,7},{6,4},{7,5},{8,10},{9,11},{10,... | collective-permute-start | bytes 393224 | tf_op jit(solution)/shard_map/ppermute | solution.py:33
  2.9 0.0 collective-permute-start
  2.9 0.2 collective-permute-start.2
  3.1 6.7 %fetch.1 = (bf16[4096,2304]{1,0:T(8,128)(2,1)S(1)}, f32[16,128]{1,0:T(8,128)S(1)}, f32[16,128]{1,0:T(8,128)S(1)}) custom-call(bf16[4096,3584]{1,0:T(8,128)(2,1)} %refs_2_.1, s32[8]{0:T(128)} %pos_any.1, f32[1,128]{1,0:T(1,128)} %constant.2.clone.freq_any), custom_call_target="tpu_custom_call" | custom-call | bytes 37748736 | tf_op jit(solution)/shard_map/fetch/pallas_call | solution.py:149
  9.8 0.0 collective-permute-done.1.refs_2_
  9.8 0.0 collective-permute-done.refs_1_
  9.8 0.0 collective-permute-done.2.refs_3_
  9.8 0.0 copy-done
  9.9 4.2 %project.2 = (f32[16,2560]{1,0:T(8,128)S(1)}, bf16[16,2560]{1,0:T(8,128)(2,1)S(1)}, bf16[16,2560]{1,0:T(8,128)(2,1)S(1)}, bf16[16,2560]{1,0:T(8,128)(2,1)S(1)}, ...) custom-call(bf16[8,2,4096]{2,1,0:T(2,128)(2,1)S(1)} %copy-done, ...), custom_call_target="tpu_custom_call" | custom-call | flops 1342177280 | bytes 20971520 | tf_op jit(solution)/shard_map/project/pallas_call | solution.py:227
  14.1 2.1 %collective-permute-start.6 = (bf16[16,2560]{1,0:T(8,128)(2,1)S(1)}, bf16[16,2560]{1,0:T(8,128)(2,1)S(1)}, u32[]{:S(2)}, u32[]{:S(2)}) collective-permute-start(bf16[16,2560]{1,0:T(8,128)(2,1)S(1)} %get-tuple-element.33), channel_id=1, source_target_pairs={{0,4},{4,0},{8,12},{12,8},{1,5},{5,1},{9,13},{13,9},{2,6},{6,2},{1... | collective-permute-start | bytes 245768 | tf_op jit(solution)/shard_map/ppermute | solution.py:33
  16.2 2.6 %collective-permute-start.7 = (bf16[16,2560]{1,0:T(8,128)(2,1)S(1)}, bf16[16,2560]{1,0:T(8,128)(2,1)S(1)}, u32[]{:S(2)}, u32[]{:S(2)}) collective-permute-start(bf16[16,2560]{1,0:T(8,128)(2,1)S(1)} %get-tuple-element.34), channel_id=1, source_target_pairs={{0,8},{4,12},{8,0},{12,4},{1,9},{5,13},{9,1},{13,5},{2,10},{6,14},... | collective-permute-start | bytes 245768 | tf_op jit(solution)/shard_map/ppermute | solution.py:33
  18.8 0.0 collective-permute-start.8
  18.8 0.0 copy-start.1
  18.8 0.0 copy-start.2
  18.8 0.0 copy-start.3
  18.8 0.0 slice-start
  18.8 0.0 slice-start.1
  18.8 0.0 slice-start.2
  18.8 0.0 slice-start.3
  18.8 0.0 slice-start.4
  18.8 1.7 %project.3 = (f32[16,1024]{1,0:T(8,128)S(1)}, bf16[16,1024]{1,0:T(8,128)(2,1)S(1)}, bf16[16,1024]{1,0:T(8,128)(2,1)S(1)}, bf16[16,1024]{1,0:T(8,128)(2,1)S(1)}) custom-call(bf16[64,4096]{1,0:T(8,128)(2,1)S(1)} %get-tuple-element.26.refs_0_, bf16[4096,1024]{1,0:T(8,128)(2,1)S(1)} %get-tuple-element.27.refs_1_, bf16[4096,3584]{1,0:T(8,128)(2,1)} %refs_2_.1), custom_call_target="tpu_custom_call" | custom-call | flops 536870912 | bytes 8388608 | tf_op jit(solution)/shard_map/project/pallas_call | solution.py:227
  20.6 0.9 %collective-permute-start.3 = (bf16[16,1024]{1,0:T(8,128)(2,1)S(1)}, bf16[16,1024]{1,0:T(8,128)(2,1)S(1)}, u32[]{:S(2)}, u32[]{:S(2)}) collective-permute-start(bf16[16,1024]{1,0:T(8,128)(2,1)S(1)} %get-tuple-element.29), channel_id=1, source_target_pairs={{0,4},{4,0},{8,12},{12,8},{1,5},{5,1},{9,13},{13,9},{2,6},{6,2},{1... | collective-permute-start | bytes 98312 | tf_op jit(solution)/shard_map/ppermute | solution.py:33
  21.5 3.5 %collective-permute-start.4 = (bf16[16,1024]{1,0:T(8,128)(2,1)S(1)}, bf16[16,1024]{1,0:T(8,128)(2,1)S(1)}, u32[]{:S(2)}, u32[]{:S(2)}) collective-permute-start(bf16[16,1024]{1,0:T(8,128)(2,1)S(1)} %get-tuple-element.30), channel_id=1, source_target_pairs={{0,8},{4,12},{8,0},{12,4},{1,9},{5,13},{9,1},{13,5},{2,10},{6,14},... | collective-permute-start | bytes 98312 | tf_op jit(solution)/shard_map/ppermute | solution.py:33
  25.0 0.0 collective-permute-done.6.refs_1_
  25.0 0.0 collective-permute-start.5
  25.0 0.9 %collective-permute-done.7.refs_2_ = bf16[16,2560]{1,0:T(8,128)(2,1)S(1)} collective-permute-done((bf16[16,2560]{1,0:T(8,128)(2,1)S(1)}, bf16[16,2560]{1,0:T(8,128)(2,1)S(1)}, u32[]{:S(2)}, u32[]{:S(2)}) %collective-permute-start.7) | collective-permute-done | bytes 81952 | tf_op jit(solution)/shard_map/ppermute | solution.py:33
  25.9 0.0 collective-permute-done.8.refs_3_
  25.9 0.0 copy-done.1
  25.9 0.0 copy-done.2
  25.9 0.0 copy-done.3
  25.9 0.0 slice-start.5
  26.0 2.4 %attend.2 = (bf16[16,2048]{1,0:T(8,128)(2,1)S(1)}, bf16[16,128]{1,0:T(8,128)(2,1)S(1)}, bf16[16,128]{1,0:T(8,128)(2,1)S(1)}) custom-call(f32[16,2560]{1,0:T(8,128)S(1)} %get-tuple-element.32.refs_0_, bf16[16,2560]{1,0:T(8,128)(2,1)S(1)} %collective-permute-done.6.refs_1_, bf16[16,2560]{1,0:T(8,128)(2,1)S(1)} %collective-permute-done.7.refs_2_, ...), custom_call_target="tpu_custom_call" | custom-call | flops 2147483648 | bytes 12582912 | tf_op jit(solution)/shard_map/attend/pallas_call | solution.py:332
  28.4 3.0 %collective-permute-start.14 = (bf16[16,2048]{1,0:T(8,128)(2,1)S(1)}, bf16[16,2048]{1,0:T(8,128)(2,1)S(1)}, u32[]{:S(2)}, u32[]{:S(2)}) collective-permute-start(bf16[16,2048]{1,0:T(8,128)(2,1)S(1)} %get-tuple-element.40.refs_0_), channel_id=1, source_target_pairs={{0,12},{4,8},{8,4},{12,0},{1,13},{5,9},{9,5},{13,1},{2,14},{6,10},... | collective-permute-start | bytes 196616 | tf_op jit(solution)/shard_map/ppermute | solution.py:33
  31.4 1.0 %collective-permute-start.13 = (bf16[16,2048]{1,0:T(8,128)(2,1)S(1)}, bf16[16,2048]{1,0:T(8,128)(2,1)S(1)}, u32[]{:S(2)}, u32[]{:S(2)}) collective-permute-start(bf16[16,2048]{1,0:T(8,128)(2,1)S(1)} %get-tuple-element.40.refs_0_), channel_id=1, source_target_pairs={{0,8},{4,12},{8,0},{12,4},{1,9},{5,13},{9,1},{13,5},{2,10},{6,14},... | collective-permute-start | bytes 196616 | tf_op jit(solution)/shard_map/ppermute | solution.py:33
  32.4 0.0 collective-permute-done.3.refs_1_
  32.4 0.4 collective-permute-start.12
  32.9 0.0 collective-permute-done.4.refs_2_
  32.9 0.0 collective-permute-done.5.refs_3_
  32.9 2.0 %attend.3.refs_0_ = bf16[16,1024]{1,0:T(8,128)(2,1)S(1)} custom-call(f32[16,1024]{1,0:T(8,128)S(1)} %get-tuple-element.28.refs_0_, bf16[16,1024]{1,0:T(8,128)(2,1)S(1)} %collective-permute-done.3.refs_1_, bf16[16,1024]{1,0:T(8,128)(2,1)S(1)} %collective-permute-done.4.refs_2_, bf16[16,1024]{1,0:T(8,128)(2,1)S(1)} %collective-permute-done.5.refs_3_, ...), custom_call_target="tpu_custom_call" | custom-call | flops 2147483648 | bytes 12582912 | tf_op jit(solution)/shard_map/attend/pallas_call | solution.py:332
  34.9 3.0 %collective-permute-start.11 = (bf16[16,1024]{1,0:T(8,128)(2,1)S(1)}, bf16[16,1024]{1,0:T(8,128)(2,1)S(1)}, u32[]{:S(2)}, u32[]{:S(2)}) collective-permute-start(bf16[16,1024]{1,0:T(8,128)(2,1)S(1)} %attend.3.refs_0_), channel_id=1, source_target_pairs={{0,12},{4,8},{8,4},{12,0},{1,13},{5,9},{9,5},{13,1},{2,14},{6,10},... | collective-permute-start | bytes 98312 | tf_op jit(solution)/shard_map/ppermute | solution.py:33
  37.8 0.1 collective-permute-start.10
  38.0 0.0 collective-permute-done.14.refs_3_
  38.0 1.3 %collective-permute-start.9 = (bf16[16,1024]{1,0:T(8,128)(2,1)S(1)}, bf16[16,1024]{1,0:T(8,128)(2,1)S(1)}, u32[]{:S(2)}, u32[]{:S(2)}) collective-permute-start(bf16[16,1024]{1,0:T(8,128)(2,1)S(1)} %attend.3.refs_0_), channel_id=1, source_target_pairs={{0,4},{4,0},{8,12},{12,8},{1,5},{5,1},{9,13},{13,9},{2,6},{6,2},{1... | collective-permute-start | bytes 98312 | tf_op jit(solution)/shard_map/ppermute | solution.py:33
  39.3 0.0 collective-permute-done.13.refs_2_
  39.3 0.0 collective-permute-done.12.refs_1_
  39.3 0.0 slice-done
  39.3 0.0 slice-done.1
  39.3 0.0 slice-done.2
  39.3 0.0 slice-done.3
  39.3 0.0 slice-done.4
  39.4 0.0 slice-done.5
  39.4 3.0 %project_out.2.refs_5_ = f32[64,4096]{1,0:T(8,128)S(1)} custom-call(bf16[16,2048]{1,0:T(8,128)(2,1)S(1)} %get-tuple-element.40.refs_0_, bf16[16,2048]{1,0:T(8,128)(2,1)S(1)} %collective-permute-done.12.refs_1_, bf16[16,2048]{1,0:T(8,128)(2,1)S(1)} %collective-permute-done.13.refs_2_, bf16[16,2048]{1,0:T(8,128)(2,1)S(1)} %collective-permute-done.14.refs_3_, ...), custom_call_target="tpu_custom_call" | custom-call | flops 1073741824 | bytes 16777216 | tf_op jit(solution)/shard_map/project_out/pallas_call | solution.py:379
  42.4 0.0 collective-permute-done.11.refs_3_
  42.4 0.2 collective-permute-done.10.refs_2_
  42.7 0.0 collective-permute-done.9.refs_1_
  42.7 1.6 %project_out.3 = (f32[16,4096]{1,0:T(8,128)S(1)}, bf16[16,4096]{1,0:T(8,128)(2,1)S(1)}, bf16[16,4096]{1,0:T(8,128)(2,1)S(1)}, bf16[16,4096]{1,0:T(8,128)(2,1)S(1)}) custom-call(bf16[16,1024]{1,0:T(8,128)(2,1)S(1)} %attend.3.refs_0_, bf16[16,1024]{1,0:T(8,128)(2,1)S(1)} %collective-permute-done.9.refs_1_, ...), custom_call_target="tpu_custom_call" | custom-call | flops 536870912 | bytes 8388608 | tf_op jit(solution)/shard_map/project_out/pallas_call | solution.py:379
  44.3 0.1 collective-permute-start.15
  44.4 1.6 %collective-permute-start.16 = (bf16[16,4096]{1,0:T(8,128)(2,1)S(1)}, bf16[16,4096]{1,0:T(8,128)(2,1)S(1)}, u32[]{:S(2)}, u32[]{:S(2)}) collective-permute-start(bf16[16,4096]{1,0:T(8,128)(2,1)S(1)} %get-tuple-element.43), channel_id=1, source_target_pairs={{0,2},{1,3},{2,0},{3,1},{4,6},{5,7},{6,4},{7,5},{8,10},{9,11},{10,... | collective-permute-start | bytes 393224 | tf_op jit(solution)/shard_map/ppermute | solution.py:33
  45.9 0.3 collective-permute-start.17
  46.2 0.0 collective-permute-done.15.refs_1_
  46.2 4.5 %collective-permute-done.16.refs_2_ = bf16[16,4096]{1,0:T(8,128)(2,1)S(1)} collective-permute-done((bf16[16,4096]{1,0:T(8,128)(2,1)S(1)}, bf16[16,4096]{1,0:T(8,128)(2,1)S(1)}, u32[]{:S(2)}, u32[]{:S(2)}) %collective-permute-start.16) | collective-permute-done | bytes 131104 | tf_op jit(solution)/shard_map/ppermute | solution.py:33
  50.7 1.9 %collective-permute-done.17.refs_3_ = bf16[16,4096]{1,0:T(8,128)(2,1)S(1)} collective-permute-done((bf16[16,4096]{1,0:T(8,128)(2,1)S(1)}, bf16[16,4096]{1,0:T(8,128)(2,1)S(1)}, u32[]{:S(2)}, u32[]{:S(2)}) %collective-permute-start.17) | collective-permute-done | bytes 131104 | tf_op jit(solution)/shard_map/ppermute | solution.py:33
  52.6 0.8 %finish.1 = bf16[8,2,4096]{2,1,0:T(2,128)(2,1)} custom-call(f32[16,4096]{1,0:T(8,128)S(1)} %get-tuple-element.41.refs_0_, bf16[16,4096]{1,0:T(8,128)(2,1)S(1)} %collective-permute-done.15.refs_1_, bf16[16,4096]{1,0:T(8,128)(2,1)S(1)} %collective-permute-done.16.refs_2_, bf16[16,4096]{1,0:T(8,128)(2,1)S(1)} %collective-permute-done.17.refs_3_), custom_call_target="tpu_custom_call" | custom-call | tf_op jit(solution)/shard_map/finish/pallas_call | solution.py:401
  (1 shorter events, 0.0 us)
Async XLA Ops:
  0.0 9.8 %copy-start = (bf16[8,2,4096]{2,1,0:T(2,128)(2,1)S(1)}, bf16[8,2,4096]{2,1,0:T(2,128)(2,1)}, u32[]{:S(2)}) copy-start(bf16[8,2,4096]{2,1,0:T(2,128)(2,1)} %refs_0_.1) | copy-start | bytes 393220
  0.0 9.8 %collective-permute-start.1 = (bf16[8,2,4096]{2,1,0:T(2,128)(2,1)}, bf16[8,2,4096]{2,1,0:T(2,128)(2,1)S(1)}, u32[]{:S(2)}, u32[]{:S(2)}) collective-permute-start(bf16[8,2,4096]{2,1,0:T(2,128)(2,1)} %refs_0_.1), channel_id=1, source_target_pairs={{0,2},{1,3},{2,0},{3,1},{4,6},{5,7},{6,4},{7,5},{8,10},{9,11},{10,... | collective-permute-start | bytes 393224 | tf_op jit(solution)/shard_map/ppermute | solution.py:33
  2.9 6.9 %collective-permute-start = (bf16[8,2,4096]{2,1,0:T(2,128)(2,1)}, bf16[8,2,4096]{2,1,0:T(2,128)(2,1)S(1)}, u32[]{:S(2)}, u32[]{:S(2)}) collective-permute-start(bf16[8,2,4096]{2,1,0:T(2,128)(2,1)} %refs_0_.1), channel_id=1, source_target_pairs={{0,1},{1,0},{2,3},{3,2},{4,5},{5,4},{6,7},{7,6},{8,9},{9,8},{10,11... | collective-permute-start | bytes 393224 | tf_op jit(solution)/shard_map/ppermute | solution.py:33
  2.9 6.9 %collective-permute-start.2 = (bf16[8,2,4096]{2,1,0:T(2,128)(2,1)}, bf16[8,2,4096]{2,1,0:T(2,128)(2,1)S(1)}, u32[]{:S(2)}, u32[]{:S(2)}) collective-permute-start(bf16[8,2,4096]{2,1,0:T(2,128)(2,1)} %refs_0_.1), channel_id=1, source_target_pairs={{0,3},{1,2},{2,1},{3,0},{4,7},{5,6},{6,5},{7,4},{8,11},{9,10},{10,... | collective-permute-start | bytes 393224 | tf_op jit(solution)/shard_map/ppermute | solution.py:33
  14.1 10.9 %collective-permute-start.6 = (bf16[16,2560]{1,0:T(8,128)(2,1)S(1)}, bf16[16,2560]{1,0:T(8,128)(2,1)S(1)}, u32[]{:S(2)}, u32[]{:S(2)}) collective-permute-start(bf16[16,2560]{1,0:T(8,128)(2,1)S(1)} %get-tuple-element.33), channel_id=1, source_target_pairs={{0,4},{4,0},{8,12},{12,8},{1,5},{5,1},{9,13},{13,9},{2,6},{6,2},{1... | collective-permute-start | bytes 245768 | tf_op jit(solution)/shard_map/ppermute | solution.py:33
  16.2 9.7 %collective-permute-start.7 = (bf16[16,2560]{1,0:T(8,128)(2,1)S(1)}, bf16[16,2560]{1,0:T(8,128)(2,1)S(1)}, u32[]{:S(2)}, u32[]{:S(2)}) collective-permute-start(bf16[16,2560]{1,0:T(8,128)(2,1)S(1)} %get-tuple-element.34), channel_id=1, source_target_pairs={{0,8},{4,12},{8,0},{12,4},{1,9},{5,13},{9,1},{13,5},{2,10},{6,14},... | collective-permute-start | bytes 245768 | tf_op jit(solution)/shard_map/ppermute | solution.py:33
  18.8 7.2 %collective-permute-start.8 = (bf16[16,2560]{1,0:T(8,128)(2,1)S(1)}, bf16[16,2560]{1,0:T(8,128)(2,1)S(1)}, u32[]{:S(2)}, u32[]{:S(2)}) collective-permute-start(bf16[16,2560]{1,0:T(8,128)(2,1)S(1)} %get-tuple-element.35), channel_id=1, source_target_pairs={{0,12},{4,8},{8,4},{12,0},{1,13},{5,9},{9,5},{13,1},{2,14},{6,10},... | collective-permute-start | bytes 245768 | tf_op jit(solution)/shard_map/ppermute | solution.py:33
  18.8 7.2 %copy-start.1 = (bf16[8,768,2,128]{3,2,1,0:T(2,128)(2,1)S(1)}, bf16[8,768,2,128]{3,2,1,0:T(2,128)(2,1)}, u32[]{:S(2)}) copy-start(bf16[8,768,2,128]{3,2,1,0:T(2,128)(2,1)} %param.11) | copy-start | bytes 9437188
  18.8 7.2 %copy-start.2 = (bf16[8,768,2,128]{3,2,1,0:T(2,128)(2,1)S(1)}, bf16[8,768,2,128]{3,2,1,0:T(2,128)(2,1)}, u32[]{:S(2)}) copy-start(bf16[8,768,2,128]{3,2,1,0:T(2,128)(2,1)} %param.12) | copy-start | bytes 9437188
  18.8 7.2 %copy-start.3 = (s32[8]{0:T(128)S(1)}, s32[8]{0:T(128)}, u32[]{:S(2)}) copy-start(s32[8]{0:T(128)} %refs_8_.1) | copy-start | bytes 100
  18.8 20.5 %slice-start = ((s8[25165824]{0:T(1024)(128)(4,1)}), s8[4194304]{0:T(1024)(128)(4,1)S(1)}, s32[]{:S(2)}) async-start(s8[25165824]{0:T(1024)(128)(4,1)} %bitcast.2), calls=%async_computation | async-start | bytes 8388608
  18.8 20.5 %slice-start.1 = ((s8[25165824]{0:T(1024)(128)(4,1)}), s8[4194304]{0:T(1024)(128)(4,1)S(1)}, s32[]{:S(2)}) async-start(s8[25165824]{0:T(1024)(128)(4,1)} %bitcast.2), calls=%async_computation.1 | async-start | bytes 8388608
  18.8 20.5 %slice-start.2 = ((s8[25165824]{0:T(1024)(128)(4,1)}), s8[4194304]{0:T(1024)(128)(4,1)S(1)}, s32[]{:S(2)}) async-start(s8[25165824]{0:T(1024)(128)(4,1)} %bitcast.2), calls=%async_computation.2 | async-start | bytes 8388608
  18.8 20.5 %slice-start.3 = ((s8[25165824]{0:T(1024)(128)(4,1)}), s8[4194304]{0:T(1024)(128)(4,1)S(1)}, s32[]{:S(2)}) async-start(s8[25165824]{0:T(1024)(128)(4,1)} %bitcast.2), calls=%async_computation.3 | async-start | bytes 8388608
  18.8 20.5 %slice-start.4 = ((s8[25165824]{0:T(1024)(128)(4,1)}), s8[4194304]{0:T(1024)(128)(4,1)S(1)}, s32[]{:S(2)}) async-start(s8[25165824]{0:T(1024)(128)(4,1)} %bitcast.2), calls=%async_computation.4 | async-start | bytes 8388608
  20.6 11.9 %collective-permute-start.3 = (bf16[16,1024]{1,0:T(8,128)(2,1)S(1)}, bf16[16,1024]{1,0:T(8,128)(2,1)S(1)}, u32[]{:S(2)}, u32[]{:S(2)}) collective-permute-start(bf16[16,1024]{1,0:T(8,128)(2,1)S(1)} %get-tuple-element.29), channel_id=1, source_target_pairs={{0,4},{4,0},{8,12},{12,8},{1,5},{5,1},{9,13},{13,9},{2,6},{6,2},{1... | collective-permute-start | bytes 98312 | tf_op jit(solution)/shard_map/ppermute | solution.py:33
  21.5 11.3 %collective-permute-start.4 = (bf16[16,1024]{1,0:T(8,128)(2,1)S(1)}, bf16[16,1024]{1,0:T(8,128)(2,1)S(1)}, u32[]{:S(2)}, u32[]{:S(2)}) collective-permute-start(bf16[16,1024]{1,0:T(8,128)(2,1)S(1)} %get-tuple-element.30), channel_id=1, source_target_pairs={{0,8},{4,12},{8,0},{12,4},{1,9},{5,13},{9,1},{13,5},{2,10},{6,14},... | collective-permute-start | bytes 98312 | tf_op jit(solution)/shard_map/ppermute | solution.py:33
  25.0 7.8 %collective-permute-start.5 = (bf16[16,1024]{1,0:T(8,128)(2,1)S(1)}, bf16[16,1024]{1,0:T(8,128)(2,1)S(1)}, u32[]{:S(2)}, u32[]{:S(2)}) collective-permute-start(bf16[16,1024]{1,0:T(8,128)(2,1)S(1)} %get-tuple-element.31), channel_id=1, source_target_pairs={{0,12},{4,8},{8,4},{12,0},{1,13},{5,9},{9,5},{13,1},{2,14},{6,10},... | collective-permute-start | bytes 98312 | tf_op jit(solution)/shard_map/ppermute | solution.py:33
  25.9 13.4 %slice-start.5 = ((s8[25165824]{0:T(1024)(128)(4,1)}), s8[4194304]{0:T(1024)(128)(4,1)S(1)}, s32[]{:S(2)}) async-start(s8[25165824]{0:T(1024)(128)(4,1)} %bitcast.2), calls=%async_computation.5 | async-start | bytes 8388608
  28.4 9.6 %collective-permute-start.14 = (bf16[16,2048]{1,0:T(8,128)(2,1)S(1)}, bf16[16,2048]{1,0:T(8,128)(2,1)S(1)}, u32[]{:S(2)}, u32[]{:S(2)}) collective-permute-start(bf16[16,2048]{1,0:T(8,128)(2,1)S(1)} %get-tuple-element.40.refs_0_), channel_id=1, source_target_pairs={{0,12},{4,8},{8,4},{12,0},{1,13},{5,9},{9,5},{13,1},{2,14},{6,10},... | collective-permute-start | bytes 196616 | tf_op jit(solution)/shard_map/ppermute | solution.py:33
  31.4 7.9 %collective-permute-start.13 = (bf16[16,2048]{1,0:T(8,128)(2,1)S(1)}, bf16[16,2048]{1,0:T(8,128)(2,1)S(1)}, u32[]{:S(2)}, u32[]{:S(2)}) collective-permute-start(bf16[16,2048]{1,0:T(8,128)(2,1)S(1)} %get-tuple-element.40.refs_0_), channel_id=1, source_target_pairs={{0,8},{4,12},{8,0},{12,4},{1,9},{5,13},{9,1},{13,5},{2,10},{6,14},... | collective-permute-start | bytes 196616 | tf_op jit(solution)/shard_map/ppermute | solution.py:33
  32.4 6.9 %collective-permute-start.12 = (bf16[16,2048]{1,0:T(8,128)(2,1)S(1)}, bf16[16,2048]{1,0:T(8,128)(2,1)S(1)}, u32[]{:S(2)}, u32[]{:S(2)}) collective-permute-start(bf16[16,2048]{1,0:T(8,128)(2,1)S(1)} %get-tuple-element.40.refs_0_), channel_id=1, source_target_pairs={{0,4},{4,0},{8,12},{12,8},{1,5},{5,1},{9,13},{13,9},{2,6},{6,2},{1... | collective-permute-start | bytes 196616 | tf_op jit(solution)/shard_map/ppermute | solution.py:33
  34.9 7.6 %collective-permute-start.11 = (bf16[16,1024]{1,0:T(8,128)(2,1)S(1)}, bf16[16,1024]{1,0:T(8,128)(2,1)S(1)}, u32[]{:S(2)}, u32[]{:S(2)}) collective-permute-start(bf16[16,1024]{1,0:T(8,128)(2,1)S(1)} %attend.3.refs_0_), channel_id=1, source_target_pairs={{0,12},{4,8},{8,4},{12,0},{1,13},{5,9},{9,5},{13,1},{2,14},{6,10},... | collective-permute-start | bytes 98312 | tf_op jit(solution)/shard_map/ppermute | solution.py:33
  37.8 4.8 %collective-permute-start.10 = (bf16[16,1024]{1,0:T(8,128)(2,1)S(1)}, bf16[16,1024]{1,0:T(8,128)(2,1)S(1)}, u32[]{:S(2)}, u32[]{:S(2)}) collective-permute-start(bf16[16,1024]{1,0:T(8,128)(2,1)S(1)} %attend.3.refs_0_), channel_id=1, source_target_pairs={{0,8},{4,12},{8,0},{12,4},{1,9},{5,13},{9,1},{13,5},{2,10},{6,14},... | collective-permute-start | bytes 98312 | tf_op jit(solution)/shard_map/ppermute | solution.py:33
  38.0 4.7 %collective-permute-start.9 = (bf16[16,1024]{1,0:T(8,128)(2,1)S(1)}, bf16[16,1024]{1,0:T(8,128)(2,1)S(1)}, u32[]{:S(2)}, u32[]{:S(2)}) collective-permute-start(bf16[16,1024]{1,0:T(8,128)(2,1)S(1)} %attend.3.refs_0_), channel_id=1, source_target_pairs={{0,4},{4,0},{8,12},{12,8},{1,5},{5,1},{9,13},{13,9},{2,6},{6,2},{1... | collective-permute-start | bytes 98312 | tf_op jit(solution)/shard_map/ppermute | solution.py:33
  44.3 1.9 %collective-permute-start.15 = (bf16[16,4096]{1,0:T(8,128)(2,1)S(1)}, bf16[16,4096]{1,0:T(8,128)(2,1)S(1)}, u32[]{:S(2)}, u32[]{:S(2)}) collective-permute-start(bf16[16,4096]{1,0:T(8,128)(2,1)S(1)} %get-tuple-element.42), channel_id=1, source_target_pairs={{0,1},{1,0},{2,3},{3,2},{4,5},{5,4},{6,7},{7,6},{8,9},{9,8},{10,11... | collective-permute-start | bytes 393224 | tf_op jit(solution)/shard_map/ppermute | solution.py:33
  44.4 6.4 %collective-permute-start.16 = (bf16[16,4096]{1,0:T(8,128)(2,1)S(1)}, bf16[16,4096]{1,0:T(8,128)(2,1)S(1)}, u32[]{:S(2)}, u32[]{:S(2)}) collective-permute-start(bf16[16,4096]{1,0:T(8,128)(2,1)S(1)} %get-tuple-element.43), channel_id=1, source_target_pairs={{0,2},{1,3},{2,0},{3,1},{4,6},{5,7},{6,4},{7,5},{8,10},{9,11},{10,... | collective-permute-start | bytes 393224 | tf_op jit(solution)/shard_map/ppermute | solution.py:33
  45.9 6.7 %collective-permute-start.17 = (bf16[16,4096]{1,0:T(8,128)(2,1)S(1)}, bf16[16,4096]{1,0:T(8,128)(2,1)S(1)}, u32[]{:S(2)}, u32[]{:S(2)}) collective-permute-start(bf16[16,4096]{1,0:T(8,128)(2,1)S(1)} %get-tuple-element.44), channel_id=1, source_target_pairs={{0,3},{1,2},{2,1},{3,0},{4,7},{5,6},{6,5},{7,4},{8,11},{9,10},{10,... | collective-permute-start | bytes 393224 | tf_op jit(solution)/shard_map/ppermute | solution.py:33

commit v5 on v4

--- a/solution.py
+++ b/solution.py
@@ -31,6 +31,10 @@
 
 def swap(block, axis, step, count):
     return lax.ppermute(block, axis, [(i, target(i, step, count)) for i in range(count)])
+
+
+def order_of(count):
+    return [*range(count // 2, count), *range(1, count // 2)] if count > 2 else [*range(1, count)]
 
 
 def hbm(array):
@@ -439,7 +443,7 @@
         last = n == len(chunks) - 1
         coming = [] if last else cut(ranges[n + 1], 0, max(head_dim, widths[n + 1] // 256 * 256))
         made = project(rows, near, joined_projection_weight, ranges[n], coming, ngx, ngy)
-        joined.append((made[0], [swap(made[s], "gx", s, ngx) for s in range(1, ngx)]))
+        joined.append((made[0], [swap(made[s], "gx", s, ngx) for s in order_of(ngx)]))
         if not last:
             near = made[ngx]
         if len(rows) > 1:
@@ -458,7 +462,7 @@
         made = project_out(attended[n], total, w_out, first, n == len(chunks) - 1, ngx, ngy)
         first += attended[n][0].shape[1]
         total = made[0]
-    return finish(made[0], [swap(made[s], "gy", s, ngy) for s in range(1, ngy)])
+    return finish(made[0], [swap(made[s], "gy", s, ngy) for s in order_of(ngy)])
 
 
 def solution(mesh):

time: 53.6 us -> 52.1 us (0.972)
  waiting for transfers between devices: 7.55 us -> 5.76 us
    ppermute x18, waiting for transfers between devices: 7.55 us -> 5.76 us  [swap(): lax.ppermute(block, axis, [(i, target(i, step, count)) for i in range(cou...]
  transfers between devices with their start and end apart: 18 -> 18, of which waited for: 4 -> 3; matrix products, arithmetic and copies ran while one was open for 0% -> 0% of each run, Pallas kernels for 30% -> 30%
where the time goes in v5:
time: 52.1 us; the launch traced here: 52 us
  starting transfers between devices  23.4 us (45%)
  Pallas kernels  22.5 us (43%)
  waiting for transfers between devices  5.76 us (11%)
    ppermute x18, starting transfers between devices, swap(): lax.ppermute(block, axis, [(i, target(i, step, count)) for i in range(cou...  23.4 us
    pallas_call x1, Pallas kernels, fetch(): pl.pallas_call(kernel, out_shape=[pltpu.VMEM((depth, width), weight.dtype...  6.67 us
    pallas_call x2, Pallas kernels, project(): pl.pallas_call(kernel, out_shape=out_shape, in_specs=[IN_VMEM] * (count +...  5.95 us
    ppermute x18, waiting for transfers between devices, swap(): lax.ppermute(block, axis, [(i, target(i, step, count)) for i in range(cou...  5.76 us
    pallas_call x2, Pallas kernels, project_out(): pl.pallas_call(kernel, out_shape=out_shape, in_specs=[IN_VMEM] * (ngx + 1...  4.65 us
    pallas_call x2, Pallas kernels, attend(): pl.pallas_call(kernel, out_shape=out_shape, in_specs=[IN_VMEM] * (1 + nre...  4.41 us
  transfers between devices with their start and end apart: 18, of which 3 were waited for; matrix products, arithmetic and copies ran while one was open for 0% of the time, Pallas kernels for 30%

profile of v5, /device:TPU:0, one launch (start us, length us, event | category | flops | bytes accessed | tf_op | source)
XLA Modules:
  0.0 52.0 jit_solution(8592802708891278054)
XLA Ops:
  0.0 0.0 copy-start
  0.0 2.9 %collective-permute-start.1 = (bf16[8,2,4096]{2,1,0:T(2,128)(2,1)}, bf16[8,2,4096]{2,1,0:T(2,128)(2,1)S(1)}, u32[]{:S(2)}, u32[]{:S(2)}) collective-permute-start(bf16[8,2,4096]{2,1,0:T(2,128)(2,1)} %refs_0_.1), channel_id=1, source_target_pairs={{0,2},{1,3},{2,0},{3,1},{4,6},{5,7},{6,4},{7,5},{8,10},{9,11},{10,... | collective-permute-start | bytes 393224 | tf_op jit(solution)/shard_map/ppermute | solution.py:33
  2.9 0.0 collective-permute-start
  2.9 0.2 collective-permute-start.2
  3.1 6.7 %fetch.1 = (bf16[4096,2304]{1,0:T(8,128)(2,1)S(1)}, f32[16,128]{1,0:T(8,128)S(1)}, f32[16,128]{1,0:T(8,128)S(1)}) custom-call(bf16[4096,3584]{1,0:T(8,128)(2,1)} %refs_2_.1, s32[8]{0:T(128)} %pos_any.1, f32[1,128]{1,0:T(1,128)} %constant.2.clone.freq_any), custom_call_target="tpu_custom_call" | custom-call | bytes 37748736 | tf_op jit(solution)/shard_map/fetch/pallas_call | solution.py:153
  9.8 0.0 collective-permute-done.1.refs_2_
  9.8 0.0 collective-permute-done.refs_1_
  9.8 0.0 collective-permute-done.2.refs_3_
  9.8 0.0 copy-done
  9.9 4.2 %project.2 = (f32[16,2560]{1,0:T(8,128)S(1)}, bf16[16,2560]{1,0:T(8,128)(2,1)S(1)}, bf16[16,2560]{1,0:T(8,128)(2,1)S(1)}, bf16[16,2560]{1,0:T(8,128)(2,1)S(1)}, ...) custom-call(bf16[8,2,4096]{2,1,0:T(2,128)(2,1)S(1)} %copy-done, ...), custom_call_target="tpu_custom_call" | custom-call | flops 1342177280 | bytes 20971520 | tf_op jit(solution)/shard_map/project/pallas_call | solution.py:231
  14.1 3.1 %collective-permute-start.6 = (bf16[16,2560]{1,0:T(8,128)(2,1)S(1)}, bf16[16,2560]{1,0:T(8,128)(2,1)S(1)}, u32[]{:S(2)}, u32[]{:S(2)}) collective-permute-start(bf16[16,2560]{1,0:T(8,128)(2,1)S(1)} %get-tuple-element.33), channel_id=1, source_target_pairs={{0,8},{4,12},{8,0},{12,4},{1,9},{5,13},{9,1},{13,5},{2,10},{6,14},... | collective-permute-start | bytes 245768 | tf_op jit(solution)/shard_map/ppermute | solution.py:33
  17.2 1.3 %collective-permute-start.7 = (bf16[16,2560]{1,0:T(8,128)(2,1)S(1)}, bf16[16,2560]{1,0:T(8,128)(2,1)S(1)}, u32[]{:S(2)}, u32[]{:S(2)}) collective-permute-start(bf16[16,2560]{1,0:T(8,128)(2,1)S(1)} %get-tuple-element.34), channel_id=1, source_target_pairs={{0,12},{4,8},{8,4},{12,0},{1,13},{5,9},{9,5},{13,1},{2,14},{6,10},... | collective-permute-start | bytes 245768 | tf_op jit(solution)/shard_map/ppermute | solution.py:33
  18.5 0.2 collective-permute-start.8
  18.8 0.0 copy-start.1
  18.8 0.0 copy-start.2
  18.8 0.0 copy-start.3
  18.8 0.0 slice-start
  18.8 0.0 slice-start.1
  18.8 0.0 slice-start.2
  18.8 0.0 slice-start.3
  18.8 0.0 slice-start.4
  18.8 1.7 %project.3 = (f32[16,1024]{1,0:T(8,128)S(1)}, bf16[16,1024]{1,0:T(8,128)(2,1)S(1)}, bf16[16,1024]{1,0:T(8,128)(2,1)S(1)}, bf16[16,1024]{1,0:T(8,128)(2,1)S(1)}) custom-call(bf16[64,4096]{1,0:T(8,128)(2,1)S(1)} %get-tuple-element.26.refs_0_, bf16[4096,1024]{1,0:T(8,128)(2,1)S(1)} %get-tuple-element.27.refs_1_, bf16[4096,3584]{1,0:T(8,128)(2,1)} %refs_2_.1), custom_call_target="tpu_custom_call" | custom-call | flops 536870912 | bytes 8388608 | tf_op jit(solution)/shard_map/project/pallas_call | solution.py:231
  20.6 2.9 %collective-permute-start.3 = (bf16[16,1024]{1,0:T(8,128)(2,1)S(1)}, bf16[16,1024]{1,0:T(8,128)(2,1)S(1)}, u32[]{:S(2)}, u32[]{:S(2)}) collective-permute-start(bf16[16,1024]{1,0:T(8,128)(2,1)S(1)} %get-tuple-element.29), channel_id=1, source_target_pairs={{0,8},{4,12},{8,0},{12,4},{1,9},{5,13},{9,1},{13,5},{2,10},{6,14},... | collective-permute-start | bytes 98312 | tf_op jit(solution)/shard_map/ppermute | solution.py:33
  23.4 1.3 %collective-permute-start.4 = (bf16[16,1024]{1,0:T(8,128)(2,1)S(1)}, bf16[16,1024]{1,0:T(8,128)(2,1)S(1)}, u32[]{:S(2)}, u32[]{:S(2)}) collective-permute-start(bf16[16,1024]{1,0:T(8,128)(2,1)S(1)} %get-tuple-element.30), channel_id=1, source_target_pairs={{0,12},{4,8},{8,4},{12,0},{1,13},{5,9},{9,5},{13,1},{2,14},{6,10},... | collective-permute-start | bytes 98312 | tf_op jit(solution)/shard_map/ppermute | solution.py:33
  24.8 0.0 collective-permute-done.6.refs_1_
  24.8 0.0 collective-permute-start.5
  24.8 0.0 collective-permute-done.7.refs_2_
  24.8 0.0 collective-permute-done.8.refs_3_
  24.8 0.0 copy-done.1
  24.8 0.0 copy-done.2
  24.8 0.0 copy-done.3
  24.8 0.0 slice-start.5
  24.9 2.4 %attend.2 = (bf16[16,2048]{1,0:T(8,128)(2,1)S(1)}, bf16[16,128]{1,0:T(8,128)(2,1)S(1)}, bf16[16,128]{1,0:T(8,128)(2,1)S(1)}) custom-call(f32[16,2560]{1,0:T(8,128)S(1)} %get-tuple-element.32.refs_0_, bf16[16,2560]{1,0:T(8,128)(2,1)S(1)} %collective-permute-done.6.refs_1_, bf16[16,2560]{1,0:T(8,128)(2,1)S(1)} %collective-permute-done.7.refs_2_, ...), custom_call_target="tpu_custom_call" | custom-call | flops 2147483648 | bytes 12582912 | tf_op jit(solution)/shard_map/attend/pallas_call | solution.py:336
  27.3 3.3 %collective-permute-start.14 = (bf16[16,2048]{1,0:T(8,128)(2,1)S(1)}, bf16[16,2048]{1,0:T(8,128)(2,1)S(1)}, u32[]{:S(2)}, u32[]{:S(2)}) collective-permute-start(bf16[16,2048]{1,0:T(8,128)(2,1)S(1)} %get-tuple-element.40.refs_0_), channel_id=1, source_target_pairs={{0,12},{4,8},{8,4},{12,0},{1,13},{5,9},{9,5},{13,1},{2,14},{6,10},... | collective-permute-start | bytes 196616 | tf_op jit(solution)/shard_map/ppermute | solution.py:33
  30.6 1.0 %collective-permute-start.13 = (bf16[16,2048]{1,0:T(8,128)(2,1)S(1)}, bf16[16,2048]{1,0:T(8,128)(2,1)S(1)}, u32[]{:S(2)}, u32[]{:S(2)}) collective-permute-start(bf16[16,2048]{1,0:T(8,128)(2,1)S(1)} %get-tuple-element.40.refs_0_), channel_id=1, source_target_pairs={{0,8},{4,12},{8,0},{12,4},{1,9},{5,13},{9,1},{13,5},{2,10},{6,14},... | collective-permute-start | bytes 196616 | tf_op jit(solution)/shard_map/ppermute | solution.py:33
  31.5 0.0 collective-permute-done.3.refs_1_
  31.5 0.5 collective-permute-start.12
  32.0 0.0 collective-permute-done.4.refs_2_
  32.0 0.0 collective-permute-done.5.refs_3_
  32.0 2.0 %attend.3.refs_0_ = bf16[16,1024]{1,0:T(8,128)(2,1)S(1)} custom-call(f32[16,1024]{1,0:T(8,128)S(1)} %get-tuple-element.28.refs_0_, bf16[16,1024]{1,0:T(8,128)(2,1)S(1)} %collective-permute-done.3.refs_1_, bf16[16,1024]{1,0:T(8,128)(2,1)S(1)} %collective-permute-done.4.refs_2_, bf16[16,1024]{1,0:T(8,128)(2,1)S(1)} %collective-permute-done.5.refs_3_, ...), custom_call_target="tpu_custom_call" | custom-call | flops 2147483648 | bytes 12582912 | tf_op jit(solution)/shard_map/attend/pallas_call | solution.py:336
  34.0 3.0 %collective-permute-start.11 = (bf16[16,1024]{1,0:T(8,128)(2,1)S(1)}, bf16[16,1024]{1,0:T(8,128)(2,1)S(1)}, u32[]{:S(2)}, u32[]{:S(2)}) collective-permute-start(bf16[16,1024]{1,0:T(8,128)(2,1)S(1)} %attend.3.refs_0_), channel_id=1, source_target_pairs={{0,12},{4,8},{8,4},{12,0},{1,13},{5,9},{9,5},{13,1},{2,14},{6,10},... | collective-permute-start | bytes 98312 | tf_op jit(solution)/shard_map/ppermute | solution.py:33
  37.0 0.1 collective-permute-start.10
  37.1 0.0 collective-permute-done.14.refs_3_
  37.1 1.4 %collective-permute-start.9 = (bf16[16,1024]{1,0:T(8,128)(2,1)S(1)}, bf16[16,1024]{1,0:T(8,128)(2,1)S(1)}, u32[]{:S(2)}, u32[]{:S(2)}) collective-permute-start(bf16[16,1024]{1,0:T(8,128)(2,1)S(1)} %attend.3.refs_0_), channel_id=1, source_target_pairs={{0,4},{4,0},{8,12},{12,8},{1,5},{5,1},{9,13},{13,9},{2,6},{6,2},{1... | collective-permute-start | bytes 98312 | tf_op jit(solution)/shard_map/ppermute | solution.py:33
  38.5 0.0 collective-permute-done.13.refs_2_
  38.5 0.0 collective-permute-done.12.refs_1_
  38.5 0.0 slice-done
  38.5 0.0 slice-done.1
  38.5 0.0 slice-done.2
  38.5 0.0 slice-done.3
  38.5 0.0 slice-done.4
  38.5 0.0 slice-done.5
  38.5 3.0 %project_out.2.refs_5_ = f32[64,4096]{1,0:T(8,128)S(1)} custom-call(bf16[16,2048]{1,0:T(8,128)(2,1)S(1)} %get-tuple-element.40.refs_0_, bf16[16,2048]{1,0:T(8,128)(2,1)S(1)} %collective-permute-done.12.refs_1_, bf16[16,2048]{1,0:T(8,128)(2,1)S(1)} %collective-permute-done.13.refs_2_, bf16[16,2048]{1,0:T(8,128)(2,1)S(1)} %collective-permute-done.14.refs_3_, ...), custom_call_target="tpu_custom_call" | custom-call | flops 1073741824 | bytes 16777216 | tf_op jit(solution)/shard_map/project_out/pallas_call | solution.py:383
  41.6 0.0 collective-permute-done.11.refs_3_
  41.6 0.6 %collective-permute-done.10.refs_2_ = bf16[16,1024]{1,0:T(8,128)(2,1)S(1)} collective-permute-done((bf16[16,1024]{1,0:T(8,128)(2,1)S(1)}, bf16[16,1024]{1,0:T(8,128)(2,1)S(1)}, u32[]{:S(2)}, u32[]{:S(2)}) %collective-permute-start.10) | collective-permute-done | bytes 32800 | tf_op jit(solution)/shard_map/ppermute | solution.py:33
  42.2 0.0 collective-permute-done.9.refs_1_
  42.2 1.6 %project_out.3 = (f32[16,4096]{1,0:T(8,128)S(1)}, bf16[16,4096]{1,0:T(8,128)(2,1)S(1)}, bf16[16,4096]{1,0:T(8,128)(2,1)S(1)}, bf16[16,4096]{1,0:T(8,128)(2,1)S(1)}) custom-call(bf16[16,1024]{1,0:T(8,128)(2,1)S(1)} %attend.3.refs_0_, bf16[16,1024]{1,0:T(8,128)(2,1)S(1)} %collective-permute-done.9.refs_1_, ...), custom_call_target="tpu_custom_call" | custom-call | flops 536870912 | bytes 8388608 | tf_op jit(solution)/shard_map/project_out/pallas_call | solution.py:383
  43.8 1.6 %collective-permute-start.15 = (bf16[16,4096]{1,0:T(8,128)(2,1)S(1)}, bf16[16,4096]{1,0:T(8,128)(2,1)S(1)}, u32[]{:S(2)}, u32[]{:S(2)}) collective-permute-start(bf16[16,4096]{1,0:T(8,128)(2,1)S(1)} %get-tuple-element.42), channel_id=1, source_target_pairs={{0,2},{1,3},{2,0},{3,1},{4,6},{5,7},{6,4},{7,5},{8,10},{9,11},{10,... | collective-permute-start | bytes 393224 | tf_op jit(solution)/shard_map/ppermute | solution.py:33
  45.3 0.0 collective-permute-start.16
  45.3 0.6 %collective-permute-start.17 = (bf16[16,4096]{1,0:T(8,128)(2,1)S(1)}, bf16[16,4096]{1,0:T(8,128)(2,1)S(1)}, u32[]{:S(2)}, u32[]{:S(2)}) collective-permute-start(bf16[16,4096]{1,0:T(8,128)(2,1)S(1)} %get-tuple-element.44), channel_id=1, source_target_pairs={{0,1},{1,0},{2,3},{3,2},{4,5},{5,4},{6,7},{7,6},{8,9},{9,8},{10,11... | collective-permute-start | bytes 393224 | tf_op jit(solution)/shard_map/ppermute | solution.py:33
  46.0 3.3 %collective-permute-done.15.refs_1_ = bf16[16,4096]{1,0:T(8,128)(2,1)S(1)} collective-permute-done((bf16[16,4096]{1,0:T(8,128)(2,1)S(1)}, bf16[16,4096]{1,0:T(8,128)(2,1)S(1)}, u32[]{:S(2)}, u32[]{:S(2)}) %collective-permute-start.15) | collective-permute-done | bytes 131104 | tf_op jit(solution)/shard_map/ppermute | solution.py:33
  49.3 1.8 %collective-permute-done.16.refs_2_ = bf16[16,4096]{1,0:T(8,128)(2,1)S(1)} collective-permute-done((bf16[16,4096]{1,0:T(8,128)(2,1)S(1)}, bf16[16,4096]{1,0:T(8,128)(2,1)S(1)}, u32[]{:S(2)}, u32[]{:S(2)}) %collective-permute-start.16) | collective-permute-done | bytes 131104 | tf_op jit(solution)/shard_map/ppermute | solution.py:33
  51.1 0.0 collective-permute-done.17.refs_3_
  51.1 0.8 %finish.1 = bf16[8,2,4096]{2,1,0:T(2,128)(2,1)} custom-call(f32[16,4096]{1,0:T(8,128)S(1)} %get-tuple-element.41.refs_0_, bf16[16,4096]{1,0:T(8,128)(2,1)S(1)} %collective-permute-done.15.refs_1_, bf16[16,4096]{1,0:T(8,128)(2,1)S(1)} %collective-permute-done.16.refs_2_, bf16[16,4096]{1,0:T(8,128)(2,1)S(1)} %collective-permute-done.17.refs_3_), custom_call_target="tpu_custom_call" | custom-call | tf_op jit(solution)/shard_map/finish/pallas_call | solution.py:405
  (1 shorter events, 0.0 us)
Async XLA Ops:
  0.0 9.8 %copy-start = (bf16[8,2,4096]{2,1,0:T(2,128)(2,1)S(1)}, bf16[8,2,4096]{2,1,0:T(2,128)(2,1)}, u32[]{:S(2)}) copy-start(bf16[8,2,4096]{2,1,0:T(2,128)(2,1)} %refs_0_.1) | copy-start | bytes 393220
  0.0 9.8 %collective-permute-start.1 = (bf16[8,2,4096]{2,1,0:T(2,128)(2,1)}, bf16[8,2,4096]{2,1,0:T(2,128)(2,1)S(1)}, u32[]{:S(2)}, u32[]{:S(2)}) collective-permute-start(bf16[8,2,4096]{2,1,0:T(2,128)(2,1)} %refs_0_.1), channel_id=1, source_target_pairs={{0,2},{1,3},{2,0},{3,1},{4,6},{5,7},{6,4},{7,5},{8,10},{9,11},{10,... | collective-permute-start | bytes 393224 | tf_op jit(solution)/shard_map/ppermute | solution.py:33
  2.9 6.9 %collective-permute-start = (bf16[8,2,4096]{2,1,0:T(2,128)(2,1)}, bf16[8,2,4096]{2,1,0:T(2,128)(2,1)S(1)}, u32[]{:S(2)}, u32[]{:S(2)}) collective-permute-start(bf16[8,2,4096]{2,1,0:T(2,128)(2,1)} %refs_0_.1), channel_id=1, source_target_pairs={{0,1},{1,0},{2,3},{3,2},{4,5},{5,4},{6,7},{7,6},{8,9},{9,8},{10,11... | collective-permute-start | bytes 393224 | tf_op jit(solution)/shard_map/ppermute | solution.py:33
  2.9 6.9 %collective-permute-start.2 = (bf16[8,2,4096]{2,1,0:T(2,128)(2,1)}, bf16[8,2,4096]{2,1,0:T(2,128)(2,1)S(1)}, u32[]{:S(2)}, u32[]{:S(2)}) collective-permute-start(bf16[8,2,4096]{2,1,0:T(2,128)(2,1)} %refs_0_.1), channel_id=1, source_target_pairs={{0,3},{1,2},{2,1},{3,0},{4,7},{5,6},{6,5},{7,4},{8,11},{9,10},{10,... | collective-permute-start | bytes 393224 | tf_op jit(solution)/shard_map/ppermute | solution.py:33
  14.1 10.7 %collective-permute-start.6 = (bf16[16,2560]{1,0:T(8,128)(2,1)S(1)}, bf16[16,2560]{1,0:T(8,128)(2,1)S(1)}, u32[]{:S(2)}, u32[]{:S(2)}) collective-permute-start(bf16[16,2560]{1,0:T(8,128)(2,1)S(1)} %get-tuple-element.33), channel_id=1, source_target_pairs={{0,8},{4,12},{8,0},{12,4},{1,9},{5,13},{9,1},{13,5},{2,10},{6,14},... | collective-permute-start | bytes 245768 | tf_op jit(solution)/shard_map/ppermute | solution.py:33
  17.2 7.6 %collective-permute-start.7 = (bf16[16,2560]{1,0:T(8,128)(2,1)S(1)}, bf16[16,2560]{1,0:T(8,128)(2,1)S(1)}, u32[]{:S(2)}, u32[]{:S(2)}) collective-permute-start(bf16[16,2560]{1,0:T(8,128)(2,1)S(1)} %get-tuple-element.34), channel_id=1, source_target_pairs={{0,12},{4,8},{8,4},{12,0},{1,13},{5,9},{9,5},{13,1},{2,14},{6,10},... | collective-permute-start | bytes 245768 | tf_op jit(solution)/shard_map/ppermute | solution.py:33
  18.5 6.3 %collective-permute-start.8 = (bf16[16,2560]{1,0:T(8,128)(2,1)S(1)}, bf16[16,2560]{1,0:T(8,128)(2,1)S(1)}, u32[]{:S(2)}, u32[]{:S(2)}) collective-permute-start(bf16[16,2560]{1,0:T(8,128)(2,1)S(1)} %get-tuple-element.35), channel_id=1, source_target_pairs={{0,4},{4,0},{8,12},{12,8},{1,5},{5,1},{9,13},{13,9},{2,6},{6,2},{1... | collective-permute-start | bytes 245768 | tf_op jit(solution)/shard_map/ppermute | solution.py:33
  18.8 6.0 %copy-start.1 = (bf16[8,768,2,128]{3,2,1,0:T(2,128)(2,1)S(1)}, bf16[8,768,2,128]{3,2,1,0:T(2,128)(2,1)}, u32[]{:S(2)}) copy-start(bf16[8,768,2,128]{3,2,1,0:T(2,128)(2,1)} %param.11) | copy-start | bytes 9437188
  18.8 6.0 %copy-start.2 = (bf16[8,768,2,128]{3,2,1,0:T(2,128)(2,1)S(1)}, bf16[8,768,2,128]{3,2,1,0:T(2,128)(2,1)}, u32[]{:S(2)}) copy-start(bf16[8,768,2,128]{3,2,1,0:T(2,128)(2,1)} %param.12) | copy-start | bytes 9437188
  18.8 6.1 %copy-start.3 = (s32[8]{0:T(128)S(1)}, s32[8]{0:T(128)}, u32[]{:S(2)}) copy-start(s32[8]{0:T(128)} %refs_8_.1) | copy-start | bytes 100
  18.8 19.7 %slice-start = ((s8[25165824]{0:T(1024)(128)(4,1)}), s8[4194304]{0:T(1024)(128)(4,1)S(1)}, s32[]{:S(2)}) async-start(s8[25165824]{0:T(1024)(128)(4,1)} %bitcast.2), calls=%async_computation | async-start | bytes 8388608
  18.8 19.7 %slice-start.1 = ((s8[25165824]{0:T(1024)(128)(4,1)}), s8[4194304]{0:T(1024)(128)(4,1)S(1)}, s32[]{:S(2)}) async-start(s8[25165824]{0:T(1024)(128)(4,1)} %bitcast.2), calls=%async_computation.1 | async-start | bytes 8388608
  18.8 19.7 %slice-start.2 = ((s8[25165824]{0:T(1024)(128)(4,1)}), s8[4194304]{0:T(1024)(128)(4,1)S(1)}, s32[]{:S(2)}) async-start(s8[25165824]{0:T(1024)(128)(4,1)} %bitcast.2), calls=%async_computation.2 | async-start | bytes 8388608
  18.8 19.7 %slice-start.3 = ((s8[25165824]{0:T(1024)(128)(4,1)}), s8[4194304]{0:T(1024)(128)(4,1)S(1)}, s32[]{:S(2)}) async-start(s8[25165824]{0:T(1024)(128)(4,1)} %bitcast.2), calls=%async_computation.3 | async-start | bytes 8388608
  18.8 19.7 %slice-start.4 = ((s8[25165824]{0:T(1024)(128)(4,1)}), s8[4194304]{0:T(1024)(128)(4,1)S(1)}, s32[]{:S(2)}) async-start(s8[25165824]{0:T(1024)(128)(4,1)} %bitcast.2), calls=%async_computation.4 | async-start | bytes 8388608
  20.6 11.0 %collective-permute-start.3 = (bf16[16,1024]{1,0:T(8,128)(2,1)S(1)}, bf16[16,1024]{1,0:T(8,128)(2,1)S(1)}, u32[]{:S(2)}, u32[]{:S(2)}) collective-permute-start(bf16[16,1024]{1,0:T(8,128)(2,1)S(1)} %get-tuple-element.29), channel_id=1, source_target_pairs={{0,8},{4,12},{8,0},{12,4},{1,9},{5,13},{9,1},{13,5},{2,10},{6,14},... | collective-permute-start | bytes 98312 | tf_op jit(solution)/shard_map/ppermute | solution.py:33
  23.4 8.6 %collective-permute-start.4 = (bf16[16,1024]{1,0:T(8,128)(2,1)S(1)}, bf16[16,1024]{1,0:T(8,128)(2,1)S(1)}, u32[]{:S(2)}, u32[]{:S(2)}) collective-permute-start(bf16[16,1024]{1,0:T(8,128)(2,1)S(1)} %get-tuple-element.30), channel_id=1, source_target_pairs={{0,12},{4,8},{8,4},{12,0},{1,13},{5,9},{9,5},{13,1},{2,14},{6,10},... | collective-permute-start | bytes 98312 | tf_op jit(solution)/shard_map/ppermute | solution.py:33
  24.8 7.2 %collective-permute-start.5 = (bf16[16,1024]{1,0:T(8,128)(2,1)S(1)}, bf16[16,1024]{1,0:T(8,128)(2,1)S(1)}, u32[]{:S(2)}, u32[]{:S(2)}) collective-permute-start(bf16[16,1024]{1,0:T(8,128)(2,1)S(1)} %get-tuple-element.31), channel_id=1, source_target_pairs={{0,4},{4,0},{8,12},{12,8},{1,5},{5,1},{9,13},{13,9},{2,6},{6,2},{1... | collective-permute-start | bytes 98312 | tf_op jit(solution)/shard_map/ppermute | solution.py:33
  24.8 13.7 %slice-start.5 = ((s8[25165824]{0:T(1024)(128)(4,1)}), s8[4194304]{0:T(1024)(128)(4,1)S(1)}, s32[]{:S(2)}) async-start(s8[25165824]{0:T(1024)(128)(4,1)} %bitcast.2), calls=%async_computation.5 | async-start | bytes 8388608
  27.3 9.8 %collective-permute-start.14 = (bf16[16,2048]{1,0:T(8,128)(2,1)S(1)}, bf16[16,2048]{1,0:T(8,128)(2,1)S(1)}, u32[]{:S(2)}, u32[]{:S(2)}) collective-permute-start(bf16[16,2048]{1,0:T(8,128)(2,1)S(1)} %get-tuple-element.40.refs_0_), channel_id=1, source_target_pairs={{0,12},{4,8},{8,4},{12,0},{1,13},{5,9},{9,5},{13,1},{2,14},{6,10},... | collective-permute-start | bytes 196616 | tf_op jit(solution)/shard_map/ppermute | solution.py:33
  30.6 7.9 %collective-permute-start.13 = (bf16[16,2048]{1,0:T(8,128)(2,1)S(1)}, bf16[16,2048]{1,0:T(8,128)(2,1)S(1)}, u32[]{:S(2)}, u32[]{:S(2)}) collective-permute-start(bf16[16,2048]{1,0:T(8,128)(2,1)S(1)} %get-tuple-element.40.refs_0_), channel_id=1, source_target_pairs={{0,8},{4,12},{8,0},{12,4},{1,9},{5,13},{9,1},{13,5},{2,10},{6,14},... | collective-permute-start | bytes 196616 | tf_op jit(solution)/shard_map/ppermute | solution.py:33
  31.5 7.0 %collective-permute-start.12 = (bf16[16,2048]{1,0:T(8,128)(2,1)S(1)}, bf16[16,2048]{1,0:T(8,128)(2,1)S(1)}, u32[]{:S(2)}, u32[]{:S(2)}) collective-permute-start(bf16[16,2048]{1,0:T(8,128)(2,1)S(1)} %get-tuple-element.40.refs_0_), channel_id=1, source_target_pairs={{0,4},{4,0},{8,12},{12,8},{1,5},{5,1},{9,13},{13,9},{2,6},{6,2},{1... | collective-permute-start | bytes 196616 | tf_op jit(solution)/shard_map/ppermute | solution.py:33
  34.0 7.6 %collective-permute-start.11 = (bf16[16,1024]{1,0:T(8,128)(2,1)S(1)}, bf16[16,1024]{1,0:T(8,128)(2,1)S(1)}, u32[]{:S(2)}, u32[]{:S(2)}) collective-permute-start(bf16[16,1024]{1,0:T(8,128)(2,1)S(1)} %attend.3.refs_0_), channel_id=1, source_target_pairs={{0,12},{4,8},{8,4},{12,0},{1,13},{5,9},{9,5},{13,1},{2,14},{6,10},... | collective-permute-start | bytes 98312 | tf_op jit(solution)/shard_map/ppermute | solution.py:33
  37.0 5.1 %collective-permute-start.10 = (bf16[16,1024]{1,0:T(8,128)(2,1)S(1)}, bf16[16,1024]{1,0:T(8,128)(2,1)S(1)}, u32[]{:S(2)}, u32[]{:S(2)}) collective-permute-start(bf16[16,1024]{1,0:T(8,128)(2,1)S(1)} %attend.3.refs_0_), channel_id=1, source_target_pairs={{0,8},{4,12},{8,0},{12,4},{1,9},{5,13},{9,1},{13,5},{2,10},{6,14},... | collective-permute-start | bytes 98312 | tf_op jit(solution)/shard_map/ppermute | solution.py:33
  37.1 5.1 %collective-permute-start.9 = (bf16[16,1024]{1,0:T(8,128)(2,1)S(1)}, bf16[16,1024]{1,0:T(8,128)(2,1)S(1)}, u32[]{:S(2)}, u32[]{:S(2)}) collective-permute-start(bf16[16,1024]{1,0:T(8,128)(2,1)S(1)} %attend.3.refs_0_), channel_id=1, source_target_pairs={{0,4},{4,0},{8,12},{12,8},{1,5},{5,1},{9,13},{13,9},{2,6},{6,2},{1... | collective-permute-start | bytes 98312 | tf_op jit(solution)/shard_map/ppermute | solution.py:33
  43.8 5.5 %collective-permute-start.15 = (bf16[16,4096]{1,0:T(8,128)(2,1)S(1)}, bf16[16,4096]{1,0:T(8,128)(2,1)S(1)}, u32[]{:S(2)}, u32[]{:S(2)}) collective-permute-start(bf16[16,4096]{1,0:T(8,128)(2,1)S(1)} %get-tuple-element.42), channel_id=1, source_target_pairs={{0,2},{1,3},{2,0},{3,1},{4,6},{5,7},{6,4},{7,5},{8,10},{9,11},{10,... | collective-permute-start | bytes 393224 | tf_op jit(solution)/shard_map/ppermute | solution.py:33
  45.3 5.8 %collective-permute-start.16 = (bf16[16,4096]{1,0:T(8,128)(2,1)S(1)}, bf16[16,4096]{1,0:T(8,128)(2,1)S(1)}, u32[]{:S(2)}, u32[]{:S(2)}) collective-permute-start(bf16[16,4096]{1,0:T(8,128)(2,1)S(1)} %get-tuple-element.43), channel_id=1, source_target_pairs={{0,3},{1,2},{2,1},{3,0},{4,7},{5,6},{6,5},{7,4},{8,11},{9,10},{10,... | collective-permute-start | bytes 393224 | tf_op jit(solution)/shard_map/ppermute | solution.py:33
  45.3 5.8 %collective-permute-start.17 = (bf16[16,4096]{1,0:T(8,128)(2,1)S(1)}, bf16[16,4096]{1,0:T(8,128)(2,1)S(1)}, u32[]{:S(2)}, u32[]{:S(2)}) collective-permute-start(bf16[16,4096]{1,0:T(8,128)(2,1)S(1)} %get-tuple-element.44), channel_id=1, source_target_pairs={{0,1},{1,0},{2,3},{3,2},{4,5},{5,4},{6,7},{7,6},{8,9},{9,8},{10,11... | collective-permute-start | bytes 393224 | tf_op jit(solution)/shard_map/ppermute | solution.py:33

commit v6 on v5

--- a/solution.py
+++ b/solution.py
@@ -170,7 +170,7 @@
 def project(blocks, near, weight, ranges, coming, ngx, ngy):
     depth, ready = near.shape
     width = sum(count for _, count in ranges)
-    late_tiles = column_tiles(width - ready, 256)
+    late_tiles = column_tiles(width - ready)
     late_parts = [cut(ranges, ready + t.start, ready + t.stop) for t in late_tiles]
     ahead = sum(part[2] for part in coming)
     count = len(blocks)
@@ -270,7 +270,7 @@
             return x * cosine + pltpu.roll(x, half, 1) * sine
 
         contract = (((1,), (1,)), ((), ()))
-        column, fresh, new_values = 0, [], []
+        column, new_keys, new_values = 0, [], []
         for n, (_, first, count) in enumerate(chunk):
             pad = pads[n]
             for h in range(pad):
@@ -284,12 +284,7 @@
             else:
                 new_key, new_value = pair_refs[0][...], pair_refs[1][...]
             new_values.append(new_value.astype(F32))
-            scores = lax.dot_general(
-                qs[n][...].astype(BF16), new_key, contract, preferred_element_type=F32
-            )
-            row = lax.broadcasted_iota(jnp.int32, scores.shape, 0) // pad
-            col = lax.broadcasted_iota(jnp.int32, scores.shape, 1)
-            fresh.append(jnp.where((row // 2 == col // 2) & (col <= row), scores * scale, -1e30))
+            new_keys.append(new_key.astype(F32))
         if keep:
             kept_refs[0][...], kept_refs[1][...] = new_key, new_value
 
@@ -306,20 +301,26 @@
                 s = slice(r * rows + starts[n], r * rows + starts[n + 1])
                 own_rows = slice(2 * r * pads[n], 2 * (r + 1) * pads[n])
                 score = jnp.where(live & mine[n], sc[s, :] * scale, -1e30)
-                f = fresh[n][own_rows]
-                top = jnp.maximum(score.max(axis=1, keepdims=True), f.max(axis=1, keepdims=True))
-                e, fe = jnp.exp(score - top), jnp.exp(f - top)
-                inverse = 1.0 / (e.sum(axis=1, keepdims=True) + fe.sum(axis=1, keepdims=True))
+                q = qs[n][own_rows, :].astype(BF16).astype(F32)
+                second = lax.broadcasted_iota(jnp.int32, (2 * pads[n], 1), 0) >= pads[n]
+                f = [
+                    (q * new_keys[n][token : token + 1]).sum(axis=1, keepdims=True) * scale
+                    for token in (2 * r, 2 * r + 1)
+                ]
+                f[1] = jnp.where(second, f[1], -1e30)
+                top = jnp.maximum(score.max(axis=1, keepdims=True), jnp.maximum(f[0], f[1]))
+                e, fe = jnp.exp(score - top), [jnp.exp(x - top) for x in f]
+                inverse = 1.0 / (e.sum(axis=1, keepdims=True) + (fe[0] + fe[1]))
                 wt[s, :] = (e * inverse).astype(BF16)
-                fw[n][own_rows, :] = (fe * inverse).astype(BF16).astype(F32)
+                fw[n][own_rows, :] = sum(
+                    (x * inverse).astype(BF16).astype(F32) * new_values[n][token : token + 1]
+                    for x, token in zip(fe, (2 * r, 2 * r + 1))
+                )
         for r in range(requests):
             total = dot(wt[r * rows : (r + 1) * rows, :], v_ref[r])
             for n in range(parts):
                 own_rows = slice(2 * r * pads[n], 2 * (r + 1) * pads[n])
-                value = total[starts[n] : starts[n + 1]]
-                for token in (2 * r, 2 * r + 1):
-                    value = value + fw[n][own_rows, token : token + 1] * new_values[n][token : token + 1]
-                at[n][own_rows, :] = value
+                at[n][own_rows, :] = total[starts[n] : starts[n + 1]] + fw[n][own_rows, :]
         column = 0
         for n, (_, _, count) in enumerate(chunk):
             for h in range(count):
@@ -344,7 +345,7 @@
         ]
         + per_part
         + per_part
-        + [pltpu.VMEM((tokens * pad, tokens), F32) for pad in pads],
+        + per_part,
         cost_estimate=cost(1 << 31, 12 << 20),
         compiler_params=pltpu.CompilerParams(vmem_limit_bytes=10 << 20),
         name="attend",
@@ -434,14 +435,14 @@
     rows = [hidden_in] + [swap(hidden_in, "gy", s, ngy) for s in range(1, ngy)]
     near, cosine, sine = fetch(
         joined_projection_weight,
-        cut(ranges[0], 0, max(head_dim, widths[0] * 9 // 10 // 256 * 256)),
+        cut(ranges[0], 0, max(head_dim, widths[0] * 4 // 5 // 256 * 256)),
         positions,
         frequencies_of(head_dim),
     )
     joined = []
     for n in range(len(chunks)):
         last = n == len(chunks) - 1
-        coming = [] if last else cut(ranges[n + 1], 0, max(head_dim, widths[n + 1] // 256 * 256))
+        coming = [] if last else cut(ranges[n + 1], 0, max(head_dim, widths[n + 1] * 3 // 4 // 256 * 256))
         made = project(rows, near, joined_projection_weight, ranges[n], coming, ngx, ngy)
         joined.append((made[0], [swap(made[s], "gx", s, ngx) for s in order_of(ngx)]))
         if not last:

time: 52.1 us -> 51.9 us (level)
    pallas_call x2, Pallas kernels: 5.95 us -> 6.82 us  [project(): pl.pallas_call(kernel, out_shape=out_shape, in_specs=[IN_VMEM] * (count +...]
    pallas_call x1, Pallas kernels: 6.67 us -> 6.12 us  [fetch(): pl.pallas_call(kernel, out_shape=[pltpu.VMEM((depth, width), weight.dtype...]
where the time goes in v6:
time: 51.9 us; the launch traced here: 51.8 us
  starting transfers between devices  23.2 us (45%)
  Pallas kernels  22.8 us (44%)
  waiting for transfers between devices  5.51 us (11%)
    ppermute x18, starting transfers between devices, swap(): lax.ppermute(block, axis, [(i, target(i, step, count)) for i in range(cou...  23.2 us
    pallas_call x2, Pallas kernels, project(): pl.pallas_call(kernel, out_shape=out_shape, in_specs=[IN_VMEM] * (count +...  6.82 us
    pallas_call x1, Pallas kernels, fetch(): pl.pallas_call(kernel, out_shape=[pltpu.VMEM((depth, width), weight.dtype...  6.12 us
    ppermute x18, waiting for transfers between devices, swap(): lax.ppermute(block, axis, [(i, target(i, step, count)) for i in range(cou...  5.51 us
    pallas_call x2, Pallas kernels, project_out(): pl.pallas_call(kernel, out_shape=out_shape, in_specs=[IN_VMEM] * (ngx + 1...  4.65 us
    pallas_call x2, Pallas kernels, attend(): pl.pallas_call(kernel, out_shape=out_shape, in_specs=[IN_VMEM] * (1 + nre...  4.37 us
  transfers between devices with their start and end apart: 18, of which 3 were waited for; matrix products, arithmetic and copies ran while one was open for 0% of the time, Pallas kernels for 30%

profile of v6, /device:TPU:0, one launch (start us, length us, event | category | flops | bytes accessed | tf_op | source)
XLA Modules:
  0.0 51.8 jit_solution(2226753039449210328)
XLA Ops:
  0.0 0.0 copy-start
  0.0 2.9 %collective-permute-start.1 = (bf16[8,2,4096]{2,1,0:T(2,128)(2,1)}, bf16[8,2,4096]{2,1,0:T(2,128)(2,1)S(1)}, u32[]{:S(2)}, u32[]{:S(2)}) collective-permute-start(bf16[8,2,4096]{2,1,0:T(2,128)(2,1)} %refs_0_.1), channel_id=1, source_target_pairs={{0,2},{1,3},{2,0},{3,1},{4,6},{5,7},{6,4},{7,5},{8,10},{9,11},{10,... | collective-permute-start | bytes 393224 | tf_op jit(solution)/shard_map/ppermute | solution.py:33
  2.9 0.0 collective-permute-start
  2.9 0.2 collective-permute-start.2
  3.1 6.1 %fetch.1 = (bf16[4096,2048]{1,0:T(8,128)(2,1)S(1)}, f32[16,128]{1,0:T(8,128)S(1)}, f32[16,128]{1,0:T(8,128)S(1)}) custom-call(bf16[4096,3584]{1,0:T(8,128)(2,1)} %refs_2_.1, s32[8]{0:T(128)} %pos_any.1, f32[1,128]{1,0:T(1,128)} %constant.2.clone.freq_any), custom_call_target="tpu_custom_call" | custom-call | bytes 33554432 | tf_op jit(solution)/shard_map/fetch/pallas_call | solution.py:153
  9.3 0.0 collective-permute-done.1.refs_2_
  9.3 0.0 collective-permute-done.refs_1_
  9.3 0.0 collective-permute-done.2.refs_3_
  9.3 0.0 copy-done
  9.3 4.6 %project.2 = (f32[16,2560]{1,0:T(8,128)S(1)}, bf16[16,2560]{1,0:T(8,128)(2,1)S(1)}, bf16[16,2560]{1,0:T(8,128)(2,1)S(1)}, bf16[16,2560]{1,0:T(8,128)(2,1)S(1)}, ...) custom-call(bf16[8,2,4096]{2,1,0:T(2,128)(2,1)S(1)} %copy-done, ...), custom_call_target="tpu_custom_call" | custom-call | flops 1342177280 | bytes 20971520 | tf_op jit(solution)/shard_map/project/pallas_call | solution.py:231
  13.9 3.1 %collective-permute-start.6 = (bf16[16,2560]{1,0:T(8,128)(2,1)S(1)}, bf16[16,2560]{1,0:T(8,128)(2,1)S(1)}, u32[]{:S(2)}, u32[]{:S(2)}) collective-permute-start(bf16[16,2560]{1,0:T(8,128)(2,1)S(1)} %get-tuple-element.33), channel_id=1, source_target_pairs={{0,8},{4,12},{8,0},{12,4},{1,9},{5,13},{9,1},{13,5},{2,10},{6,14},... | collective-permute-start | bytes 245768 | tf_op jit(solution)/shard_map/ppermute | solution.py:33
  17.0 1.3 %collective-permute-start.7 = (bf16[16,2560]{1,0:T(8,128)(2,1)S(1)}, bf16[16,2560]{1,0:T(8,128)(2,1)S(1)}, u32[]{:S(2)}, u32[]{:S(2)}) collective-permute-start(bf16[16,2560]{1,0:T(8,128)(2,1)S(1)} %get-tuple-element.34), channel_id=1, source_target_pairs={{0,12},{4,8},{8,4},{12,0},{1,13},{5,9},{9,5},{13,1},{2,14},{6,10},... | collective-permute-start | bytes 245768 | tf_op jit(solution)/shard_map/ppermute | solution.py:33
  18.4 0.2 collective-permute-start.8
  18.6 0.0 copy-start.1
  18.6 0.0 copy-start.2
  18.6 0.0 copy-start.3
  18.6 0.0 slice-start
  18.6 0.0 slice-start.1
  18.6 0.0 slice-start.2
  18.6 0.0 slice-start.3
  18.7 0.0 slice-start.4
  18.7 2.2 %project.3 = (f32[16,1024]{1,0:T(8,128)S(1)}, bf16[16,1024]{1,0:T(8,128)(2,1)S(1)}, bf16[16,1024]{1,0:T(8,128)(2,1)S(1)}, bf16[16,1024]{1,0:T(8,128)(2,1)S(1)}) custom-call(bf16[64,4096]{1,0:T(8,128)(2,1)S(1)} %get-tuple-element.26.refs_0_, bf16[4096,768]{1,0:T(8,128)(2,1)S(1)} %get-tuple-element.27.refs_1_, bf16[4096,3584]{1,0:T(8,128)(2,1)} %refs_2_.1), custom_call_target="tpu_custom_call" | custom-call | flops 536870912 | bytes 8388608 | tf_op jit(solution)/shard_map/project/pallas_call | solution.py:231
  20.9 2.9 %collective-permute-start.3 = (bf16[16,1024]{1,0:T(8,128)(2,1)S(1)}, bf16[16,1024]{1,0:T(8,128)(2,1)S(1)}, u32[]{:S(2)}, u32[]{:S(2)}) collective-permute-start(bf16[16,1024]{1,0:T(8,128)(2,1)S(1)} %get-tuple-element.29), channel_id=1, source_target_pairs={{0,8},{4,12},{8,0},{12,4},{1,9},{5,13},{9,1},{13,5},{2,10},{6,14},... | collective-permute-start | bytes 98312 | tf_op jit(solution)/shard_map/ppermute | solution.py:33
  23.8 1.3 %collective-permute-start.4 = (bf16[16,1024]{1,0:T(8,128)(2,1)S(1)}, bf16[16,1024]{1,0:T(8,128)(2,1)S(1)}, u32[]{:S(2)}, u32[]{:S(2)}) collective-permute-start(bf16[16,1024]{1,0:T(8,128)(2,1)S(1)} %get-tuple-element.30), channel_id=1, source_target_pairs={{0,12},{4,8},{8,4},{12,0},{1,13},{5,9},{9,5},{13,1},{2,14},{6,10},... | collective-permute-start | bytes 98312 | tf_op jit(solution)/shard_map/ppermute | solution.py:33
  25.1 0.0 collective-permute-done.6.refs_1_
  25.1 0.0 collective-permute-start.5
  25.1 0.0 collective-permute-done.7.refs_2_
  25.1 0.0 collective-permute-done.8.refs_3_
  25.1 0.0 copy-done.1
  25.1 0.0 copy-done.2
  25.2 0.0 copy-done.3
  25.2 0.0 slice-start.5
  25.2 2.4 %attend.2 = (bf16[16,2048]{1,0:T(8,128)(2,1)S(1)}, bf16[16,128]{1,0:T(8,128)(2,1)S(1)}, bf16[16,128]{1,0:T(8,128)(2,1)S(1)}) custom-call(f32[16,2560]{1,0:T(8,128)S(1)} %get-tuple-element.32.refs_0_, bf16[16,2560]{1,0:T(8,128)(2,1)S(1)} %collective-permute-done.6.refs_1_, bf16[16,2560]{1,0:T(8,128)(2,1)S(1)} %collective-permute-done.7.refs_2_, ...), custom_call_target="tpu_custom_call" | custom-call | flops 2147483648 | bytes 12582912 | tf_op jit(solution)/shard_map/attend/pallas_call | solution.py:337
  27.6 2.8 %collective-permute-start.14 = (bf16[16,2048]{1,0:T(8,128)(2,1)S(1)}, bf16[16,2048]{1,0:T(8,128)(2,1)S(1)}, u32[]{:S(2)}, u32[]{:S(2)}) collective-permute-start(bf16[16,2048]{1,0:T(8,128)(2,1)S(1)} %get-tuple-element.40.refs_0_), channel_id=1, source_target_pairs={{0,12},{4,8},{8,4},{12,0},{1,13},{5,9},{9,5},{13,1},{2,14},{6,10},... | collective-permute-start | bytes 196616 | tf_op jit(solution)/shard_map/ppermute | solution.py:33
  30.4 1.0 %collective-permute-start.13 = (bf16[16,2048]{1,0:T(8,128)(2,1)S(1)}, bf16[16,2048]{1,0:T(8,128)(2,1)S(1)}, u32[]{:S(2)}, u32[]{:S(2)}) collective-permute-start(bf16[16,2048]{1,0:T(8,128)(2,1)S(1)} %get-tuple-element.40.refs_0_), channel_id=1, source_target_pairs={{0,8},{4,12},{8,0},{12,4},{1,9},{5,13},{9,1},{13,5},{2,10},{6,14},... | collective-permute-start | bytes 196616 | tf_op jit(solution)/shard_map/ppermute | solution.py:33
  31.3 0.0 collective-permute-done.3.refs_1_
  31.3 0.7 %collective-permute-start.12 = (bf16[16,2048]{1,0:T(8,128)(2,1)S(1)}, bf16[16,2048]{1,0:T(8,128)(2,1)S(1)}, u32[]{:S(2)}, u32[]{:S(2)}) collective-permute-start(bf16[16,2048]{1,0:T(8,128)(2,1)S(1)} %get-tuple-element.40.refs_0_), channel_id=1, source_target_pairs={{0,4},{4,0},{8,12},{12,8},{1,5},{5,1},{9,13},{13,9},{2,6},{6,2},{1... | collective-permute-start | bytes 196616 | tf_op jit(solution)/shard_map/ppermute | solution.py:33
  32.1 0.0 collective-permute-done.4.refs_2_
  32.1 0.0 collective-permute-done.5.refs_3_
  32.1 1.9 %attend.3.refs_0_ = bf16[16,1024]{1,0:T(8,128)(2,1)S(1)} custom-call(f32[16,1024]{1,0:T(8,128)S(1)} %get-tuple-element.28.refs_0_, bf16[16,1024]{1,0:T(8,128)(2,1)S(1)} %collective-permute-done.3.refs_1_, bf16[16,1024]{1,0:T(8,128)(2,1)S(1)} %collective-permute-done.4.refs_2_, bf16[16,1024]{1,0:T(8,128)(2,1)S(1)} %collective-permute-done.5.refs_3_, ...), custom_call_target="tpu_custom_call" | custom-call | flops 2147483648 | bytes 12582912 | tf_op jit(solution)/shard_map/attend/pallas_call | solution.py:337
  34.0 2.8 %collective-permute-start.11 = (bf16[16,1024]{1,0:T(8,128)(2,1)S(1)}, bf16[16,1024]{1,0:T(8,128)(2,1)S(1)}, u32[]{:S(2)}, u32[]{:S(2)}) collective-permute-start(bf16[16,1024]{1,0:T(8,128)(2,1)S(1)} %attend.3.refs_0_), channel_id=1, source_target_pairs={{0,12},{4,8},{8,4},{12,0},{1,13},{5,9},{9,5},{13,1},{2,14},{6,10},... | collective-permute-start | bytes 98312 | tf_op jit(solution)/shard_map/ppermute | solution.py:33
  36.8 0.1 collective-permute-start.10
  36.9 0.0 collective-permute-done.14.refs_3_
  36.9 1.6 %collective-permute-start.9 = (bf16[16,1024]{1,0:T(8,128)(2,1)S(1)}, bf16[16,1024]{1,0:T(8,128)(2,1)S(1)}, u32[]{:S(2)}, u32[]{:S(2)}) collective-permute-start(bf16[16,1024]{1,0:T(8,128)(2,1)S(1)} %attend.3.refs_0_), channel_id=1, source_target_pairs={{0,4},{4,0},{8,12},{12,8},{1,5},{5,1},{9,13},{13,9},{2,6},{6,2},{1... | collective-permute-start | bytes 98312 | tf_op jit(solution)/shard_map/ppermute | solution.py:33
  38.5 0.0 collective-permute-done.13.refs_2_
  38.5 0.0 collective-permute-done.12.refs_1_
  38.5 0.0 slice-done
  38.5 0.0 slice-done.1
  38.5 0.0 slice-done.2
  38.5 0.0 slice-done.3
  38.5 0.0 slice-done.4
  38.5 0.0 slice-done.5
  38.6 3.0 %project_out.2.refs_5_ = f32[64,4096]{1,0:T(8,128)S(1)} custom-call(bf16[16,2048]{1,0:T(8,128)(2,1)S(1)} %get-tuple-element.40.refs_0_, bf16[16,2048]{1,0:T(8,128)(2,1)S(1)} %collective-permute-done.12.refs_1_, bf16[16,2048]{1,0:T(8,128)(2,1)S(1)} %collective-permute-done.13.refs_2_, bf16[16,2048]{1,0:T(8,128)(2,1)S(1)} %collective-permute-done.14.refs_3_, ...), custom_call_target="tpu_custom_call" | custom-call | flops 1073741824 | bytes 16777216 | tf_op jit(solution)/shard_map/project_out/pallas_call | solution.py:384
  41.6 0.0 collective-permute-done.11.refs_3_
  41.6 0.3 collective-permute-done.10.refs_2_
  42.0 0.0 collective-permute-done.9.refs_1_
  42.0 1.6 %project_out.3 = (f32[16,4096]{1,0:T(8,128)S(1)}, bf16[16,4096]{1,0:T(8,128)(2,1)S(1)}, bf16[16,4096]{1,0:T(8,128)(2,1)S(1)}, bf16[16,4096]{1,0:T(8,128)(2,1)S(1)}) custom-call(bf16[16,1024]{1,0:T(8,128)(2,1)S(1)} %attend.3.refs_0_, bf16[16,1024]{1,0:T(8,128)(2,1)S(1)} %collective-permute-done.9.refs_1_, ...), custom_call_target="tpu_custom_call" | custom-call | flops 536870912 | bytes 8388608 | tf_op jit(solution)/shard_map/project_out/pallas_call | solution.py:384
  43.6 1.6 %collective-permute-start.15 = (bf16[16,4096]{1,0:T(8,128)(2,1)S(1)}, bf16[16,4096]{1,0:T(8,128)(2,1)S(1)}, u32[]{:S(2)}, u32[]{:S(2)}) collective-permute-start(bf16[16,4096]{1,0:T(8,128)(2,1)S(1)} %get-tuple-element.42), channel_id=1, source_target_pairs={{0,2},{1,3},{2,0},{3,1},{4,6},{5,7},{6,4},{7,5},{8,10},{9,11},{10,... | collective-permute-start | bytes 393224 | tf_op jit(solution)/shard_map/ppermute | solution.py:33
  45.1 0.0 collective-permute-start.16
  45.1 0.6 %collective-permute-start.17 = (bf16[16,4096]{1,0:T(8,128)(2,1)S(1)}, bf16[16,4096]{1,0:T(8,128)(2,1)S(1)}, u32[]{:S(2)}, u32[]{:S(2)}) collective-permute-start(bf16[16,4096]{1,0:T(8,128)(2,1)S(1)} %get-tuple-element.44), channel_id=1, source_target_pairs={{0,1},{1,0},{2,3},{3,2},{4,5},{5,4},{6,7},{7,6},{8,9},{9,8},{10,11... | collective-permute-start | bytes 393224 | tf_op jit(solution)/shard_map/ppermute | solution.py:33
  45.8 3.3 %collective-permute-done.15.refs_1_ = bf16[16,4096]{1,0:T(8,128)(2,1)S(1)} collective-permute-done((bf16[16,4096]{1,0:T(8,128)(2,1)S(1)}, bf16[16,4096]{1,0:T(8,128)(2,1)S(1)}, u32[]{:S(2)}, u32[]{:S(2)}) %collective-permute-start.15) | collective-permute-done | bytes 131104 | tf_op jit(solution)/shard_map/ppermute | solution.py:33
  49.1 1.8 %collective-permute-done.16.refs_2_ = bf16[16,4096]{1,0:T(8,128)(2,1)S(1)} collective-permute-done((bf16[16,4096]{1,0:T(8,128)(2,1)S(1)}, bf16[16,4096]{1,0:T(8,128)(2,1)S(1)}, u32[]{:S(2)}, u32[]{:S(2)}) %collective-permute-start.16) | collective-permute-done | bytes 131104 | tf_op jit(solution)/shard_map/ppermute | solution.py:33
  50.9 0.0 collective-permute-done.17.refs_3_
  50.9 0.8 %finish.1 = bf16[8,2,4096]{2,1,0:T(2,128)(2,1)} custom-call(f32[16,4096]{1,0:T(8,128)S(1)} %get-tuple-element.41.refs_0_, bf16[16,4096]{1,0:T(8,128)(2,1)S(1)} %collective-permute-done.15.refs_1_, bf16[16,4096]{1,0:T(8,128)(2,1)S(1)} %collective-permute-done.16.refs_2_, bf16[16,4096]{1,0:T(8,128)(2,1)S(1)} %collective-permute-done.17.refs_3_), custom_call_target="tpu_custom_call" | custom-call | tf_op jit(solution)/shard_map/finish/pallas_call | solution.py:406
  (1 shorter events, 0.0 us)
Async XLA Ops:
  0.0 9.3 %copy-start = (bf16[8,2,4096]{2,1,0:T(2,128)(2,1)S(1)}, bf16[8,2,4096]{2,1,0:T(2,128)(2,1)}, u32[]{:S(2)}) copy-start(bf16[8,2,4096]{2,1,0:T(2,128)(2,1)} %refs_0_.1) | copy-start | bytes 393220
  0.0 9.3 %collective-permute-start.1 = (bf16[8,2,4096]{2,1,0:T(2,128)(2,1)}, bf16[8,2,4096]{2,1,0:T(2,128)(2,1)S(1)}, u32[]{:S(2)}, u32[]{:S(2)}) collective-permute-start(bf16[8,2,4096]{2,1,0:T(2,128)(2,1)} %refs_0_.1), channel_id=1, source_target_pairs={{0,2},{1,3},{2,0},{3,1},{4,6},{5,7},{6,4},{7,5},{8,10},{9,11},{10,... | collective-permute-start | bytes 393224 | tf_op jit(solution)/shard_map/ppermute | solution.py:33
  2.9 6.3 %collective-permute-start = (bf16[8,2,4096]{2,1,0:T(2,128)(2,1)}, bf16[8,2,4096]{2,1,0:T(2,128)(2,1)S(1)}, u32[]{:S(2)}, u32[]{:S(2)}) collective-permute-start(bf16[8,2,4096]{2,1,0:T(2,128)(2,1)} %refs_0_.1), channel_id=1, source_target_pairs={{0,1},{1,0},{2,3},{3,2},{4,5},{5,4},{6,7},{7,6},{8,9},{9,8},{10,11... | collective-permute-start | bytes 393224 | tf_op jit(solution)/shard_map/ppermute | solution.py:33
  2.9 6.3 %collective-permute-start.2 = (bf16[8,2,4096]{2,1,0:T(2,128)(2,1)}, bf16[8,2,4096]{2,1,0:T(2,128)(2,1)S(1)}, u32[]{:S(2)}, u32[]{:S(2)}) collective-permute-start(bf16[8,2,4096]{2,1,0:T(2,128)(2,1)} %refs_0_.1), channel_id=1, source_target_pairs={{0,3},{1,2},{2,1},{3,0},{4,7},{5,6},{6,5},{7,4},{8,11},{9,10},{10,... | collective-permute-start | bytes 393224 | tf_op jit(solution)/shard_map/ppermute | solution.py:33
  13.9 11.2 %collective-permute-start.6 = (bf16[16,2560]{1,0:T(8,128)(2,1)S(1)}, bf16[16,2560]{1,0:T(8,128)(2,1)S(1)}, u32[]{:S(2)}, u32[]{:S(2)}) collective-permute-start(bf16[16,2560]{1,0:T(8,128)(2,1)S(1)} %get-tuple-element.33), channel_id=1, source_target_pairs={{0,8},{4,12},{8,0},{12,4},{1,9},{5,13},{9,1},{13,5},{2,10},{6,14},... | collective-permute-start | bytes 245768 | tf_op jit(solution)/shard_map/ppermute | solution.py:33
  17.0 8.1 %collective-permute-start.7 = (bf16[16,2560]{1,0:T(8,128)(2,1)S(1)}, bf16[16,2560]{1,0:T(8,128)(2,1)S(1)}, u32[]{:S(2)}, u32[]{:S(2)}) collective-permute-start(bf16[16,2560]{1,0:T(8,128)(2,1)S(1)} %get-tuple-element.34), channel_id=1, source_target_pairs={{0,12},{4,8},{8,4},{12,0},{1,13},{5,9},{9,5},{13,1},{2,14},{6,10},... | collective-permute-start | bytes 245768 | tf_op jit(solution)/shard_map/ppermute | solution.py:33
  18.4 6.8 %collective-permute-start.8 = (bf16[16,2560]{1,0:T(8,128)(2,1)S(1)}, bf16[16,2560]{1,0:T(8,128)(2,1)S(1)}, u32[]{:S(2)}, u32[]{:S(2)}) collective-permute-start(bf16[16,2560]{1,0:T(8,128)(2,1)S(1)} %get-tuple-element.35), channel_id=1, source_target_pairs={{0,4},{4,0},{8,12},{12,8},{1,5},{5,1},{9,13},{13,9},{2,6},{6,2},{1... | collective-permute-start | bytes 245768 | tf_op jit(solution)/shard_map/ppermute | solution.py:33
  18.6 6.5 %copy-start.1 = (bf16[8,768,2,128]{3,2,1,0:T(2,128)(2,1)S(1)}, bf16[8,768,2,128]{3,2,1,0:T(2,128)(2,1)}, u32[]{:S(2)}) copy-start(bf16[8,768,2,128]{3,2,1,0:T(2,128)(2,1)} %param.11) | copy-start | bytes 9437188
  18.6 6.5 %copy-start.2 = (bf16[8,768,2,128]{3,2,1,0:T(2,128)(2,1)S(1)}, bf16[8,768,2,128]{3,2,1,0:T(2,128)(2,1)}, u32[]{:S(2)}) copy-start(bf16[8,768,2,128]{3,2,1,0:T(2,128)(2,1)} %param.12) | copy-start | bytes 9437188
  18.6 6.5 %copy-start.3 = (s32[8]{0:T(128)S(1)}, s32[8]{0:T(128)}, u32[]{:S(2)}) copy-start(s32[8]{0:T(128)} %refs_8_.1) | copy-start | bytes 100
  18.6 19.9 %slice-start = ((s8[25165824]{0:T(1024)(128)(4,1)}), s8[4194304]{0:T(1024)(128)(4,1)S(1)}, s32[]{:S(2)}) async-start(s8[25165824]{0:T(1024)(128)(4,1)} %bitcast.2), calls=%async_computation | async-start | bytes 8388608
  18.6 19.9 %slice-start.1 = ((s8[25165824]{0:T(1024)(128)(4,1)}), s8[4194304]{0:T(1024)(128)(4,1)S(1)}, s32[]{:S(2)}) async-start(s8[25165824]{0:T(1024)(128)(4,1)} %bitcast.2), calls=%async_computation.1 | async-start | bytes 8388608
  18.6 19.9 %slice-start.2 = ((s8[25165824]{0:T(1024)(128)(4,1)}), s8[4194304]{0:T(1024)(128)(4,1)S(1)}, s32[]{:S(2)}) async-start(s8[25165824]{0:T(1024)(128)(4,1)} %bitcast.2), calls=%async_computation.2 | async-start | bytes 8388608
  18.6 19.9 %slice-start.3 = ((s8[25165824]{0:T(1024)(128)(4,1)}), s8[4194304]{0:T(1024)(128)(4,1)S(1)}, s32[]{:S(2)}) async-start(s8[25165824]{0:T(1024)(128)(4,1)} %bitcast.2), calls=%async_computation.3 | async-start | bytes 8388608
  18.7 19.9 %slice-start.4 = ((s8[25165824]{0:T(1024)(128)(4,1)}), s8[4194304]{0:T(1024)(128)(4,1)S(1)}, s32[]{:S(2)}) async-start(s8[25165824]{0:T(1024)(128)(4,1)} %bitcast.2), calls=%async_computation.4 | async-start | bytes 8388608
  20.9 10.5 %collective-permute-start.3 = (bf16[16,1024]{1,0:T(8,128)(2,1)S(1)}, bf16[16,1024]{1,0:T(8,128)(2,1)S(1)}, u32[]{:S(2)}, u32[]{:S(2)}) collective-permute-start(bf16[16,1024]{1,0:T(8,128)(2,1)S(1)} %get-tuple-element.29), channel_id=1, source_target_pairs={{0,8},{4,12},{8,0},{12,4},{1,9},{5,13},{9,1},{13,5},{2,10},{6,14},... | collective-permute-start | bytes 98312 | tf_op jit(solution)/shard_map/ppermute | solution.py:33
  23.8 8.3 %collective-permute-start.4 = (bf16[16,1024]{1,0:T(8,128)(2,1)S(1)}, bf16[16,1024]{1,0:T(8,128)(2,1)S(1)}, u32[]{:S(2)}, u32[]{:S(2)}) collective-permute-start(bf16[16,1024]{1,0:T(8,128)(2,1)S(1)} %get-tuple-element.30), channel_id=1, source_target_pairs={{0,12},{4,8},{8,4},{12,0},{1,13},{5,9},{9,5},{13,1},{2,14},{6,10},... | collective-permute-start | bytes 98312 | tf_op jit(solution)/shard_map/ppermute | solution.py:33
  25.1 7.0 %collective-permute-start.5 = (bf16[16,1024]{1,0:T(8,128)(2,1)S(1)}, bf16[16,1024]{1,0:T(8,128)(2,1)S(1)}, u32[]{:S(2)}, u32[]{:S(2)}) collective-permute-start(bf16[16,1024]{1,0:T(8,128)(2,1)S(1)} %get-tuple-element.31), channel_id=1, source_target_pairs={{0,4},{4,0},{8,12},{12,8},{1,5},{5,1},{9,13},{13,9},{2,6},{6,2},{1... | collective-permute-start | bytes 98312 | tf_op jit(solution)/shard_map/ppermute | solution.py:33
  25.2 13.4 %slice-start.5 = ((s8[25165824]{0:T(1024)(128)(4,1)}), s8[4194304]{0:T(1024)(128)(4,1)S(1)}, s32[]{:S(2)}) async-start(s8[25165824]{0:T(1024)(128)(4,1)} %bitcast.2), calls=%async_computation.5 | async-start | bytes 8388608
  27.6 9.3 %collective-permute-start.14 = (bf16[16,2048]{1,0:T(8,128)(2,1)S(1)}, bf16[16,2048]{1,0:T(8,128)(2,1)S(1)}, u32[]{:S(2)}, u32[]{:S(2)}) collective-permute-start(bf16[16,2048]{1,0:T(8,128)(2,1)S(1)} %get-tuple-element.40.refs_0_), channel_id=1, source_target_pairs={{0,12},{4,8},{8,4},{12,0},{1,13},{5,9},{9,5},{13,1},{2,14},{6,10},... | collective-permute-start | bytes 196616 | tf_op jit(solution)/shard_map/ppermute | solution.py:33
  30.4 8.1 %collective-permute-start.13 = (bf16[16,2048]{1,0:T(8,128)(2,1)S(1)}, bf16[16,2048]{1,0:T(8,128)(2,1)S(1)}, u32[]{:S(2)}, u32[]{:S(2)}) collective-permute-start(bf16[16,2048]{1,0:T(8,128)(2,1)S(1)} %get-tuple-element.40.refs_0_), channel_id=1, source_target_pairs={{0,8},{4,12},{8,0},{12,4},{1,9},{5,13},{9,1},{13,5},{2,10},{6,14},... | collective-permute-start | bytes 196616 | tf_op jit(solution)/shard_map/ppermute | solution.py:33
  31.3 7.1 %collective-permute-start.12 = (bf16[16,2048]{1,0:T(8,128)(2,1)S(1)}, bf16[16,2048]{1,0:T(8,128)(2,1)S(1)}, u32[]{:S(2)}, u32[]{:S(2)}) collective-permute-start(bf16[16,2048]{1,0:T(8,128)(2,1)S(1)} %get-tuple-element.40.refs_0_), channel_id=1, source_target_pairs={{0,4},{4,0},{8,12},{12,8},{1,5},{5,1},{9,13},{13,9},{2,6},{6,2},{1... | collective-permute-start | bytes 196616 | tf_op jit(solution)/shard_map/ppermute | solution.py:33
  34.0 7.6 %collective-permute-start.11 = (bf16[16,1024]{1,0:T(8,128)(2,1)S(1)}, bf16[16,1024]{1,0:T(8,128)(2,1)S(1)}, u32[]{:S(2)}, u32[]{:S(2)}) collective-permute-start(bf16[16,1024]{1,0:T(8,128)(2,1)S(1)} %attend.3.refs_0_), channel_id=1, source_target_pairs={{0,12},{4,8},{8,4},{12,0},{1,13},{5,9},{9,5},{13,1},{2,14},{6,10},... | collective-permute-start | bytes 98312 | tf_op jit(solution)/shard_map/ppermute | solution.py:33
  36.8 5.1 %collective-permute-start.10 = (bf16[16,1024]{1,0:T(8,128)(2,1)S(1)}, bf16[16,1024]{1,0:T(8,128)(2,1)S(1)}, u32[]{:S(2)}, u32[]{:S(2)}) collective-permute-start(bf16[16,1024]{1,0:T(8,128)(2,1)S(1)} %attend.3.refs_0_), channel_id=1, source_target_pairs={{0,8},{4,12},{8,0},{12,4},{1,9},{5,13},{9,1},{13,5},{2,10},{6,14},... | collective-permute-start | bytes 98312 | tf_op jit(solution)/shard_map/ppermute | solution.py:33
  36.9 5.1 %collective-permute-start.9 = (bf16[16,1024]{1,0:T(8,128)(2,1)S(1)}, bf16[16,1024]{1,0:T(8,128)(2,1)S(1)}, u32[]{:S(2)}, u32[]{:S(2)}) collective-permute-start(bf16[16,1024]{1,0:T(8,128)(2,1)S(1)} %attend.3.refs_0_), channel_id=1, source_target_pairs={{0,4},{4,0},{8,12},{12,8},{1,5},{5,1},{9,13},{13,9},{2,6},{6,2},{1... | collective-permute-start | bytes 98312 | tf_op jit(solution)/shard_map/ppermute | solution.py:33
  43.6 5.5 %collective-permute-start.15 = (bf16[16,4096]{1,0:T(8,128)(2,1)S(1)}, bf16[16,4096]{1,0:T(8,128)(2,1)S(1)}, u32[]{:S(2)}, u32[]{:S(2)}) collective-permute-start(bf16[16,4096]{1,0:T(8,128)(2,1)S(1)} %get-tuple-element.42), channel_id=1, source_target_pairs={{0,2},{1,3},{2,0},{3,1},{4,6},{5,7},{6,4},{7,5},{8,10},{9,11},{10,... | collective-permute-start | bytes 393224 | tf_op jit(solution)/shard_map/ppermute | solution.py:33
  45.1 5.8 %collective-permute-start.16 = (bf16[16,4096]{1,0:T(8,128)(2,1)S(1)}, bf16[16,4096]{1,0:T(8,128)(2,1)S(1)}, u32[]{:S(2)}, u32[]{:S(2)}) collective-permute-start(bf16[16,4096]{1,0:T(8,128)(2,1)S(1)} %get-tuple-element.43), channel_id=1, source_target_pairs={{0,3},{1,2},{2,1},{3,0},{4,7},{5,6},{6,5},{7,4},{8,11},{9,10},{10,... | collective-permute-start | bytes 393224 | tf_op jit(solution)/shard_map/ppermute | solution.py:33
  45.1 5.8 %collective-permute-start.17 = (bf16[16,4096]{1,0:T(8,128)(2,1)S(1)}, bf16[16,4096]{1,0:T(8,128)(2,1)S(1)}, u32[]{:S(2)}, u32[]{:S(2)}) collective-permute-start(bf16[16,4096]{1,0:T(8,128)(2,1)S(1)} %get-tuple-element.44), channel_id=1, source_target_pairs={{0,1},{1,0},{2,3},{3,2},{4,5},{5,4},{6,7},{7,6},{8,9},{9,8},{10,11... | collective-permute-start | bytes 393224 | tf_op jit(solution)/shard_map/ppermute | solution.py:33
